TPU v7x, 32 devices: a whole 2x2x4 slice. The times are simulated.
32 devices in a mesh: parts: 1, local: 32 (over z, y, x, core).
Axes of the slice: x: 2, y: 2, z: 4, core: 2. Of those that a mesh axis runs over, the one named last changes fastest.
Arguments:
- tokens: bfloat16 [256, 7168], P(('parts', 'local')), may hold values from -6 to 6
- routes: int32 [256, 2], P(('parts', 'local')), may hold values from 0 to 3, all different within a row; in each aligned block of 8 rows (0 to 7, 8 to 15, ...) at most 8 rows name the same one
- route_weight: float32 [256, 2], P(('parts', 'local')), may hold values from 0.25 to 1
- gate_weight: bfloat16 [32, 7168, 256], P('local'), may hold values from -0.0625 to 0.0625
- up_weight: bfloat16 [32, 7168, 256], P('local'), may hold values from -0.0625 to 0.0625
- down_weight: bfloat16 [32, 256, 7168], P('local'), may hold values from -0.125 to 0.125
Outputs:
- mixed: bfloat16 [256, 7168], P(('parts', 'local'))
Inputs may be any that keep to these rules, and one draw needn't show every extreme that they name: `routes`: among the rows of one device no expert is named by more than 8 rows, a bound that some block reaches.
All inputs are finite; a program needn't handle non-finite values.
Results may differ from a plain program's by a relative error of at most 0.0051.
Values may be sent and summed in bfloat16 or wider, within the bound.
No kernel may reach another device: no remote copies, remote signals or barrier semaphores. Data moves between devices by JAX's collectives and lax.ppermute only.
A program may use at most 128 MiB of HBM per device.

v0:
```python
import jax
import jax.numpy as jnp
from jax import lax
from jax.sharding import PartitionSpec as P

SPLIT = 8


def body(tokens, routes, route_weight, gate_weight, up_weight, down_weight):
    members = lax.axis_size("local")
    sharers = SPLIT
    experts = members // sharers
    rows_dev, features = tokens.shape
    fanout = routes.shape[1]
    capacity = min(rows_dev, max(2, 2 * rows_dev * fanout // experts))
    matches = (routes[:, :, None] == jnp.arange(experts, dtype=jnp.int32)).astype(jnp.int32)
    stacked = matches.reshape(rows_dev * fanout, experts)
    earlier = jnp.cumsum(stacked, axis=0) - stacked
    slot_index = jnp.sum(earlier * stacked, axis=-1).reshape(rows_dev, fanout)
    slot_match = (slot_index[:, :, None] == jnp.arange(capacity, dtype=jnp.int32)).astype(jnp.int32)
    placement = matches[:, :, :, None] * slot_match[:, :, None, :]
    dispatch = jnp.sum(placement, axis=1)
    slot_weight = jnp.einsum(
        "rkec,rk->ec", placement.astype(jnp.float32), route_weight, precision=lax.Precision.HIGHEST
    )
    buffer = jnp.einsum(
        "rec,rd->ecd", dispatch.astype(jnp.bfloat16), tokens, preferred_element_type=jnp.float32
    ).astype(jnp.bfloat16)
    outgoing = jnp.repeat(buffer, sharers, axis=0)
    slot_rows = lax.all_to_all(outgoing, "local", split_axis=0, concat_axis=0, tiled=True)
    sources, slots, cols = slot_rows.shape
    lined = slot_rows.reshape(sources * slots, cols)
    gate_part = jnp.dot(lined, gate_weight[0], preferred_element_type=jnp.float32)
    up_part = jnp.dot(lined, up_weight[0], preferred_element_type=jnp.float32)
    hidden = (jax.nn.silu(gate_part) * up_part).astype(jnp.bfloat16)
    result = jnp.dot(hidden, down_weight[0], preferred_element_type=jnp.float32)
    partial_value = result.reshape(sources, slots, cols)
    returned = lax.all_to_all(partial_value, "local", split_axis=0, concat_axis=0, tiled=True)
    summed = jnp.sum(returned.reshape(experts, sharers, capacity, features), axis=1)
    weighted = summed * slot_weight[:, :, None]
    mixed = jnp.einsum(
        "rec,ecd->rd", dispatch.astype(jnp.float32), weighted, precision=lax.Precision.HIGHEST
    )
    return mixed.astype(jnp.bfloat16)


def solution(mesh):
    return jax.shard_map(
        body,
        mesh=mesh,
        in_specs=(
            P(("parts", "local"), None),
            P(("parts", "local"), None),
            P(("parts", "local"), None),
            P("local", None, None),
            P("local", None, None),
            P("local", None, None),
        ),
        out_specs=P(("parts", "local"), None),
        check_vma=False,
    )
```

profile of v0, /device:TPU:0, one launch (start us, length us, event | category | flops | bytes accessed | tf_op | source)
XLA Modules:
  0.0 280.1 jit_solution(2855761091376810281)
XLA Ops:
  0.0 0.0 copy-start
  0.0 0.7 fusion.44
  0.7 0.8 copy.13
  1.5 0.1 eq.48
  1.6 0.1 fusion.42
  1.7 0.2 select_reduce_fusion
  1.9 0.1 eq.52
  1.9 0.1 copy.14
  2.0 0.1 fusion.43
  2.1 0.1 multiply_reduce_fusion
  2.2 0.0 copy-done
  2.2 0.3 convolution_convert_fusion
  2.5 0.4 broadcast_in_dim.2
  2.9 0.0 copy-start.2
  2.9 90.1 %all_to_all.10 = bf16[32,8,7168]{2,1,0:T(8,128)(2,1)S(1)} all-to-all(bf16[32,8,7168]{2,1,0:T(8,128)(2,1)S(1)} %bitcast.52), channel_id=1, replica_groups=mesh['parts'=1,'local'=32] {'local'}, dimensions={0} | all-to-all | bytes 7340032 | tf_op jit(solution)/shard_map/all_to_all | solution.py:30
  93.0 1.9 copy-done.1
  94.9 0.0 copy-done.2
  94.9 1.1 fusion.5
  96.0 11.2 %fusion.1 = f32[32,8,7168]{2,1,0:T(8,128)} fusion(bf16[1,256,7168]{2,1,0:T(8,128)(2,1)} %param.11, bf16[1,7168,256]{2,1,0:T(8,128)(2,1)} %param.10, bf16[32,8,7168]{2,1,0:T(8,128)(2,1)} %copy-done.1, f32[256,256]{1,0:T(8,128)S(1)} %fusion.5), kind=kOutput, calls=%fused_computation.4 | convolution fusion | flops 1879441408 | bytes 18612224 | tf_op jit(solution)/shard_map/dot_general | solution.py:36
  107.2 3.8 %all-to-all-start.1 = ((f32[32,8,7168]{2,1,0:T(8,128)}), f32[32,8,7168]{2,1,0:T(8,128)}, u32[]{:S(2)}, u32[]{:S(2)}) async-start(f32[32,8,7168]{2,1,0:T(8,128)} %fusion.1), calls=%async_computation.1 | async-start | bytes 14680064 | tf_op jit(solution)/shard_map/all_to_all | solution.py:38
  111.0 0.2 fusion.37
  111.2 162.9 %all-to-all-done.1 = f32[32,8,7168]{2,1,0:T(8,128)} async-done(((f32[32,8,7168]{2,1,0:T(8,128)}), f32[32,8,7168]{2,1,0:T(8,128)}, u32[]{:S(2)}, u32[]{:S(2)}) %all-to-all-start.1) | async-done | bytes 7340064 | tf_op jit(solution)/shard_map/all_to_all | solution.py:38
  274.1 3.6 %bitcast_reduce_fusion = f32[4,8,7168]{2,1,0:T(8,128)S(1)} fusion(f32[32,8,7168]{2,1,0:T(8,128)} %all-to-all-done.1), kind=kLoop, calls=%fused_computation.3 | loop fusion | flops 1605632 | bytes 8257536 | tf_op jit(solution)/shard_map/reduce_sum | solution.py:39
  277.7 2.5 fusion
  (4 shorter events, 0.0 us)
Async XLA Ops:
  0.0 2.2 copy-start
  2.9 92.0 %copy-start.2 = (bf16[1,7168,256]{2,1,0:T(8,128)(2,1)S(1)}, bf16[1,7168,256]{2,1,0:T(8,128)(2,1)}, u32[]{:S(2)}) copy-start(bf16[1,7168,256]{2,1,0:T(8,128)(2,1)} %param.9) | copy-start | bytes 11010052
  93.0 1.9 copy-start.1
  107.2 3.8 %copy-start.3 = (f32[8,2]{0,1:T(2,128)S(1)}, f32[8,2]{0,1:T(2,128)}, u32[]{:S(2)}) copy-start(f32[8,2]{0,1:T(2,128)} %param.8) | copy-start | bytes 196
  107.2 166.9 %all-to-all-start.1 = ((f32[32,8,7168]{2,1,0:T(8,128)}), f32[32,8,7168]{2,1,0:T(8,128)}, u32[]{:S(2)}, u32[]{:S(2)}) async-start(f32[32,8,7168]{2,1,0:T(8,128)} %fusion.1), calls=%async_computation.1 | async-start | bytes 14680064 | tf_op jit(solution)/shard_map/all_to_all | solution.py:38
where the time goes:
time: 280 us
  waiting for transfers between devices  163 us (58%)
  blocking collectives  90.1 us (32%)
  matrix products  15.2 us (5%)
  other arithmetic  4.74 us (2%)
  starting transfers between devices  3.77 us (1%)
  local copies, waits for them, and re-layouts  3.33 us (1%)
    all_to_all x1, waiting for transfers between devices, body(): lax.all_to_all(partial_value, 'local', split_axis=0, concat_axis=0, tiled...  163 us
    all_to_all x1, blocking collectives, body(): lax.all_to_all(outgoing, 'local', split_axis=0, concat_axis=0, tiled=True)  90.1 us
    dot_general x1, matrix products, body(): result = jnp.dot(hidden, down_weight[0], preferred_element_type=jnp.float32)  11.2 us
  transfers between devices with their start and end apart: 1, of which 1 were waited for; matrix products, arithmetic and copies ran while one was open for 0% of the time, Pallas kernels for 0%

commit v1 on v0

v1 whole, which is shorter than its diff:
```python
import jax
import jax.numpy as jnp
from jax import lax
from jax.sharding import PartitionSpec as P

SPLIT = 8
LANES = 128
GATHER_CHUNKS = 2
RETURN_CHUNKS = 2


def pieces(width, count):
    tiles = width // LANES
    edges = [tiles * i // count * LANES for i in range(count)] + [width]
    return list(zip(edges[:-1], edges[1:]))


def swap(members, mask):
    pairs = [(d, d ^ mask(d)) for d in range(members)]
    return lambda x: lax.ppermute(x, "local", pairs)


def body(tokens, routes, route_weight, gate_weight, up_weight, down_weight):
    members = lax.axis_size("local")
    experts = members // SPLIT
    rows_dev, features = tokens.shape
    rows = members * rows_dev
    fanout = routes.shape[1]

    expert_ids = jnp.arange(experts, dtype=jnp.int32)
    coef = sum(
        jnp.where(routes[:, k, None] == expert_ids, route_weight[:, k, None], 0.0)
        for k in range(fanout)
    )
    high = lax.reduce_precision(coef, 8, 7)
    middle = lax.reduce_precision(coef - high, 8, 7)
    low = coef - high - middle
    width = -(-3 * experts // LANES) * LANES
    terms = jnp.concatenate([high, middle, low], axis=1).astype(jnp.bfloat16)
    terms = jnp.pad(terms, ((0, 0), (0, width - 3 * experts)))

    outer = [swap(members, lambda d, e=e: e * SPLIT) for e in range(1, experts)]
    first = swap(members, lambda d: 4 if d & 1 else 2)
    second = swap(members, lambda d: 2 if d & 1 else 4)
    sibling = swap(members, lambda d: 1)

    def gather(x):
        x = jnp.concatenate([x] + [step(x) for step in outer], axis=0)
        for step in (first, second, sibling):
            x = jnp.concatenate([x, step(x)], axis=0)
        return x

    def give_back(x):
        for step in (sibling, second, first):
            kept, sent = jnp.split(x, 2, axis=0)
            x = kept + step(sent.astype(jnp.bfloat16)).astype(jnp.float32)
        blocks = jnp.split(x, experts, axis=0)
        total = blocks[0]
        for block, step in zip(blocks[1:], outer):
            total = total + step(block.astype(jnp.bfloat16)).astype(jnp.float32)
        return total.astype(jnp.bfloat16)

    gate_part = up_part = 0.0
    spans = pieces(features, GATHER_CHUNKS)
    for n, (lo, hi) in enumerate(spans):
        part = tokens[:, lo:hi]
        if n == len(spans) - 1:
            part = jnp.concatenate([part, terms], axis=1)
        lined = gather(part)
        if n == len(spans) - 1:
            arrived = lined[:, hi - lo :].astype(jnp.float32)
            lined = lined[:, : hi - lo]
        gate_part += jnp.dot(lined, gate_weight[0, lo:hi], preferred_element_type=jnp.float32)
        up_part += jnp.dot(lined, up_weight[0, lo:hi], preferred_element_type=jnp.float32)
    hidden = (jax.nn.silu(gate_part) * up_part).astype(jnp.bfloat16)

    mine = lax.axis_index("local") // SPLIT
    column = jnp.arange(width, dtype=jnp.int32)
    wanted = (column % experts == mine) & (column < 3 * experts)
    scale = jnp.sum(jnp.where(wanted, arrived, 0.0), axis=1, keepdims=True)

    results = []
    for lo, hi in pieces(features, RETURN_CHUNKS):
        result = jnp.dot(hidden, down_weight[0, :, lo:hi], preferred_element_type=jnp.float32)
        results.append(give_back(result * scale))
    return jnp.concatenate(results, axis=1)


def solution(mesh):
    return jax.shard_map(
        body,
        mesh=mesh,
        in_specs=(
            P(("parts", "local"), None),
            P(("parts", "local"), None),
            P(("parts", "local"), None),
            P("local", None, None),
            P("local", None, None),
            P("local", None, None),
        ),
        out_specs=P(("parts", "local"), None),
        check_vma=False,
    )
```

time: 280 us -> 83.7 us (0.30)
  waiting for transfers between devices: 163 us -> 31 us
  blocking collectives: 90.1 us -> 0 us
  starting transfers between devices: 3.77 us -> 31.7 us
  local copies, waits for them, and re-layouts: 3.33 us -> 13.3 us
  matrix products: 15.2 us -> 5.52 us
  other arithmetic: 4.74 us -> 1.66 us
    all_to_all x1 -> x0, waiting for transfers between devices: 163 us -> none  [body(): lax.all_to_all(partial_value, 'local', split_axis=0, concat_axis=0, tiled...]
    all_to_all x1 -> x0, blocking collectives: 90.1 us -> none  [body(): lax.all_to_all(outgoing, 'local', split_axis=0, concat_axis=0, tiled=True)]
    ppermute x0 -> x24, starting transfers between devices: none -> 31.7 us  [swap(): return lambda x: lax.ppermute(x, 'local', pairs)]
    ppermute x0 -> x24, waiting for transfers between devices: none -> 31 us  [swap(): return lambda x: lax.ppermute(x, 'local', pairs)]
    dot_general x5 -> x6, matrix products: 15.2 us -> 5.52 us  [the longest x2 2.92 us: body(): jnp.dot(lined, gate_weight[0, lo:hi], preferred_element_type=jnp.float32)]
    unnamed x9 -> x23, local copies, waits for them, and re-layouts: 2.68 us -> 8.48 us
    all_to_all x1 -> x0, starting transfers between devices: 3.77 us -> none  [body(): lax.all_to_all(partial_value, 'local', split_axis=0, concat_axis=0, tiled...]
    reduce_sum x3 -> x1, other arithmetic: 3.84 us -> 0.11 us  [body(): scale = jnp.sum(jnp.where(wanted, arrived, 0.0), axis=1, keepdims=True)]
  transfers between devices with their start and end apart: 1 -> 24, of which waited for: 1 -> 12; matrix products, arithmetic and copies ran while one was open for 0% -> 10% of each run, Pallas kernels for 0% -> 0%
where the time goes in v1:
time: 83.7 us; the launch traced here: 83.4 us
  starting transfers between devices  31.7 us (38%)
  waiting for transfers between devices  31 us (37%)
  local copies, waits for them, and re-layouts  13.3 us (16%)
  matrix products  5.52 us (7%)
  other arithmetic  1.66 us (2%)
    ppermute x24, starting transfers between devices, swap(): return lambda x: lax.ppermute(x, 'local', pairs)  31.7 us
    ppermute x24, waiting for transfers between devices, swap(): return lambda x: lax.ppermute(x, 'local', pairs)  31 us
    unnamed x23, local copies, waits for them, and re-layouts  8.48 us
    concatenate x4, local copies, waits for them, and re-layouts, gather(): x = jnp.concatenate([x, step(x)], axis=0)  2.92 us
    dot_general x2, matrix products, body(): jnp.dot(lined, gate_weight[0, lo:hi], preferred_element_type=jnp.float32)  2.92 us
  transfers between devices with their start and end apart: 24, of which 12 were waited for; matrix products, arithmetic and copies ran while one was open for 10% of the time, Pallas kernels for 0%

profile of v1, /device:TPU:0, one launch (start us, length us, event | category | flops | bytes accessed | tf_op | source)
XLA Modules:
  0.0 83.4 jit_solution(11951404246193687491)
XLA Ops:
  0.0 1.5 %constant_dynamic-update-slice_fusion.10 = (bf16[128,3584]{1,0:T(8,128)(2,1)}, bf16[64,3584]{1,0:T(8,128)(2,1)S(1)}, bf16[256,3584]{1,0:T(8,128)(2,1)S(1)}, bf16[8,3584]{1,0:T(8,128)(2,1)S(1)}, bf16[8,3584]{1,0:T(8,128)(2,1)S(1)}) fusion(bf16[8,7168]{1,0:T(8,128)(2,1)} %param.6), kind=kLoop, calls=%fused_computation.57 | loop fusion | bytes 401408
  1.5 3.0 %collective-permute-start = (bf16[8,3584]{1,0:T(8,128)(2,1)S(1)}, bf16[8,3584]{1,0:T(8,128)(2,1)S(1)}, u32[]{:S(2)}, u32[]{:S(2)}) collective-permute-start(bf16[8,3584]{1,0:T(8,128)(2,1)S(1)} %get-tuple-element.29), channel_id=1, source_target_pairs={{0,8},{1,9},{2,10},{3,11},{4,12},{5,13},{6,14},{7,15},{8,0},{9,1},... | collective-permute-start | bytes 172040 | tf_op jit(solution)/shard_map/ppermute | solution.py:20
  4.5 2.6 %collective-permute-start.1 = (bf16[8,3584]{1,0:T(8,128)(2,1)S(1)}, bf16[8,3584]{1,0:T(8,128)(2,1)S(1)}, u32[]{:S(2)}, u32[]{:S(2)}) collective-permute-start(bf16[8,3584]{1,0:T(8,128)(2,1)S(1)} %get-tuple-element.29), channel_id=1, source_target_pairs={{0,16},{1,17},{2,18},{3,19},{4,20},{5,21},{6,22},{7,23},{8,24},{9,... | collective-permute-start | bytes 172040 | tf_op jit(solution)/shard_map/ppermute | solution.py:20
  9.8 3.5 %collective-permute-start.7 = (bf16[8,3712]{1,0:T(8,128)(2,1)S(1)}, bf16[8,3712]{1,0:T(8,128)(2,1)S(1)}, u32[]{:S(2)}, u32[]{:S(2)}) collective-permute-start(bf16[8,3712]{1,0:T(8,128)(2,1)S(1)} %get-tuple-element.42), channel_id=1, source_target_pairs={{0,16},{1,17},{2,18},{3,19},{4,20},{5,21},{6,22},{7,23},{8,24},{9,... | collective-permute-start | bytes 178184 | tf_op jit(solution)/shard_map/ppermute | solution.py:20
  13.7 1.6 %collective-permute-start.3 = (bf16[32,3584]{1,0:T(8,128)(2,1)S(1)}, bf16[32,3584]{1,0:T(8,128)(2,1)S(1)}, u32[]{:S(2)}, u32[]{:S(2)}) collective-permute-start(bf16[32,3584]{1,0:T(8,128)(2,1)S(1)} %pad_maximum_fusion.1), channel_id=1, source_target_pairs={{0,2},{1,5},{2,0},{3,7},{4,6},{5,1},{6,4},{7,3},{8,10},{9,13},{10,... | collective-permute-start | bytes 688136 | tf_op jit(solution)/shard_map/ppermute | solution.py:20
  17.2 2.1 %collective-permute-done.8 = bf16[8,3712]{1,0:T(8,128)(2,1)S(1)} collective-permute-done((bf16[8,3712]{1,0:T(8,128)(2,1)S(1)}, bf16[8,3712]{1,0:T(8,128)(2,1)S(1)}, u32[]{:S(2)}, u32[]{:S(2)}) %collective-permute-start.8) | collective-permute-done | bytes 59424 | tf_op jit(solution)/shard_map/ppermute | solution.py:20
  19.3 1.6 %collective-permute-start.9 = (bf16[32,3712]{1,0:T(8,128)(2,1)S(1)}, bf16[32,3712]{1,0:T(8,128)(2,1)S(1)}, u32[]{:S(2)}, u32[]{:S(2)}) collective-permute-start(bf16[32,3712]{1,0:T(8,128)(2,1)S(1)} %pad_maximum_fusion), channel_id=1, source_target_pairs={{0,2},{1,5},{2,0},{3,7},{4,6},{5,1},{6,4},{7,3},{8,10},{9,13},{10,... | collective-permute-start | bytes 712712 | tf_op jit(solution)/shard_map/ppermute | solution.py:20
  21.6 1.5 %collective-permute-start.4 = (bf16[64,3584]{1,0:T(8,128)(2,1)S(1)}, bf16[64,3584]{1,0:T(8,128)(2,1)S(1)}, u32[]{:S(2)}, u32[]{:S(2)}) collective-permute-start(bf16[64,3584]{1,0:T(8,128)(2,1)S(1)} %get-tuple-element.24), channel_id=1, source_target_pairs={{0,4},{1,3},{2,6},{3,1},{4,0},{5,7},{6,2},{7,5},{8,12},{9,11},{10,... | collective-permute-start | bytes 1376264 | tf_op jit(solution)/shard_map/ppermute | solution.py:20
  23.2 4.9 %collective-permute-done.9 = bf16[32,3712]{1,0:T(8,128)(2,1)S(1)} collective-permute-done((bf16[32,3712]{1,0:T(8,128)(2,1)S(1)}, bf16[32,3712]{1,0:T(8,128)(2,1)S(1)}, u32[]{:S(2)}, u32[]{:S(2)}) %collective-permute-start.9) | collective-permute-done | bytes 237600 | tf_op jit(solution)/shard_map/ppermute | solution.py:20
  28.1 1.6 %collective-permute-start.10 = (bf16[64,3712]{1,0:T(8,128)(2,1)S(1)}, bf16[64,3712]{1,0:T(8,128)(2,1)S(1)}, u32[]{:S(2)}, u32[]{:S(2)}) collective-permute-start(bf16[64,3712]{1,0:T(8,128)(2,1)S(1)} %get-tuple-element.15), channel_id=1, source_target_pairs={{0,4},{1,3},{2,6},{3,1},{4,0},{5,7},{6,2},{7,5},{8,12},{9,11},{10,... | collective-permute-start | bytes 1425416 | tf_op jit(solution)/shard_map/ppermute | solution.py:20
  31.0 5.9 %collective-permute-done.10 = bf16[64,3712]{1,0:T(8,128)(2,1)S(1)} collective-permute-done((bf16[64,3712]{1,0:T(8,128)(2,1)S(1)}, bf16[64,3712]{1,0:T(8,128)(2,1)S(1)}, u32[]{:S(2)}, u32[]{:S(2)}) %collective-permute-start.10) | collective-permute-done | bytes 475168 | tf_op jit(solution)/shard_map/ppermute | solution.py:20
  37.0 1.3 %copy-done.1 = bf16[256,3712]{1,0:T(8,128)(2,1)} copy-done((bf16[256,3712]{1,0:T(8,128)(2,1)}, bf16[256,3712]{1,0:T(8,128)(2,1)S(1)}, u32[]{:S(2)}) %copy-start.1) | copy-done | bytes 1900568
  39.3 1.5 %collective-permute-done.11 = bf16[128,3712]{1,0:T(8,128)(2,1)S(1)} collective-permute-done((bf16[128,3712]{1,0:T(8,128)(2,1)S(1)}, bf16[128,3712]{1,0:T(8,128)(2,1)S(1)}, u32[]{:S(2)}, u32[]{:S(2)}) %collective-permute-start.11) | collective-permute-done | bytes 950304 | tf_op jit(solution)/shard_map/ppermute | solution.py:20
  41.8 2.3 %fusion.6 = f32[256,256]{1,0:T(8,128)S(1)} fusion(bf16[1,7168,256]{2,1,0:T(8,128)(2,1)S(1)} %copy-done.5, bf16[256,3712]{1,0:T(8,128)(2,1)} %constant_dynamic-update-slice_fusion.29), kind=kOutput, calls=%fused_computation.12 | convolution fusion | flops 469762048 | bytes 3932160 | tf_op jit(solution)/shard_map/dot_general | solution.py:73
  47.7 1.4 %copy-done = bf16[1,256,7168]{2,1,0:T(8,128)(2,1)S(1)} copy-done((bf16[1,256,7168]{2,1,0:T(8,128)(2,1)S(1)}, bf16[1,256,7168]{2,1,0:T(8,128)(2,1)}, u32[]{:S(2)}) %copy-start) | copy-done | bytes 3670040
  52.6 1.6 %collective-permute-start.13 = (bf16[64,3584]{1,0:T(8,128)(2,1)S(1)}, bf16[64,3584]{1,0:T(8,128)(2,1)S(1)}, u32[]{:S(2)}, u32[]{:S(2)}) collective-permute-start(bf16[64,3584]{1,0:T(8,128)(2,1)S(1)} %split.141), channel_id=1, source_target_pairs={{0,4},{1,3},{2,6},{3,1},{4,0},{5,7},{6,2},{7,5},{8,12},{9,11},{10,... | collective-permute-start | bytes 1376264 | tf_op jit(solution)/shard_map/ppermute | solution.py:20
  55.5 5.6 %collective-permute-done.13 = bf16[64,3584]{1,0:T(8,128)(2,1)S(1)} collective-permute-done((bf16[64,3584]{1,0:T(8,128)(2,1)S(1)}, bf16[64,3584]{1,0:T(8,128)(2,1)S(1)}, u32[]{:S(2)}, u32[]{:S(2)}) %collective-permute-start.13) | collective-permute-done | bytes 458784 | tf_op jit(solution)/shard_map/ppermute | solution.py:20
  61.3 1.6 %collective-permute-start.14 = (bf16[32,3584]{1,0:T(8,128)(2,1)S(1)}, bf16[32,3584]{1,0:T(8,128)(2,1)S(1)}, u32[]{:S(2)}, u32[]{:S(2)}) collective-permute-start(bf16[32,3584]{1,0:T(8,128)(2,1)S(1)} %split.143), channel_id=1, source_target_pairs={{0,2},{1,5},{2,0},{3,7},{4,6},{5,1},{6,4},{7,3},{8,10},{9,13},{10,... | collective-permute-start | bytes 688136 | tf_op jit(solution)/shard_map/ppermute | solution.py:20
  62.8 5.7 %collective-permute-done.19 = bf16[64,3584]{1,0:T(8,128)(2,1)S(1)} collective-permute-done((bf16[64,3584]{1,0:T(8,128)(2,1)S(1)}, bf16[64,3584]{1,0:T(8,128)(2,1)S(1)}, u32[]{:S(2)}, u32[]{:S(2)}) %collective-permute-start.19) | collective-permute-done | bytes 458784 | tf_op jit(solution)/shard_map/ppermute | solution.py:20
  68.7 1.6 %collective-permute-start.20 = (bf16[32,3584]{1,0:T(8,128)(2,1)S(1)}, bf16[32,3584]{1,0:T(8,128)(2,1)S(1)}, u32[]{:S(2)}, u32[]{:S(2)}) collective-permute-start(bf16[32,3584]{1,0:T(8,128)(2,1)S(1)} %split.142), channel_id=1, source_target_pairs={{0,2},{1,5},{2,0},{3,7},{4,6},{5,1},{6,4},{7,3},{8,10},{9,13},{10,... | collective-permute-start | bytes 688136 | tf_op jit(solution)/shard_map/ppermute | solution.py:20
  71.7 3.1 %collective-permute-start.17 = (bf16[8,3584]{1,0:T(8,128)(2,1)S(1)}, bf16[8,3584]{1,0:T(8,128)(2,1)S(1)}, u32[]{:S(2)}, u32[]{:S(2)}) collective-permute-start(bf16[8,3584]{1,0:T(8,128)(2,1)S(1)} %get-tuple-element.17), channel_id=1, source_target_pairs={{0,24},{1,25},{2,26},{3,27},{4,28},{5,29},{6,30},{7,31},{8,16},{9,... | collective-permute-start | bytes 172040 | tf_op jit(solution)/shard_map/ppermute | solution.py:20
  75.0 1.8 %collective-permute-start.22 = (bf16[8,3584]{1,0:T(8,128)(2,1)S(1)}, bf16[8,3584]{1,0:T(8,128)(2,1)S(1)}, u32[]{:S(2)}, u32[]{:S(2)}) collective-permute-start(bf16[8,3584]{1,0:T(8,128)(2,1)S(1)} %get-tuple-element.21), channel_id=1, source_target_pairs={{0,16},{1,17},{2,18},{3,19},{4,20},{5,21},{6,22},{7,23},{8,24},{9,... | collective-permute-start | bytes 172040 | tf_op jit(solution)/shard_map/ppermute | solution.py:20
  76.7 2.6 %collective-permute-start.23 = (bf16[8,3584]{1,0:T(8,128)(2,1)S(1)}, bf16[8,3584]{1,0:T(8,128)(2,1)S(1)}, u32[]{:S(2)}, u32[]{:S(2)}) collective-permute-start(bf16[8,3584]{1,0:T(8,128)(2,1)S(1)} %get-tuple-element.20), channel_id=1, source_target_pairs={{0,24},{1,25},{2,26},{3,27},{4,28},{5,29},{6,30},{7,31},{8,16},{9,... | collective-permute-start | bytes 172040 | tf_op jit(solution)/shard_map/ppermute | solution.py:20
  80.5 2.2 %collective-permute-done.23 = bf16[8,3584]{1,0:T(8,128)(2,1)S(1)} collective-permute-done((bf16[8,3584]{1,0:T(8,128)(2,1)S(1)}, bf16[8,3584]{1,0:T(8,128)(2,1)S(1)}, u32[]{:S(2)}, u32[]{:S(2)}) %collective-permute-start.23) | collective-permute-done | bytes 57376 | tf_op jit(solution)/shard_map/ppermute | solution.py:20
  (83 shorter events, 21.2 us)
Async XLA Ops:
  1.5 11.8 %collective-permute-start = (bf16[8,3584]{1,0:T(8,128)(2,1)S(1)}, bf16[8,3584]{1,0:T(8,128)(2,1)S(1)}, u32[]{:S(2)}, u32[]{:S(2)}) collective-permute-start(bf16[8,3584]{1,0:T(8,128)(2,1)S(1)} %get-tuple-element.29), channel_id=1, source_target_pairs={{0,8},{1,9},{2,10},{3,11},{4,12},{5,13},{6,14},{7,15},{8,0},{9,1},... | collective-permute-start | bytes 172040 | tf_op jit(solution)/shard_map/ppermute | solution.py:20
  4.5 8.8 %collective-permute-start.1 = (bf16[8,3584]{1,0:T(8,128)(2,1)S(1)}, bf16[8,3584]{1,0:T(8,128)(2,1)S(1)}, u32[]{:S(2)}, u32[]{:S(2)}) collective-permute-start(bf16[8,3584]{1,0:T(8,128)(2,1)S(1)} %get-tuple-element.29), channel_id=1, source_target_pairs={{0,16},{1,17},{2,18},{3,19},{4,20},{5,21},{6,22},{7,23},{8,24},{9,... | collective-permute-start | bytes 172040 | tf_op jit(solution)/shard_map/ppermute | solution.py:20
  7.1 6.6 %collective-permute-start.2 = (bf16[8,3584]{1,0:T(8,128)(2,1)S(1)}, bf16[8,3584]{1,0:T(8,128)(2,1)S(1)}, u32[]{:S(2)}, u32[]{:S(2)}) collective-permute-start(bf16[8,3584]{1,0:T(8,128)(2,1)S(1)} %get-tuple-element.29), channel_id=1, source_target_pairs={{0,24},{1,25},{2,26},{3,27},{4,28},{5,29},{6,30},{7,31},{8,16},{9,... | collective-permute-start | bytes 172040 | tf_op jit(solution)/shard_map/ppermute | solution.py:20
  8.8 8.4 %collective-permute-start.6 = (bf16[8,3712]{1,0:T(8,128)(2,1)S(1)}, bf16[8,3712]{1,0:T(8,128)(2,1)S(1)}, u32[]{:S(2)}, u32[]{:S(2)}) collective-permute-start(bf16[8,3712]{1,0:T(8,128)(2,1)S(1)} %get-tuple-element.42), channel_id=1, source_target_pairs={{0,8},{1,9},{2,10},{3,11},{4,12},{5,13},{6,14},{7,15},{8,0},{9,1},... | collective-permute-start | bytes 178184 | tf_op jit(solution)/shard_map/ppermute | solution.py:20
  9.8 7.4 %collective-permute-start.7 = (bf16[8,3712]{1,0:T(8,128)(2,1)S(1)}, bf16[8,3712]{1,0:T(8,128)(2,1)S(1)}, u32[]{:S(2)}, u32[]{:S(2)}) collective-permute-start(bf16[8,3712]{1,0:T(8,128)(2,1)S(1)} %get-tuple-element.42), channel_id=1, source_target_pairs={{0,16},{1,17},{2,18},{3,19},{4,20},{5,21},{6,22},{7,23},{8,24},{9,... | collective-permute-start | bytes 178184 | tf_op jit(solution)/shard_map/ppermute | solution.py:20
  13.3 6.0 %collective-permute-start.8 = (bf16[8,3712]{1,0:T(8,128)(2,1)S(1)}, bf16[8,3712]{1,0:T(8,128)(2,1)S(1)}, u32[]{:S(2)}, u32[]{:S(2)}) collective-permute-start(bf16[8,3712]{1,0:T(8,128)(2,1)S(1)} %get-tuple-element.42), channel_id=1, source_target_pairs={{0,24},{1,25},{2,26},{3,27},{4,28},{5,29},{6,30},{7,31},{8,16},{9,... | collective-permute-start | bytes 178184 | tf_op jit(solution)/shard_map/ppermute | solution.py:20
  13.7 7.2 %collective-permute-start.3 = (bf16[32,3584]{1,0:T(8,128)(2,1)S(1)}, bf16[32,3584]{1,0:T(8,128)(2,1)S(1)}, u32[]{:S(2)}, u32[]{:S(2)}) collective-permute-start(bf16[32,3584]{1,0:T(8,128)(2,1)S(1)} %pad_maximum_fusion.1), channel_id=1, source_target_pairs={{0,2},{1,5},{2,0},{3,7},{4,6},{5,1},{6,4},{7,3},{8,10},{9,13},{10,... | collective-permute-start | bytes 688136 | tf_op jit(solution)/shard_map/ppermute | solution.py:20
  19.3 8.8 %collective-permute-start.9 = (bf16[32,3712]{1,0:T(8,128)(2,1)S(1)}, bf16[32,3712]{1,0:T(8,128)(2,1)S(1)}, u32[]{:S(2)}, u32[]{:S(2)}) collective-permute-start(bf16[32,3712]{1,0:T(8,128)(2,1)S(1)} %pad_maximum_fusion), channel_id=1, source_target_pairs={{0,2},{1,5},{2,0},{3,7},{4,6},{5,1},{6,4},{7,3},{8,10},{9,13},{10,... | collective-permute-start | bytes 712712 | tf_op jit(solution)/shard_map/ppermute | solution.py:20
  21.6 8.5 %collective-permute-start.4 = (bf16[64,3584]{1,0:T(8,128)(2,1)S(1)}, bf16[64,3584]{1,0:T(8,128)(2,1)S(1)}, u32[]{:S(2)}, u32[]{:S(2)}) collective-permute-start(bf16[64,3584]{1,0:T(8,128)(2,1)S(1)} %get-tuple-element.24), channel_id=1, source_target_pairs={{0,4},{1,3},{2,6},{3,1},{4,0},{5,7},{6,2},{7,5},{8,12},{9,11},{10,... | collective-permute-start | bytes 1376264 | tf_op jit(solution)/shard_map/ppermute | solution.py:20
  28.1 8.7 %collective-permute-start.10 = (bf16[64,3712]{1,0:T(8,128)(2,1)S(1)}, bf16[64,3712]{1,0:T(8,128)(2,1)S(1)}, u32[]{:S(2)}, u32[]{:S(2)}) collective-permute-start(bf16[64,3712]{1,0:T(8,128)(2,1)S(1)} %get-tuple-element.15), channel_id=1, source_target_pairs={{0,4},{1,3},{2,6},{3,1},{4,0},{5,7},{6,2},{7,5},{8,12},{9,11},{10,... | collective-permute-start | bytes 1425416 | tf_op jit(solution)/shard_map/ppermute | solution.py:20
  31.0 7.3 %collective-permute-start.5 = (bf16[128,3584]{1,0:T(8,128)(2,1)}, bf16[128,3584]{1,0:T(8,128)(2,1)S(1)}, u32[]{:S(2)}, u32[]{:S(2)}) collective-permute-start(bf16[128,3584]{1,0:T(8,128)(2,1)} %get-tuple-element.11), channel_id=1, source_target_pairs={{0,1},{1,0},{2,3},{3,2},{4,5},{5,4},{6,7},{7,6},{8,9},{9,8},{10,11... | collective-permute-start | bytes 2752520 | tf_op jit(solution)/shard_map/ppermute | solution.py:20
  38.2 2.5 %collective-permute-start.11 = (bf16[128,3712]{1,0:T(8,128)(2,1)S(1)}, bf16[128,3712]{1,0:T(8,128)(2,1)S(1)}, u32[]{:S(2)}, u32[]{:S(2)}) collective-permute-start(bf16[128,3712]{1,0:T(8,128)(2,1)S(1)} %get-tuple-element.9), channel_id=1, source_target_pairs={{0,1},{1,0},{2,3},{3,2},{4,5},{5,4},{6,7},{7,6},{8,9},{9,8},{10,11... | collective-permute-start | bytes 2850824 | tf_op jit(solution)/shard_map/ppermute | solution.py:20
  49.9 2.5 %collective-permute-start.12 = (bf16[128,3584]{1,0:T(8,128)(2,1)S(1)}, bf16[128,3584]{1,0:T(8,128)(2,1)S(1)}, u32[]{:S(2)}, u32[]{:S(2)}) collective-permute-start(bf16[128,3584]{1,0:T(8,128)(2,1)S(1)} %split.139), channel_id=1, source_target_pairs={{0,1},{1,0},{2,3},{3,2},{4,5},{5,4},{6,7},{7,6},{8,9},{9,8},{10,11... | collective-permute-start | bytes 2752520 | tf_op jit(solution)/shard_map/ppermute | solution.py:20
  50.8 3.4 %collective-permute-start.18 = (bf16[128,3584]{1,0:T(8,128)(2,1)S(1)}, bf16[128,3584]{1,0:T(8,128)(2,1)S(1)}, u32[]{:S(2)}, u32[]{:S(2)}) collective-permute-start(bf16[128,3584]{1,0:T(8,128)(2,1)S(1)} %split.138), channel_id=1, source_target_pairs={{0,1},{1,0},{2,3},{3,2},{4,5},{5,4},{6,7},{7,6},{8,9},{9,8},{10,11... | collective-permute-start | bytes 2752520 | tf_op jit(solution)/shard_map/ppermute | solution.py:20
  52.6 8.5 %collective-permute-start.13 = (bf16[64,3584]{1,0:T(8,128)(2,1)S(1)}, bf16[64,3584]{1,0:T(8,128)(2,1)S(1)}, u32[]{:S(2)}, u32[]{:S(2)}) collective-permute-start(bf16[64,3584]{1,0:T(8,128)(2,1)S(1)} %split.141), channel_id=1, source_target_pairs={{0,4},{1,3},{2,6},{3,1},{4,0},{5,7},{6,2},{7,5},{8,12},{9,11},{10,... | collective-permute-start | bytes 1376264 | tf_op jit(solution)/shard_map/ppermute | solution.py:20
  54.5 14.1 %collective-permute-start.19 = (bf16[64,3584]{1,0:T(8,128)(2,1)S(1)}, bf16[64,3584]{1,0:T(8,128)(2,1)S(1)}, u32[]{:S(2)}, u32[]{:S(2)}) collective-permute-start(bf16[64,3584]{1,0:T(8,128)(2,1)S(1)} %split.140), channel_id=1, source_target_pairs={{0,4},{1,3},{2,6},{3,1},{4,0},{5,7},{6,2},{7,5},{8,12},{9,11},{10,... | collective-permute-start | bytes 1376264 | tf_op jit(solution)/shard_map/ppermute | solution.py:20
  61.3 9.0 %collective-permute-start.14 = (bf16[32,3584]{1,0:T(8,128)(2,1)S(1)}, bf16[32,3584]{1,0:T(8,128)(2,1)S(1)}, u32[]{:S(2)}, u32[]{:S(2)}) collective-permute-start(bf16[32,3584]{1,0:T(8,128)(2,1)S(1)} %split.143), channel_id=1, source_target_pairs={{0,2},{1,5},{2,0},{3,7},{4,6},{5,1},{6,4},{7,3},{8,10},{9,13},{10,... | collective-permute-start | bytes 688136 | tf_op jit(solution)/shard_map/ppermute | solution.py:20
  68.7 6.1 %collective-permute-start.20 = (bf16[32,3584]{1,0:T(8,128)(2,1)S(1)}, bf16[32,3584]{1,0:T(8,128)(2,1)S(1)}, u32[]{:S(2)}, u32[]{:S(2)}) collective-permute-start(bf16[32,3584]{1,0:T(8,128)(2,1)S(1)} %split.142), channel_id=1, source_target_pairs={{0,2},{1,5},{2,0},{3,7},{4,6},{5,1},{6,4},{7,3},{8,10},{9,13},{10,... | collective-permute-start | bytes 688136 | tf_op jit(solution)/shard_map/ppermute | solution.py:20
  70.4 6.4 %collective-permute-start.15 = (bf16[8,3584]{1,0:T(8,128)(2,1)S(1)}, bf16[8,3584]{1,0:T(8,128)(2,1)S(1)}, u32[]{:S(2)}, u32[]{:S(2)}) collective-permute-start(bf16[8,3584]{1,0:T(8,128)(2,1)S(1)} %get-tuple-element.16), channel_id=1, source_target_pairs={{0,8},{1,9},{2,10},{3,11},{4,12},{5,13},{6,14},{7,15},{8,0},{9,1},... | collective-permute-start | bytes 172040 | tf_op jit(solution)/shard_map/ppermute | solution.py:20
  70.4 8.9 %collective-permute-start.16 = (bf16[8,3584]{1,0:T(8,128)(2,1)S(1)}, bf16[8,3584]{1,0:T(8,128)(2,1)S(1)}, u32[]{:S(2)}, u32[]{:S(2)}) collective-permute-start(bf16[8,3584]{1,0:T(8,128)(2,1)S(1)} %get-tuple-element.18), channel_id=1, source_target_pairs={{0,16},{1,17},{2,18},{3,19},{4,20},{5,21},{6,22},{7,23},{8,24},{9,... | collective-permute-start | bytes 172040 | tf_op jit(solution)/shard_map/ppermute | solution.py:20
  71.7 7.7 %collective-permute-start.17 = (bf16[8,3584]{1,0:T(8,128)(2,1)S(1)}, bf16[8,3584]{1,0:T(8,128)(2,1)S(1)}, u32[]{:S(2)}, u32[]{:S(2)}) collective-permute-start(bf16[8,3584]{1,0:T(8,128)(2,1)S(1)} %get-tuple-element.17), channel_id=1, source_target_pairs={{0,24},{1,25},{2,26},{3,27},{4,28},{5,29},{6,30},{7,31},{8,16},{9,... | collective-permute-start | bytes 172040 | tf_op jit(solution)/shard_map/ppermute | solution.py:20
  74.9 5.1 %collective-permute-start.21 = (bf16[8,3584]{1,0:T(8,128)(2,1)S(1)}, bf16[8,3584]{1,0:T(8,128)(2,1)S(1)}, u32[]{:S(2)}, u32[]{:S(2)}) collective-permute-start(bf16[8,3584]{1,0:T(8,128)(2,1)S(1)} %get-tuple-element.19), channel_id=1, source_target_pairs={{0,8},{1,9},{2,10},{3,11},{4,12},{5,13},{6,14},{7,15},{8,0},{9,1},... | collective-permute-start | bytes 172040 | tf_op jit(solution)/shard_map/ppermute | solution.py:20
  75.0 5.6 %collective-permute-start.22 = (bf16[8,3584]{1,0:T(8,128)(2,1)S(1)}, bf16[8,3584]{1,0:T(8,128)(2,1)S(1)}, u32[]{:S(2)}, u32[]{:S(2)}) collective-permute-start(bf16[8,3584]{1,0:T(8,128)(2,1)S(1)} %get-tuple-element.21), channel_id=1, source_target_pairs={{0,16},{1,17},{2,18},{3,19},{4,20},{5,21},{6,22},{7,23},{8,24},{9,... | collective-permute-start | bytes 172040 | tf_op jit(solution)/shard_map/ppermute | solution.py:20
  76.7 6.0 %collective-permute-start.23 = (bf16[8,3584]{1,0:T(8,128)(2,1)S(1)}, bf16[8,3584]{1,0:T(8,128)(2,1)S(1)}, u32[]{:S(2)}, u32[]{:S(2)}) collective-permute-start(bf16[8,3584]{1,0:T(8,128)(2,1)S(1)} %get-tuple-element.20), channel_id=1, source_target_pairs={{0,24},{1,25},{2,26},{3,27},{4,28},{5,29},{6,30},{7,31},{8,16},{9,... | collective-permute-start | bytes 172040 | tf_op jit(solution)/shard_map/ppermute | solution.py:20
  (7 other events, 21.1 us)

commit v2 on v0

v2 whole, which is shorter than its diff:
```python
import functools

import jax
import jax.numpy as jnp
from jax import lax
from jax.experimental import pallas as pl
from jax.experimental.pallas import tpu as pltpu
from jax.sharding import PartitionSpec as P

SPLIT = 8
LANES = 128
TILE = 512
MIB = 1 << 20
F32, BF16 = jnp.float32, jnp.bfloat16

VMEM = pl.BlockSpec(memory_space=pltpu.VMEM)
ANY = pl.BlockSpec(memory_space=pl.ANY)
HBM = pl.BlockSpec(memory_space=pltpu.HBM)
FREE = pl.CostEstimate(flops=0, bytes_accessed=0, transcendentals=0)


def swap(members, mask):
    pairs = [(d, d ^ mask(d)) for d in range(members)]
    return lambda x: lax.ppermute(x, "local", pairs)


def call(kernel, outs, operands, after=(), limit=8, scratch=()):
    count = len(operands)

    def run(*refs):
        kernel(*refs[:count], *refs[count + len(after) :])

    return pl.pallas_call(
        run,
        out_shape=[pltpu.VMEM(o.shape, o.dtype) for o in outs],
        in_specs=[VMEM] * count + [ANY] * len(after),
        out_specs=[VMEM] * len(outs),
        scratch_shapes=scratch,
        compiler_params=pltpu.CompilerParams(vmem_limit_bytes=limit * MIB),
        cost_estimate=FREE,
    )(*operands, *after)


def shape(rows, columns, dtype):
    return jax.ShapeDtypeStruct((rows, columns), dtype)


def pack_kernel(experts, tokens_hbm, routes_hbm, weight_hbm, out_ref, tokens_ref, routes_ref, weight_ref, sems):
    rows, features = tokens_ref.shape
    copies = [
        pltpu.make_async_copy(routes_hbm, routes_ref, sems.at[0]),
        pltpu.make_async_copy(weight_hbm, weight_ref, sems.at[1]),
        pltpu.make_async_copy(tokens_hbm, tokens_ref, sems.at[2]),
    ]
    for copy in copies:
        copy.start()
    for copy in copies:
        copy.wait()
    out_ref[:, :features] = tokens_ref[...]
    width = out_ref.shape[1] - features
    column = lax.broadcasted_iota(jnp.int32, (rows, width), 1)
    square = (rows, rows)
    own = lax.broadcasted_iota(jnp.int32, square, 0) == lax.broadcasted_iota(jnp.int32, square, 1)
    coef = jnp.zeros((rows, width), F32)
    for k in range(routes_ref.shape[0]):
        route = jnp.sum(jnp.where(own, routes_ref[k : k + 1, :], 0), axis=1, keepdims=True)
        weight = jnp.sum(jnp.where(own, weight_ref[k : k + 1, :], 0.0), axis=1, keepdims=True)
        coef += jnp.where(lax.rem(column, experts) == route, weight, 0.0)
    high = coef.astype(BF16).astype(F32)
    middle = (coef - high).astype(BF16).astype(F32)
    low = coef - high - middle
    terms = jnp.where(column < experts, high, jnp.where(column < 2 * experts, middle, low))
    out_ref[:, features:] = jnp.where(column < 3 * experts, terms, 0.0).astype(BF16)


def stack_kernel(a_ref, b_ref, out_ref):
    out_ref[...] = jnp.concatenate([a_ref[...], b_ref[...]], axis=0)


def gate_kernel(pieces, experts, mine_ref, *refs):
    x_refs, (gate_ref, up_ref), (hidden_ref, scale_ref) = refs[:pieces], refs[pieces : pieces + 2], refs[-2:]
    features = gate_ref.shape[0]
    gate = up = jnp.zeros(hidden_ref.shape, F32)
    for lo in range(0, features, TILE):
        x = jnp.concatenate([r[:, lo : lo + TILE] for r in x_refs], axis=0)
        gate += jnp.dot(x, gate_ref[lo : lo + TILE, :], preferred_element_type=F32)
        up += jnp.dot(x, up_ref[lo : lo + TILE, :], preferred_element_type=F32)
    hidden_ref[...] = (jax.nn.silu(gate) * up).astype(BF16)
    terms = jnp.concatenate([r[:, features:] for r in x_refs], axis=0).astype(F32)
    column = lax.broadcasted_iota(jnp.int32, terms.shape, 1)
    wanted = (lax.rem(column, experts) == mine_ref[0]) & (column < 3 * experts)
    scale = jnp.sum(jnp.where(wanted, terms, 0.0), axis=1, keepdims=True)
    scale_ref[...] = jnp.broadcast_to(scale, scale_ref.shape)


def down_kernel(start, hidden_ref, scale_ref, down_ref, kept_ref, sent_ref):
    half, features = kept_ref.shape
    hidden = hidden_ref[start : start + 2 * half, :]
    scale = scale_ref[start : start + 2 * half, :1]
    for lo in range(0, features, TILE):
        tile = slice(lo, lo + TILE)
        out = jnp.dot(hidden, down_ref[:, tile], preferred_element_type=F32) * scale
        kept_ref[:, tile] = out[:half]
        sent_ref[:, tile] = out[half:].astype(BF16)


def add_kernel(kept_ref, got_ref, next_ref, sent_ref):
    half = next_ref.shape[0]
    total = kept_ref[...] + got_ref[...].astype(F32)
    next_ref[...] = total[:half]
    sent_ref[...] = total[half:].astype(BF16)


def close_kernel(kept_ref, *refs):
    total = kept_ref[...]
    for got_ref in refs[:-1]:
        total += got_ref[...].astype(F32)
    refs[-1][...] = total.astype(BF16)


def load_kernel(*refs):
    count = (len(refs) - 1) // 2
    copies = [
        pltpu.make_async_copy(src, dst, refs[-1].at[i])
        for i, (src, dst) in enumerate(zip(refs[:count], refs[count:-1]))
    ]
    for copy in copies:
        copy.start()
    for copy in copies:
        copy.wait()


def load(arrays, after):
    count = len(arrays)

    def run(*refs):
        load_kernel(*refs[:count], *refs[count + len(after) :])

    return pl.pallas_call(
        run,
        out_shape=[pltpu.VMEM(a.shape, a.dtype) for a in arrays],
        in_specs=[HBM] * count + [ANY] * len(after),
        out_specs=[VMEM] * count,
        scratch_shapes=[pltpu.SemaphoreType.DMA((count,))],
        compiler_params=pltpu.CompilerParams(vmem_limit_bytes=MIB),
        cost_estimate=FREE,
    )(*[pltpu.with_memory_space_constraint(a, pltpu.HBM) for a in arrays], *after)


def body(tokens, routes, route_weight, gate_weight, up_weight, down_weight):
    members = lax.axis_size("local")
    experts = members // SPLIT
    rows, features = tokens.shape
    hid = gate_weight.shape[2]

    width = -(-3 * experts // LANES) * LANES
    full = features + width
    sources = [tokens, routes.T, route_weight.T]
    payload = pl.pallas_call(
        functools.partial(pack_kernel, experts),
        out_shape=pltpu.VMEM((rows, full), BF16),
        in_specs=[HBM] * 3,
        out_specs=VMEM,
        scratch_shapes=[pltpu.VMEM(x.shape, x.dtype) for x in sources] + [pltpu.SemaphoreType.DMA((3,))],
        compiler_params=pltpu.CompilerParams(vmem_limit_bytes=MIB),
        cost_estimate=FREE,
    )(*[pltpu.with_memory_space_constraint(x, pltpu.HBM) for x in sources])

    outer = {e: swap(members, lambda d, e=e: (e & -e) * SPLIT) for e in range(1, experts)}
    first = swap(members, lambda d: 4 if d & 1 else 2)
    second = swap(members, lambda d: 2 if d & 1 else 4)
    sibling = swap(members, lambda d: 1)
    order = list(range(experts))

    blocks = {0: payload}
    for e in order[1:]:
        blocks[e] = outer[e](blocks[e & (e - 1)])
    pieces, last = {}, ()
    for n, e in enumerate(order):
        if n > 1:
            blocks[e], _ = lax.optimization_barrier((blocks[e], pieces[order[0]][0]))
        (pair,) = call(
            stack_kernel, [shape(2 * rows, full, BF16)], [blocks[e], first(blocks[e])], last
        )
        far = second(pair)
        pieces[e] = [pair, far, sibling(pair), sibling(far)]
        last = (pair, pieces[order[0]][1]) if n else (pair,)

    gate, up, down = load([gate_weight[0], up_weight[0], down_weight[0]], last)
    mine = (lax.axis_index("local") // SPLIT).astype(jnp.int32)[None]
    hidden_of, last = {}, ()
    for at in range(0, experts, 2):
        batch = order[at : at + 2]
        xs = [p for e in batch for p in pieces[e]]
        height = sum(x.shape[0] for x in xs)
        hidden, scale = pl.pallas_call(
            functools.partial(gate_kernel, len(xs), experts),
            out_shape=[pltpu.VMEM((height, hid), BF16), pltpu.VMEM((height, LANES), F32)],
            in_specs=[pl.BlockSpec(memory_space=pltpu.SMEM)] + [VMEM] * (len(xs) + 2) + [ANY] * len(last),
            out_specs=[VMEM, VMEM],
            compiler_params=pltpu.CompilerParams(vmem_limit_bytes=8 * MIB),
            cost_estimate=FREE,
        )(mine, *xs, gate, up, *last)
        last = (hidden,)
        for n, e in enumerate(batch):
            hidden_of[e] = (n * height // len(batch), hidden, scale)

    def descend(e, after):
        start, hidden, scale = hidden_of[e]
        half = SPLIT * rows // 2
        return call(
            functools.partial(down_kernel, start),
            [shape(half, features, F32), shape(half, features, BF16)],
            [hidden, scale, down],
            after,
        )

    def add(kept, got, after):
        half = kept.shape[0] // 2
        return call(add_kernel, [shape(half, features, F32), shape(half, features, BF16)], [kept, got], after)

    def close(kept, gots, after):
        return call(close_kernel, [shape(rows, features, BF16)], [kept, *gots], after)[0]

    back = order[::-1]
    state, last, home = {}, (), {e: [] for e in order}
    lag = (0, 1, 3, 4)
    for slot in range(len(back) + lag[-1]):
        for stage in range(4):
            n = slot - lag[stage]
            if not 0 <= n < len(back):
                continue
            e = back[n]
            if stage == 0:
                kept, sent = descend(e, last)
                state[e] = (kept, sibling(sent))
            elif stage == 1:
                kept, sent = add(*state[e], last)
                state[e] = (kept, second(sent))
            elif stage == 2:
                kept, sent = add(*state[e], last)
                state[e] = (kept, first(sent))
            else:
                sent = close(state[e][0], [state[e][1], *home[e]], last)
                if not e:
                    return sent
                home[e & (e - 1)].append(outer[e](sent))
            last = (sent,)


def solution(mesh):
    return jax.shard_map(
        body,
        mesh=mesh,
        in_specs=(
            P(("parts", "local"), None),
            P(("parts", "local"), None),
            P(("parts", "local"), None),
            P("local", None, None),
            P("local", None, None),
            P("local", None, None),
        ),
        out_specs=P(("parts", "local"), None),
        check_vma=False,
    )
```

time: 280 us -> 71.2 us (0.25)
  waiting for transfers between devices: 163 us -> 20.8 us
  blocking collectives: 90.1 us -> 0 us
  starting transfers between devices: 3.77 us -> 36.9 us
  matrix products: 15.2 us -> 0 us
  Pallas kernels: 0 us -> 12.4 us
  other arithmetic: 4.74 us -> 0 us
    all_to_all x1 -> x0, waiting for transfers between devices: 163 us -> none  [body(): lax.all_to_all(partial_value, 'local', split_axis=0, concat_axis=0, tiled...]
    all_to_all x1 -> x0, blocking collectives: 90.1 us -> none  [body(): lax.all_to_all(outgoing, 'local', split_axis=0, concat_axis=0, tiled=True)]
    ppermute x0 -> x34, starting transfers between devices: none -> 36.9 us  [swap(): return lambda x: lax.ppermute(x, 'local', pairs)]
    ppermute x0 -> x34, waiting for transfers between devices: none -> 20.8 us  [swap(): return lambda x: lax.ppermute(x, 'local', pairs)]
    dot_general x5 -> x0, matrix products: 15.2 us -> none  [the longest x1 11.2 us: body(): result = jnp.dot(hidden, down_weight[0], preferred_element_type=jnp.float32)]
    pallas_call x0 -> x24, Pallas kernels: none -> 12.4 us  [the longest x1 4.23 us: load(): pl.pallas_call(run, out_shape=[pltpu.VMEM(a.shape, a.dtype) for a in arra...]
    reduce_sum x3 -> x0, other arithmetic: 3.84 us -> none  [the longest x1 3.58 us: body(): jnp.sum(returned.reshape(experts, sharers, capacity, features), axis=1)]
    all_to_all x1 -> x0, starting transfers between devices: 3.77 us -> none  [body(): lax.all_to_all(partial_value, 'local', split_axis=0, concat_axis=0, tiled...]
  transfers between devices with their start and end apart: 1 -> 34, of which waited for: 1 -> 13; matrix products, arithmetic and copies ran while one was open for 0% -> 0% of each run, Pallas kernels for 0% -> 12%
where the time goes in v2:
time: 71.2 us; the launch traced here: 71 us
  starting transfers between devices  36.9 us (52%)
  waiting for transfers between devices  20.8 us (29%)
  Pallas kernels  12.4 us (17%)
    ppermute x34, starting transfers between devices, swap(): return lambda x: lax.ppermute(x, 'local', pairs)  36.9 us
    ppermute x34, waiting for transfers between devices, swap(): return lambda x: lax.ppermute(x, 'local', pairs)  20.8 us
    pallas_call x1, Pallas kernels, load(): pl.pallas_call(run, out_shape=[pltpu.VMEM(a.shape, a.dtype) for a in arra...  4.23 us
    pallas_call x20, Pallas kernels, call(): pl.pallas_call(run, out_shape=[pltpu.VMEM(o.shape, o.dtype) for o in outs...  3.81 us
    pallas_call x2, Pallas kernels, body(): pl.pallas_call(functools.partial(gate_kernel, len(xs), experts), out_shap...  3.29 us
  transfers between devices with their start and end apart: 34, of which 13 were waited for; matrix products, arithmetic and copies ran while one was open for 0% of the time, Pallas kernels for 12%

profile of v2, /device:TPU:0, one launch (start us, length us, event | category | flops | bytes accessed | tf_op | source)
XLA Modules:
  0.0 71.0 jit_solution(5476477648735510491)
XLA Ops:
  1.1 3.0 %collective-permute-start = (bf16[8,7296]{1,0:T(8,128)(2,1)S(1)}, bf16[8,7296]{1,0:T(8,128)(2,1)S(1)}, u32[]{:S(2)}, u32[]{:S(2)}) collective-permute-start(bf16[8,7296]{1,0:T(8,128)(2,1)S(1)} %shard_map.64.refs_0_), channel_id=1, source_target_pairs={{0,2},{1,5},{2,0},{3,7},{4,6},{5,1},{6,4},{7,3},{8,10},{9,13},{10,... | collective-permute-start | bytes 350216 | tf_op jit(solution)/shard_map/ppermute | solution.py:24
  4.1 2.6 %collective-permute-start.9 = (bf16[8,7296]{1,0:T(8,128)(2,1)S(1)}, bf16[8,7296]{1,0:T(8,128)(2,1)S(1)}, u32[]{:S(2)}, u32[]{:S(2)}) collective-permute-start(bf16[8,7296]{1,0:T(8,128)(2,1)S(1)} %shard_map.64.refs_0_), channel_id=1, source_target_pairs={{0,16},{1,17},{2,18},{3,19},{4,20},{5,21},{6,22},{7,23},{8,24},{9,... | collective-permute-start | bytes 350216 | tf_op jit(solution)/shard_map/ppermute | solution.py:24
  6.7 1.6 %collective-permute-start.4 = (bf16[8,7296]{1,0:T(8,128)(2,1)S(1)}, bf16[8,7296]{1,0:T(8,128)(2,1)S(1)}, u32[]{:S(2)}, u32[]{:S(2)}) collective-permute-start(bf16[8,7296]{1,0:T(8,128)(2,1)S(1)} %shard_map.64.refs_0_), channel_id=1, source_target_pairs={{0,8},{1,9},{2,10},{3,11},{4,12},{5,13},{6,14},{7,15},{8,0},{9,1},... | collective-permute-start | bytes 350216 | tf_op jit(solution)/shard_map/ppermute | solution.py:24
  8.3 3.9 %collective-permute-done.9.refs_0_ = bf16[8,7296]{1,0:T(8,128)(2,1)S(1)} collective-permute-done((bf16[8,7296]{1,0:T(8,128)(2,1)S(1)}, bf16[8,7296]{1,0:T(8,128)(2,1)S(1)}, u32[]{:S(2)}, u32[]{:S(2)}) %collective-permute-start.9) | collective-permute-done | bytes 116768 | tf_op jit(solution)/shard_map/ppermute | solution.py:24
  17.0 1.8 %collective-permute-start.11 = (bf16[8,7296]{1,0:T(8,128)(2,1)S(1)}, bf16[8,7296]{1,0:T(8,128)(2,1)S(1)}, u32[]{:S(2)}, u32[]{:S(2)}) collective-permute-start(bf16[8,7296]{1,0:T(8,128)(2,1)S(1)} %collective-permute-done.10.refs_0_), channel_id=1, source_target_pairs={{0,2},{1,5},{2,0},{3,7},{4,6},{5,1},{6,4},{7,3},{8,10},{9,13},{10,... | collective-permute-start | bytes 350216 | tf_op jit(solution)/shard_map/ppermute | solution.py:24
  20.1 1.4 %collective-permute-start.7 = (bf16[16,7296]{1,0:T(8,128)(2,1)S(1)}, bf16[16,7296]{1,0:T(8,128)(2,1)S(1)}, u32[]{:S(2)}, u32[]{:S(2)}) collective-permute-start(bf16[16,7296]{1,0:T(8,128)(2,1)S(1)} %shard_map.66.refs_2_.refs_4_), channel_id=1, source_target_pairs={{0,1},{1,0},{2,3},{3,2},{4,5},{5,4},{6,7},{7,6},{8,9},{9,8},{10,11... | collective-permute-start | bytes 700424 | tf_op jit(solution)/shard_map/ppermute | solution.py:24
  22.6 1.4 %collective-permute-start.13 = (bf16[16,7296]{1,0:T(8,128)(2,1)S(1)}, bf16[16,7296]{1,0:T(8,128)(2,1)S(1)}, u32[]{:S(2)}, u32[]{:S(2)}) collective-permute-start(bf16[16,7296]{1,0:T(8,128)(2,1)S(1)} %shard_map.67.refs_2_.refs_0_), channel_id=1, source_target_pairs={{0,4},{1,3},{2,6},{3,1},{4,0},{5,7},{6,2},{7,5},{8,12},{9,11},{10,... | collective-permute-start | bytes 700424 | tf_op jit(solution)/shard_map/ppermute | solution.py:24
  23.9 1.2 %collective-permute-done.6.refs_5_ = bf16[16,7296]{1,0:T(8,128)(2,1)S(1)} collective-permute-done((bf16[16,7296]{1,0:T(8,128)(2,1)S(1)}, bf16[16,7296]{1,0:T(8,128)(2,1)S(1)}, u32[]{:S(2)}, u32[]{:S(2)}) %collective-permute-start.6) | collective-permute-done | bytes 233504 | tf_op jit(solution)/shard_map/ppermute | solution.py:24
  25.7 2.2 %collective-permute-done.16.refs_5_ = bf16[16,7296]{1,0:T(8,128)(2,1)S(1)} collective-permute-done((bf16[16,7296]{1,0:T(8,128)(2,1)S(1)}, bf16[16,7296]{1,0:T(8,128)(2,1)S(1)}, u32[]{:S(2)}, u32[]{:S(2)}) %collective-permute-start.16) | collective-permute-done | bytes 233504 | tf_op jit(solution)/shard_map/ppermute | solution.py:24
  28.2 2.3 %collective-permute-done.13.refs_1_ = bf16[16,7296]{1,0:T(8,128)(2,1)S(1)} collective-permute-done((bf16[16,7296]{1,0:T(8,128)(2,1)S(1)}, bf16[16,7296]{1,0:T(8,128)(2,1)S(1)}, u32[]{:S(2)}, u32[]{:S(2)}) %collective-permute-start.13) | collective-permute-done | bytes 233504 | tf_op jit(solution)/shard_map/ppermute | solution.py:24
  30.6 4.2 %shard_map.69 = (bf16[7168,256]{1,0:T(8,128)(2,1)S(1)}, bf16[7168,256]{1,0:T(8,128)(2,1)S(1)}, bf16[256,7168]{1,0:T(8,128)(2,1)S(1)}) custom-call(bf16[7168,256]{1,0:T(8,128)(2,1)} %bitcast.6, bf16[7168,256]{1,0:T(8,128)(2,1)} %bitcast.7, bf16[256,7168]{1,0:T(8,128)(2,1)} %bitcast.8, bf16[16,7296]{1,0:T(8,128)(2,1)S(1)} %shard_map.68.refs_3_.refs_4_, ...), custom_call_target="tpu_custom_call" | custom-call | tf_op jit(solution)/shard_map/pallas_call | solution.py:139
  34.8 1.2 %shard_map.70 = (bf16[128,256]{1,0:T(8,128)(2,1)S(1)}, f32[128,128]{1,0:T(8,128)S(1)}) custom-call(s32[1]{0:T(128)} %bitcast.mine_ref, bf16[16,7296]{1,0:T(8,128)(2,1)S(1)} %shard_map.65.refs_2_.refs_0_, bf16[16,7296]{1,0:T(8,128)(2,1)S(1)} %collective-permute-done.1.refs_3_.refs_4_.refs_1_, bf16[16,7296]{1,0:T(8,128)(2,1)S(1)} %collective-permute-done.2.refs_2_, ...), custom_call_target="tpu_custom_call" | custom-call | tf_op jit(solution)/shard_map/pallas_call | solution.py:196
  36.1 2.1 %shard_map.71 = (bf16[128,256]{1,0:T(8,128)(2,1)S(1)}, f32[128,128]{1,0:T(8,128)S(1)}) custom-call(s32[1]{0:T(128)} %bitcast.mine_ref, bf16[16,7296]{1,0:T(8,128)(2,1)S(1)} %shard_map.67.refs_2_.refs_0_, bf16[16,7296]{1,0:T(8,128)(2,1)S(1)} %collective-permute-done.13.refs_1_, bf16[16,7296]{1,0:T(8,128)(2,1)S(1)} %collective-permute-done.14.refs_2_, ...), custom_call_target="tpu_custom_call" | custom-call | tf_op jit(solution)/shard_map/pallas_call | solution.py:196
  43.8 1.4 %collective-permute-start.25 = (bf16[16,7168]{1,0:T(8,128)(2,1)S(1)}, bf16[16,7168]{1,0:T(8,128)(2,1)S(1)}, u32[]{:S(2)}, u32[]{:S(2)}) collective-permute-start(bf16[16,7168]{1,0:T(8,128)(2,1)S(1)} %get-tuple-element.53.refs_3_), channel_id=1, source_target_pairs={{0,4},{1,3},{2,6},{3,1},{4,0},{5,7},{6,2},{7,5},{8,12},{9,11},{10,... | collective-permute-start | bytes 688136 | tf_op jit(solution)/shard_map/ppermute | solution.py:24
  46.0 3.2 %collective-permute-done.22.refs_1_ = bf16[16,7168]{1,0:T(8,128)(2,1)S(1)} collective-permute-done((bf16[16,7168]{1,0:T(8,128)(2,1)S(1)}, bf16[16,7168]{1,0:T(8,128)(2,1)S(1)}, u32[]{:S(2)}, u32[]{:S(2)}) %collective-permute-start.22) | collective-permute-done | bytes 229408 | tf_op jit(solution)/shard_map/ppermute | solution.py:24
  49.3 2.3 %collective-permute-start.27 = (bf16[8,7168]{1,0:T(8,128)(2,1)S(1)}, bf16[8,7168]{1,0:T(8,128)(2,1)S(1)}, u32[]{:S(2)}, u32[]{:S(2)}) collective-permute-start(bf16[8,7168]{1,0:T(8,128)(2,1)S(1)} %get-tuple-element.59.refs_2_), channel_id=1, source_target_pairs={{0,2},{1,5},{2,0},{3,7},{4,6},{5,1},{6,4},{7,3},{8,10},{9,13},{10,... | collective-permute-start | bytes 344072 | tf_op jit(solution)/shard_map/ppermute | solution.py:24
  51.8 2.4 %collective-permute-start.26 = (bf16[8,7168]{1,0:T(8,128)(2,1)S(1)}, bf16[8,7168]{1,0:T(8,128)(2,1)S(1)}, u32[]{:S(2)}, u32[]{:S(2)}) collective-permute-start(bf16[8,7168]{1,0:T(8,128)(2,1)S(1)} %get-tuple-element.64.refs_2_), channel_id=1, source_target_pairs={{0,2},{1,5},{2,0},{3,7},{4,6},{5,1},{6,4},{7,3},{8,10},{9,13},{10,... | collective-permute-start | bytes 344072 | tf_op jit(solution)/shard_map/ppermute | solution.py:24
  54.2 1.4 %collective-permute-done.27.refs_1_ = bf16[8,7168]{1,0:T(8,128)(2,1)S(1)} collective-permute-done((bf16[8,7168]{1,0:T(8,128)(2,1)S(1)}, bf16[8,7168]{1,0:T(8,128)(2,1)S(1)}, u32[]{:S(2)}, u32[]{:S(2)}) %collective-permute-start.27) | collective-permute-done | bytes 114720 | tf_op jit(solution)/shard_map/ppermute | solution.py:24
  56.8 2.1 %collective-permute-start.32 = (bf16[8,7168]{1,0:T(8,128)(2,1)S(1)}, bf16[8,7168]{1,0:T(8,128)(2,1)S(1)}, u32[]{:S(2)}, u32[]{:S(2)}) collective-permute-start(bf16[8,7168]{1,0:T(8,128)(2,1)S(1)} %get-tuple-element.67.refs_3_), channel_id=1, source_target_pairs={{0,2},{1,5},{2,0},{3,7},{4,6},{5,1},{6,4},{7,3},{8,10},{9,13},{10,... | collective-permute-start | bytes 344072 | tf_op jit(solution)/shard_map/ppermute | solution.py:24
  58.9 1.6 %collective-permute-done.28.refs_2_ = bf16[8,7168]{1,0:T(8,128)(2,1)S(1)} collective-permute-done((bf16[8,7168]{1,0:T(8,128)(2,1)S(1)}, bf16[8,7168]{1,0:T(8,128)(2,1)S(1)}, u32[]{:S(2)}, u32[]{:S(2)}) %collective-permute-start.28) | collective-permute-done | bytes 114720 | tf_op jit(solution)/shard_map/ppermute | solution.py:24
  60.5 3.0 %collective-permute-start.31 = (bf16[8,7168]{1,0:T(8,128)(2,1)S(1)}, bf16[8,7168]{1,0:T(8,128)(2,1)S(1)}, u32[]{:S(2)}, u32[]{:S(2)}) collective-permute-start(bf16[8,7168]{1,0:T(8,128)(2,1)S(1)} %shard_map.84.refs_2_), channel_id=1, source_target_pairs={{0,16},{1,17},{2,18},{3,19},{4,20},{5,21},{6,22},{7,23},{8,24},{9,... | collective-permute-start | bytes 344072 | tf_op jit(solution)/shard_map/ppermute | solution.py:24
  63.6 1.8 %collective-permute-start.30 = (bf16[8,7168]{1,0:T(8,128)(2,1)S(1)}, bf16[8,7168]{1,0:T(8,128)(2,1)S(1)}, u32[]{:S(2)}, u32[]{:S(2)}) collective-permute-start(bf16[8,7168]{1,0:T(8,128)(2,1)S(1)} %get-tuple-element.69.refs_2_), channel_id=1, source_target_pairs={{0,2},{1,5},{2,0},{3,7},{4,6},{5,1},{6,4},{7,3},{8,10},{9,13},{10,... | collective-permute-start | bytes 344072 | tf_op jit(solution)/shard_map/ppermute | solution.py:24
  65.5 2.1 %collective-permute-start.33 = (bf16[8,7168]{1,0:T(8,128)(2,1)S(1)}, bf16[8,7168]{1,0:T(8,128)(2,1)S(1)}, u32[]{:S(2)}, u32[]{:S(2)}) collective-permute-start(bf16[8,7168]{1,0:T(8,128)(2,1)S(1)} %shard_map.86.refs_4_), channel_id=1, source_target_pairs={{0,8},{1,9},{2,10},{3,11},{4,12},{5,13},{6,14},{7,15},{8,0},{9,1},... | collective-permute-start | bytes 344072 | tf_op jit(solution)/shard_map/ppermute | solution.py:24
  68.5 1.9 %collective-permute-done.33.refs_3_ = bf16[8,7168]{1,0:T(8,128)(2,1)S(1)} collective-permute-done((bf16[8,7168]{1,0:T(8,128)(2,1)S(1)}, bf16[8,7168]{1,0:T(8,128)(2,1)S(1)}, u32[]{:S(2)}, u32[]{:S(2)}) %collective-permute-start.33) | collective-permute-done | bytes 114720 | tf_op jit(solution)/shard_map/ppermute | solution.py:24
  (69 shorter events, 18.7 us)
Async XLA Ops:
  1.1 7.2 %collective-permute-start = (bf16[8,7296]{1,0:T(8,128)(2,1)S(1)}, bf16[8,7296]{1,0:T(8,128)(2,1)S(1)}, u32[]{:S(2)}, u32[]{:S(2)}) collective-permute-start(bf16[8,7296]{1,0:T(8,128)(2,1)S(1)} %shard_map.64.refs_0_), channel_id=1, source_target_pairs={{0,2},{1,5},{2,0},{3,7},{4,6},{5,1},{6,4},{7,3},{8,10},{9,13},{10,... | collective-permute-start | bytes 350216 | tf_op jit(solution)/shard_map/ppermute | solution.py:24
  4.1 8.1 %collective-permute-start.9 = (bf16[8,7296]{1,0:T(8,128)(2,1)S(1)}, bf16[8,7296]{1,0:T(8,128)(2,1)S(1)}, u32[]{:S(2)}, u32[]{:S(2)}) collective-permute-start(bf16[8,7296]{1,0:T(8,128)(2,1)S(1)} %shard_map.64.refs_0_), channel_id=1, source_target_pairs={{0,16},{1,17},{2,18},{3,19},{4,20},{5,21},{6,22},{7,23},{8,24},{9,... | collective-permute-start | bytes 350216 | tf_op jit(solution)/shard_map/ppermute | solution.py:24
  6.7 7.2 %collective-permute-start.4 = (bf16[8,7296]{1,0:T(8,128)(2,1)S(1)}, bf16[8,7296]{1,0:T(8,128)(2,1)S(1)}, u32[]{:S(2)}, u32[]{:S(2)}) collective-permute-start(bf16[8,7296]{1,0:T(8,128)(2,1)S(1)} %shard_map.64.refs_0_), channel_id=1, source_target_pairs={{0,8},{1,9},{2,10},{3,11},{4,12},{5,13},{6,14},{7,15},{8,0},{9,1},... | collective-permute-start | bytes 350216 | tf_op jit(solution)/shard_map/ppermute | solution.py:24
  12.8 8.7 %collective-permute-start.1 = (bf16[16,7296]{1,0:T(8,128)(2,1)S(1)}, bf16[16,7296]{1,0:T(8,128)(2,1)S(1)}, u32[]{:S(2)}, u32[]{:S(2)}) collective-permute-start(bf16[16,7296]{1,0:T(8,128)(2,1)S(1)} %shard_map.65.refs_2_.refs_0_), channel_id=1, source_target_pairs={{0,4},{1,3},{2,6},{3,1},{4,0},{5,7},{6,2},{7,5},{8,12},{9,11},{10,... | collective-permute-start | bytes 700424 | tf_op jit(solution)/shard_map/ppermute | solution.py:24
  13.3 9.2 %collective-permute-start.2 = (bf16[16,7296]{1,0:T(8,128)(2,1)S(1)}, bf16[16,7296]{1,0:T(8,128)(2,1)S(1)}, u32[]{:S(2)}, u32[]{:S(2)}) collective-permute-start(bf16[16,7296]{1,0:T(8,128)(2,1)S(1)} %shard_map.65.refs_2_.refs_0_), channel_id=1, source_target_pairs={{0,1},{1,0},{2,3},{3,2},{4,5},{5,4},{6,7},{7,6},{8,9},{9,8},{10,11... | collective-permute-start | bytes 700424 | tf_op jit(solution)/shard_map/ppermute | solution.py:24
  14.8 5.2 %collective-permute-start.12 = (bf16[8,7296]{1,0:T(8,128)(2,1)S(1)}, bf16[8,7296]{1,0:T(8,128)(2,1)S(1)}, u32[]{:S(2)}, u32[]{:S(2)}) collective-permute-start(bf16[8,7296]{1,0:T(8,128)(2,1)S(1)} %collective-permute-done.9.refs_0_), channel_id=1, source_target_pairs={{0,2},{1,5},{2,0},{3,7},{4,6},{5,1},{6,4},{7,3},{8,10},{9,13},{10,... | collective-permute-start | bytes 350216 | tf_op jit(solution)/shard_map/ppermute | solution.py:24
  18.8 6.3 %collective-permute-start.6 = (bf16[16,7296]{1,0:T(8,128)(2,1)S(1)}, bf16[16,7296]{1,0:T(8,128)(2,1)S(1)}, u32[]{:S(2)}, u32[]{:S(2)}) collective-permute-start(bf16[16,7296]{1,0:T(8,128)(2,1)S(1)} %shard_map.66.refs_2_.refs_4_), channel_id=1, source_target_pairs={{0,4},{1,3},{2,6},{3,1},{4,0},{5,7},{6,2},{7,5},{8,12},{9,11},{10,... | collective-permute-start | bytes 700424 | tf_op jit(solution)/shard_map/ppermute | solution.py:24
  20.1 5.1 %collective-permute-start.7 = (bf16[16,7296]{1,0:T(8,128)(2,1)S(1)}, bf16[16,7296]{1,0:T(8,128)(2,1)S(1)}, u32[]{:S(2)}, u32[]{:S(2)}) collective-permute-start(bf16[16,7296]{1,0:T(8,128)(2,1)S(1)} %shard_map.66.refs_2_.refs_4_), channel_id=1, source_target_pairs={{0,1},{1,0},{2,3},{3,2},{4,5},{5,4},{6,7},{7,6},{8,9},{9,8},{10,11... | collective-permute-start | bytes 700424 | tf_op jit(solution)/shard_map/ppermute | solution.py:24
  21.8 6.1 %collective-permute-start.16 = (bf16[16,7296]{1,0:T(8,128)(2,1)S(1)}, bf16[16,7296]{1,0:T(8,128)(2,1)S(1)}, u32[]{:S(2)}, u32[]{:S(2)}) collective-permute-start(bf16[16,7296]{1,0:T(8,128)(2,1)S(1)} %shard_map.68.refs_3_.refs_4_), channel_id=1, source_target_pairs={{0,4},{1,3},{2,6},{3,1},{4,0},{5,7},{6,2},{7,5},{8,12},{9,11},{10,... | collective-permute-start | bytes 700424 | tf_op jit(solution)/shard_map/ppermute | solution.py:24
  22.6 7.9 %collective-permute-start.13 = (bf16[16,7296]{1,0:T(8,128)(2,1)S(1)}, bf16[16,7296]{1,0:T(8,128)(2,1)S(1)}, u32[]{:S(2)}, u32[]{:S(2)}) collective-permute-start(bf16[16,7296]{1,0:T(8,128)(2,1)S(1)} %shard_map.67.refs_2_.refs_0_), channel_id=1, source_target_pairs={{0,4},{1,3},{2,6},{3,1},{4,0},{5,7},{6,2},{7,5},{8,12},{9,11},{10,... | collective-permute-start | bytes 700424 | tf_op jit(solution)/shard_map/ppermute | solution.py:24
  25.1 9.7 %collective-permute-start.8 = (bf16[16,7296]{1,0:T(8,128)(2,1)S(1)}, bf16[16,7296]{1,0:T(8,128)(2,1)S(1)}, u32[]{:S(2)}, u32[]{:S(2)}) collective-permute-start(bf16[16,7296]{1,0:T(8,128)(2,1)S(1)} %collective-permute-done.6.refs_5_), channel_id=1, source_target_pairs={{0,1},{1,0},{2,3},{3,2},{4,5},{5,4},{6,7},{7,6},{8,9},{9,8},{10,11... | collective-permute-start | bytes 700424 | tf_op jit(solution)/shard_map/ppermute | solution.py:24
  25.1 10.9 %collective-permute-start.17 = (bf16[16,7296]{1,0:T(8,128)(2,1)S(1)}, bf16[16,7296]{1,0:T(8,128)(2,1)S(1)}, u32[]{:S(2)}, u32[]{:S(2)}) collective-permute-start(bf16[16,7296]{1,0:T(8,128)(2,1)S(1)} %shard_map.68.refs_3_.refs_4_), channel_id=1, source_target_pairs={{0,1},{1,0},{2,3},{3,2},{4,5},{5,4},{6,7},{7,6},{8,9},{9,8},{10,11... | collective-permute-start | bytes 700424 | tf_op jit(solution)/shard_map/ppermute | solution.py:24
  25.7 10.4 %collective-permute-start.14 = (bf16[16,7296]{1,0:T(8,128)(2,1)S(1)}, bf16[16,7296]{1,0:T(8,128)(2,1)S(1)}, u32[]{:S(2)}, u32[]{:S(2)}) collective-permute-start(bf16[16,7296]{1,0:T(8,128)(2,1)S(1)} %shard_map.67.refs_2_.refs_0_), channel_id=1, source_target_pairs={{0,1},{1,0},{2,3},{3,2},{4,5},{5,4},{6,7},{7,6},{8,9},{9,8},{10,11... | collective-permute-start | bytes 700424 | tf_op jit(solution)/shard_map/ppermute | solution.py:24
  28.0 8.1 %collective-permute-start.18 = (bf16[16,7296]{1,0:T(8,128)(2,1)S(1)}, bf16[16,7296]{1,0:T(8,128)(2,1)S(1)}, u32[]{:S(2)}, u32[]{:S(2)}) collective-permute-start(bf16[16,7296]{1,0:T(8,128)(2,1)S(1)} %collective-permute-done.16.refs_5_), channel_id=1, source_target_pairs={{0,1},{1,0},{2,3},{3,2},{4,5},{5,4},{6,7},{7,6},{8,9},{9,8},{10,11... | collective-permute-start | bytes 700424 | tf_op jit(solution)/shard_map/ppermute | solution.py:24
  30.5 5.6 %collective-permute-start.15 = (bf16[16,7296]{1,0:T(8,128)(2,1)S(1)}, bf16[16,7296]{1,0:T(8,128)(2,1)}, u32[]{:S(2)}, u32[]{:S(2)}) collective-permute-start(bf16[16,7296]{1,0:T(8,128)(2,1)S(1)} %collective-permute-done.13.refs_1_), channel_id=1, source_target_pairs={{0,1},{1,0},{2,3},{3,2},{4,5},{5,4},{6,7},{7,6},{8,9},{9,8},{10,11... | collective-permute-start | bytes 700424 | tf_op jit(solution)/shard_map/ppermute | solution.py:24
  43.0 8.5 %collective-permute-start.21 = (bf16[32,7168]{1,0:T(8,128)(2,1)S(1)}, bf16[32,7168]{1,0:T(8,128)(2,1)S(1)}, u32[]{:S(2)}, u32[]{:S(2)}) collective-permute-start(bf16[32,7168]{1,0:T(8,128)(2,1)S(1)} %get-tuple-element.55.refs_2_), channel_id=1, source_target_pairs={{0,1},{1,0},{2,3},{3,2},{4,5},{5,4},{6,7},{7,6},{8,9},{9,8},{10,11... | collective-permute-start | bytes 1376264 | tf_op jit(solution)/shard_map/ppermute | solution.py:24
  43.2 6.0 %collective-permute-start.22 = (bf16[16,7168]{1,0:T(8,128)(2,1)S(1)}, bf16[16,7168]{1,0:T(8,128)(2,1)S(1)}, u32[]{:S(2)}, u32[]{:S(2)}) collective-permute-start(bf16[16,7168]{1,0:T(8,128)(2,1)S(1)} %get-tuple-element.51.refs_3_), channel_id=1, source_target_pairs={{0,4},{1,3},{2,6},{3,1},{4,0},{5,7},{6,2},{7,5},{8,12},{9,11},{10,... | collective-permute-start | bytes 688136 | tf_op jit(solution)/shard_map/ppermute | solution.py:24
  43.8 7.9 %collective-permute-start.25 = (bf16[16,7168]{1,0:T(8,128)(2,1)S(1)}, bf16[16,7168]{1,0:T(8,128)(2,1)S(1)}, u32[]{:S(2)}, u32[]{:S(2)}) collective-permute-start(bf16[16,7168]{1,0:T(8,128)(2,1)S(1)} %get-tuple-element.53.refs_3_), channel_id=1, source_target_pairs={{0,4},{1,3},{2,6},{3,1},{4,0},{5,7},{6,2},{7,5},{8,12},{9,11},{10,... | collective-permute-start | bytes 688136 | tf_op jit(solution)/shard_map/ppermute | solution.py:24
  45.3 11.4 %collective-permute-start.29 = (bf16[16,7168]{1,0:T(8,128)(2,1)S(1)}, bf16[16,7168]{1,0:T(8,128)(2,1)S(1)}, u32[]{:S(2)}, u32[]{:S(2)}) collective-permute-start(bf16[16,7168]{1,0:T(8,128)(2,1)S(1)} %get-tuple-element.58.refs_2_), channel_id=1, source_target_pairs={{0,4},{1,3},{2,6},{3,1},{4,0},{5,7},{6,2},{7,5},{8,12},{9,11},{10,... | collective-permute-start | bytes 688136 | tf_op jit(solution)/shard_map/ppermute | solution.py:24
  49.3 6.3 %collective-permute-start.27 = (bf16[8,7168]{1,0:T(8,128)(2,1)S(1)}, bf16[8,7168]{1,0:T(8,128)(2,1)S(1)}, u32[]{:S(2)}, u32[]{:S(2)}) collective-permute-start(bf16[8,7168]{1,0:T(8,128)(2,1)S(1)} %get-tuple-element.59.refs_2_), channel_id=1, source_target_pairs={{0,2},{1,5},{2,0},{3,7},{4,6},{5,1},{6,4},{7,3},{8,10},{9,13},{10,... | collective-permute-start | bytes 344072 | tf_op jit(solution)/shard_map/ppermute | solution.py:24
  51.6 11.9 %collective-permute-start.24 = (bf16[16,7168]{1,0:T(8,128)(2,1)S(1)}, bf16[16,7168]{1,0:T(8,128)(2,1)S(1)}, u32[]{:S(2)}, u32[]{:S(2)}) collective-permute-start(bf16[16,7168]{1,0:T(8,128)(2,1)S(1)} %get-tuple-element.61.refs_2_), channel_id=1, source_target_pairs={{0,4},{1,3},{2,6},{3,1},{4,0},{5,7},{6,2},{7,5},{8,12},{9,11},{10,... | collective-permute-start | bytes 688136 | tf_op jit(solution)/shard_map/ppermute | solution.py:24
  51.8 7.2 %collective-permute-start.26 = (bf16[8,7168]{1,0:T(8,128)(2,1)S(1)}, bf16[8,7168]{1,0:T(8,128)(2,1)S(1)}, u32[]{:S(2)}, u32[]{:S(2)}) collective-permute-start(bf16[8,7168]{1,0:T(8,128)(2,1)S(1)} %get-tuple-element.64.refs_2_), channel_id=1, source_target_pairs={{0,2},{1,5},{2,0},{3,7},{4,6},{5,1},{6,4},{7,3},{8,10},{9,13},{10,... | collective-permute-start | bytes 344072 | tf_op jit(solution)/shard_map/ppermute | solution.py:24
  56.8 8.6 %collective-permute-start.32 = (bf16[8,7168]{1,0:T(8,128)(2,1)S(1)}, bf16[8,7168]{1,0:T(8,128)(2,1)S(1)}, u32[]{:S(2)}, u32[]{:S(2)}) collective-permute-start(bf16[8,7168]{1,0:T(8,128)(2,1)S(1)} %get-tuple-element.67.refs_3_), channel_id=1, source_target_pairs={{0,2},{1,5},{2,0},{3,7},{4,6},{5,1},{6,4},{7,3},{8,10},{9,13},{10,... | collective-permute-start | bytes 344072 | tf_op jit(solution)/shard_map/ppermute | solution.py:24
  60.5 7.9 %collective-permute-start.31 = (bf16[8,7168]{1,0:T(8,128)(2,1)S(1)}, bf16[8,7168]{1,0:T(8,128)(2,1)S(1)}, u32[]{:S(2)}, u32[]{:S(2)}) collective-permute-start(bf16[8,7168]{1,0:T(8,128)(2,1)S(1)} %shard_map.84.refs_2_), channel_id=1, source_target_pairs={{0,16},{1,17},{2,18},{3,19},{4,20},{5,21},{6,22},{7,23},{8,24},{9,... | collective-permute-start | bytes 344072 | tf_op jit(solution)/shard_map/ppermute | solution.py:24
  (10 other events, 40.8 us)

commit v3 on v2

--- a/solution.py
+++ b/solution.py
@@ -16,7 +16,10 @@
 VMEM = pl.BlockSpec(memory_space=pltpu.VMEM)
 ANY = pl.BlockSpec(memory_space=pl.ANY)
 HBM = pl.BlockSpec(memory_space=pltpu.HBM)
-FREE = pl.CostEstimate(flops=0, bytes_accessed=0, transcendentals=0)
+
+
+def cost(us):
+    return pl.CostEstimate(flops=0, bytes_accessed=int(us * 3.6e6), transcendentals=0)
 
 
 def swap(members, mask):
@@ -24,7 +27,7 @@
     return lambda x: lax.ppermute(x, "local", pairs)
 
 
-def call(kernel, outs, operands, after=(), limit=8, scratch=()):
+def call(kernel, outs, operands, after=(), limit=8):
     count = len(operands)
 
     def run(*refs):
@@ -35,9 +38,8 @@
         out_shape=[pltpu.VMEM(o.shape, o.dtype) for o in outs],
         in_specs=[VMEM] * count + [ANY] * len(after),
         out_specs=[VMEM] * len(outs),
-        scratch_shapes=scratch,
         compiler_params=pltpu.CompilerParams(vmem_limit_bytes=limit * MIB),
-        cost_estimate=FREE,
+        cost_estimate=cost(0),
     )(*operands, *after)
 
 
@@ -73,8 +75,8 @@
     out_ref[:, features:] = jnp.where(column < 3 * experts, terms, 0.0).astype(BF16)
 
 
-def stack_kernel(a_ref, b_ref, out_ref):
-    out_ref[...] = jnp.concatenate([a_ref[...], b_ref[...]], axis=0)
+def stack_kernel(*refs):
+    refs[-1][...] = jnp.concatenate([r[...] for r in refs[:-1]], axis=0)
 
 
 def gate_kernel(pieces, experts, mine_ref, *refs):
@@ -118,33 +120,48 @@
     refs[-1][...] = total.astype(BF16)
 
 
-def load_kernel(*refs):
-    count = (len(refs) - 1) // 2
-    copies = [
-        pltpu.make_async_copy(src, dst, refs[-1].at[i])
-        for i, (src, dst) in enumerate(zip(refs[:count], refs[count:-1]))
-    ]
-    for copy in copies:
-        copy.start()
-    for copy in copies:
-        copy.wait()
-
-
 def load(arrays, after):
-    count = len(arrays)
+    count, parts = len(arrays), 2
 
     def run(*refs):
-        load_kernel(*refs[:count], *refs[count + len(after) :])
+        outs, sems = refs[count + len(after) : -1], refs[-1]
+        copies = []
+        for i in range(count):
+            height = arrays[i].shape[0] // parts
+            for n in range(parts):
+                rows = pl.ds(n * height, height)
+                copies.append(pltpu.make_async_copy(refs[i].at[rows], outs[i].at[rows], sems.at[i, n]))
+        for copy in copies:
+            copy.start()
+        for copy in copies:
+            copy.wait()
 
     return pl.pallas_call(
         run,
         out_shape=[pltpu.VMEM(a.shape, a.dtype) for a in arrays],
         in_specs=[HBM] * count + [ANY] * len(after),
         out_specs=[VMEM] * count,
-        scratch_shapes=[pltpu.SemaphoreType.DMA((count,))],
+        scratch_shapes=[pltpu.SemaphoreType.DMA((count, parts))],
         compiler_params=pltpu.CompilerParams(vmem_limit_bytes=MIB),
-        cost_estimate=FREE,
+        cost_estimate=cost(4),
     )(*[pltpu.with_memory_space_constraint(a, pltpu.HBM) for a in arrays], *after)
+
+
+def plan(experts):
+    near, far = range(experts // 2), range(experts // 2, experts)
+    steps = [("fetch", e) for e in sorted(range(1, experts), key=lambda e: (bin(e).count("1"), -e))]
+    steps += [("behind", far[0]), ("stack", 0), ("behind", far[-1])] + [("stack", e) for e in range(1, experts)]
+    steps += [("load",)]
+    for e in near[::2]:
+        steps += [("gate", (e, e + 1)), ("down", e + 1), ("down", e)]
+    steps += [("hold", e, near[-2]) for e in far]
+    steps += [("gate", (e, e + 1)) for e in far[::2]] + [("down", e) for e in far[::-1]]
+    back = range(experts)[::-1]
+    for slot in range(experts + 3):
+        for step, lag in (("add1", 0), ("add2", 2), ("close", 3)):
+            if 0 <= slot - lag < experts:
+                steps.append((step, back[slot - lag]))
+    return steps
 
 
 def body(tokens, routes, route_weight, gate_weight, up_weight, down_weight):
@@ -163,89 +180,72 @@
         out_specs=VMEM,
         scratch_shapes=[pltpu.VMEM(x.shape, x.dtype) for x in sources] + [pltpu.SemaphoreType.DMA((3,))],
         compiler_params=pltpu.CompilerParams(vmem_limit_bytes=MIB),
-        cost_estimate=FREE,
+        cost_estimate=cost(0),
     )(*[pltpu.with_memory_space_constraint(x, pltpu.HBM) for x in sources])
 
     outer = {e: swap(members, lambda d, e=e: (e & -e) * SPLIT) for e in range(1, experts)}
     first = swap(members, lambda d: 4 if d & 1 else 2)
     second = swap(members, lambda d: 2 if d & 1 else 4)
     sibling = swap(members, lambda d: 1)
-    order = list(range(experts))
-
-    blocks = {0: payload}
-    for e in order[1:]:
-        blocks[e] = outer[e](blocks[e & (e - 1)])
-    pieces, last = {}, ()
-    for n, e in enumerate(order):
-        if n > 1:
-            blocks[e], _ = lax.optimization_barrier((blocks[e], pieces[order[0]][0]))
-        (pair,) = call(
-            stack_kernel, [shape(2 * rows, full, BF16)], [blocks[e], first(blocks[e])], last
-        )
-        far = second(pair)
-        pieces[e] = [pair, far, sibling(pair), sibling(far)]
-        last = (pair, pieces[order[0]][1]) if n else (pair,)
-
-    gate, up, down = load([gate_weight[0], up_weight[0], down_weight[0]], last)
     mine = (lax.axis_index("local") // SPLIT).astype(jnp.int32)[None]
-    hidden_of, last = {}, ()
-    for at in range(0, experts, 2):
-        batch = order[at : at + 2]
-        xs = [p for e in batch for p in pieces[e]]
-        height = sum(x.shape[0] for x in xs)
-        hidden, scale = pl.pallas_call(
-            functools.partial(gate_kernel, len(xs), experts),
-            out_shape=[pltpu.VMEM((height, hid), BF16), pltpu.VMEM((height, LANES), F32)],
-            in_specs=[pl.BlockSpec(memory_space=pltpu.SMEM)] + [VMEM] * (len(xs) + 2) + [ANY] * len(last),
-            out_specs=[VMEM, VMEM],
-            compiler_params=pltpu.CompilerParams(vmem_limit_bytes=8 * MIB),
-            cost_estimate=FREE,
-        )(mine, *xs, gate, up, *last)
-        last = (hidden,)
-        for n, e in enumerate(batch):
-            hidden_of[e] = (n * height // len(batch), hidden, scale)
-
-    def descend(e, after):
-        start, hidden, scale = hidden_of[e]
-        half = SPLIT * rows // 2
-        return call(
-            functools.partial(down_kernel, start),
-            [shape(half, features, F32), shape(half, features, BF16)],
-            [hidden, scale, down],
-            after,
-        )
-
-    def add(kept, got, after):
-        half = kept.shape[0] // 2
-        return call(add_kernel, [shape(half, features, F32), shape(half, features, BF16)], [kept, got], after)
-
-    def close(kept, gots, after):
-        return call(close_kernel, [shape(rows, features, BF16)], [kept, *gots], after)[0]
-
-    back = order[::-1]
-    state, last, home = {}, (), {e: [] for e in order}
-    lag = (0, 1, 3, 4)
-    for slot in range(len(back) + lag[-1]):
-        for stage in range(4):
-            n = slot - lag[stage]
-            if not 0 <= n < len(back):
-                continue
-            e = back[n]
-            if stage == 0:
-                kept, sent = descend(e, last)
-                state[e] = (kept, sibling(sent))
-            elif stage == 1:
-                kept, sent = add(*state[e], last)
-                state[e] = (kept, second(sent))
-            elif stage == 2:
-                kept, sent = add(*state[e], last)
-                state[e] = (kept, first(sent))
-            else:
-                sent = close(state[e][0], [state[e][1], *home[e]], last)
-                if not e:
-                    return sent
-                home[e & (e - 1)].append(outer[e](sent))
-            last = (sent,)
+    weights = [gate_weight[0], up_weight[0], down_weight[0]]
+    height = SPLIT * rows
+    blocks, pairs, fars, nears, downs = {0: payload}, {}, {}, {}, {}
+    hidden_of, state, home = {}, {}, {e: [] for e in range(experts)}
+    last = (payload,)
+    for step, *at in plan(experts):
+        e = at[0] if at else None
+        if step == "fetch":
+            blocks[e] = outer[e](blocks[e & (e - 1)])
+            continue
+        if step == "behind":
+            last = (*last, blocks[e])
+            continue
+        if step == "hold":
+            fars[e], _ = lax.optimization_barrier((fars[e], downs[at[1]]))
+            continue
+        if step == "stack":
+            (out,) = call(stack_kernel, [shape(2 * rows, full, BF16)], [blocks[e], first(blocks[e])], last)
+            pairs[e], fars[e], nears[e] = out, second(out), sibling(out)
+        elif step == "load":
+            weights = load(weights, last)
+            out = weights[0]
+        elif step == "gate":
+            xs = [x for g in e for x in (pairs[g], fars[g], nears[g], sibling(fars[g]))]
+            out, scale = pl.pallas_call(
+                functools.partial(gate_kernel, len(xs), experts),
+                out_shape=[pltpu.VMEM((2 * height, hid), BF16), pltpu.VMEM((2 * height, LANES), F32)],
+                in_specs=[pl.BlockSpec(memory_space=pltpu.SMEM)] + [VMEM] * (len(xs) + 2) + [ANY] * len(last),
+                out_specs=[VMEM, VMEM],
+                compiler_params=pltpu.CompilerParams(vmem_limit_bytes=8 * MIB),
+                cost_estimate=cost(0),
+            )(mine, *xs, weights[0], weights[1], *last)
+            for n, g in enumerate(e):
+                hidden_of[g] = (n * height, out, scale)
+        elif step == "down":
+            begin, hidden, scale = hidden_of[e]
+            half = height // 2
+            kept, out = call(
+                functools.partial(down_kernel, begin),
+                [shape(half, features, F32), shape(half, features, BF16)],
+                [hidden, scale, weights[2]],
+                last,
+            )
+            downs[e] = out
+            state[e] = (kept, sibling(out))
+        elif step in ("add1", "add2"):
+            kept, got = state[e]
+            half = kept.shape[0] // 2
+            kept, out = call(
+                add_kernel, [shape(half, features, F32), shape(half, features, BF16)], [kept, got], last
+            )
+            state[e] = (kept, (second if step == "add1" else first)(out))
+        else:
+            (out,) = call(close_kernel, [shape(rows, features, BF16)], [*state[e], *home[e]], last)
+            if not e:
+                return out
+            home[e & (e - 1)].append(outer[e](out))
+        last = (out,)
 
 
 def solution(mesh):

time: 71.2 us -> 67.1 us (0.942)
  waiting for transfers between devices: 20.8 us -> 18.8 us
  Pallas kernels: 12.4 us -> 11.4 us
  starting transfers between devices: 36.9 us -> 35.9 us
    ppermute x34, waiting for transfers between devices: 20.8 us -> 18.8 us  [swap(): return lambda x: lax.ppermute(x, 'local', pairs)]
    ppermute x34, starting transfers between devices: 36.9 us -> 35.9 us  [swap(): return lambda x: lax.ppermute(x, 'local', pairs)]
    pallas_call x2, Pallas kernels: 3.29 us -> 2.35 us  [body(): pl.pallas_call(functools.partial(gate_kernel, len(xs), experts), out_shap...]
  transfers between devices with their start and end apart: 34 -> 34, of which waited for: 13 -> 15; matrix products, arithmetic and copies ran while one was open for 0% -> 0% of each run, Pallas kernels for 12% -> 13%
where the time goes in v3:
time: 67.1 us; the launch traced here: 66.9 us
  starting transfers between devices  35.9 us (54%)
  waiting for transfers between devices  18.8 us (28%)
  Pallas kernels  11.4 us (17%)
    ppermute x34, starting transfers between devices, swap(): return lambda x: lax.ppermute(x, 'local', pairs)  35.9 us
    ppermute x34, waiting for transfers between devices, swap(): return lambda x: lax.ppermute(x, 'local', pairs)  18.8 us
    pallas_call x1, Pallas kernels, load(): pl.pallas_call(run, out_shape=[pltpu.VMEM(a.shape, a.dtype) for a in arra...  4.25 us
    pallas_call x20, Pallas kernels, call(): pl.pallas_call(run, out_shape=[pltpu.VMEM(o.shape, o.dtype) for o in outs...  3.79 us
    pallas_call x2, Pallas kernels, body(): pl.pallas_call(functools.partial(gate_kernel, len(xs), experts), out_shap...  2.35 us
  transfers between devices with their start and end apart: 34, of which 15 were waited for; matrix products, arithmetic and copies ran while one was open for 0% of the time, Pallas kernels for 13%

profile of v3, /device:TPU:0, one launch (start us, length us, event | category | flops | bytes accessed | tf_op | source)
XLA Modules:
  0.0 66.9 jit_solution(5790476771926112017)
XLA Ops:
  1.1 3.1 %collective-permute-start.5 = (bf16[8,7296]{1,0:T(8,128)(2,1)S(1)}, bf16[8,7296]{1,0:T(8,128)(2,1)S(1)}, u32[]{:S(2)}, u32[]{:S(2)}) collective-permute-start(bf16[8,7296]{1,0:T(8,128)(2,1)S(1)} %shard_map.64.refs_0_.refs_2_), channel_id=1, source_target_pairs={{0,8},{1,9},{2,10},{3,11},{4,12},{5,13},{6,14},{7,15},{8,0},{9,1},... | collective-permute-start | bytes 350216 | tf_op jit(solution)/shard_map/ppermute | solution.py:27
  4.2 2.6 %collective-permute-start.1 = (bf16[8,7296]{1,0:T(8,128)(2,1)S(1)}, bf16[8,7296]{1,0:T(8,128)(2,1)S(1)}, u32[]{:S(2)}, u32[]{:S(2)}) collective-permute-start(bf16[8,7296]{1,0:T(8,128)(2,1)S(1)} %shard_map.64.refs_0_.refs_2_), channel_id=1, source_target_pairs={{0,16},{1,17},{2,18},{3,19},{4,20},{5,21},{6,22},{7,23},{8,24},{9,... | collective-permute-start | bytes 350216 | tf_op jit(solution)/shard_map/ppermute | solution.py:27
  6.7 1.5 %collective-permute-start = (bf16[8,7296]{1,0:T(8,128)(2,1)S(1)}, bf16[8,7296]{1,0:T(8,128)(2,1)S(1)}, u32[]{:S(2)}, u32[]{:S(2)}) collective-permute-start(bf16[8,7296]{1,0:T(8,128)(2,1)S(1)} %shard_map.64.refs_0_.refs_2_), channel_id=1, source_target_pairs={{0,2},{1,5},{2,0},{3,7},{4,6},{5,1},{6,4},{7,3},{8,10},{9,13},{10,... | collective-permute-start | bytes 350216 | tf_op jit(solution)/shard_map/ppermute | solution.py:27
  8.6 1.8 %collective-permute-start.6 = (bf16[8,7296]{1,0:T(8,128)(2,1)S(1)}, bf16[8,7296]{1,0:T(8,128)(2,1)S(1)}, u32[]{:S(2)}, u32[]{:S(2)}) collective-permute-start(bf16[8,7296]{1,0:T(8,128)(2,1)S(1)} %collective-permute-done.5.refs_0_), channel_id=1, source_target_pairs={{0,2},{1,5},{2,0},{3,7},{4,6},{5,1},{6,4},{7,3},{8,10},{9,13},{10,... | collective-permute-start | bytes 350216 | tf_op jit(solution)/shard_map/ppermute | solution.py:27
  10.4 1.9 %collective-permute-done.1.refs_3_.refs_0_ = bf16[8,7296]{1,0:T(8,128)(2,1)S(1)} collective-permute-done((bf16[8,7296]{1,0:T(8,128)(2,1)S(1)}, bf16[8,7296]{1,0:T(8,128)(2,1)S(1)}, u32[]{:S(2)}, u32[]{:S(2)}) %collective-permute-start.1) | collective-permute-done | bytes 116768 | tf_op jit(solution)/shard_map/ppermute | solution.py:27
  12.7 1.6 %collective-permute-start.2 = (bf16[16,7296]{1,0:T(8,128)(2,1)S(1)}, bf16[16,7296]{1,0:T(8,128)(2,1)S(1)}, u32[]{:S(2)}, u32[]{:S(2)}) collective-permute-start(bf16[16,7296]{1,0:T(8,128)(2,1)S(1)} %shard_map.65.refs_2_.refs_0_), channel_id=1, source_target_pairs={{0,4},{1,3},{2,6},{3,1},{4,0},{5,7},{6,2},{7,5},{8,12},{9,11},{10,... | collective-permute-start | bytes 700424 | tf_op jit(solution)/shard_map/ppermute | solution.py:27
  14.3 2.7 %collective-permute-done.7.refs_3_.refs_0_ = bf16[8,7296]{1,0:T(8,128)(2,1)S(1)} collective-permute-done((bf16[8,7296]{1,0:T(8,128)(2,1)S(1)}, bf16[8,7296]{1,0:T(8,128)(2,1)S(1)}, u32[]{:S(2)}, u32[]{:S(2)}) %collective-permute-start.7) | collective-permute-done | bytes 116768 | tf_op jit(solution)/shard_map/ppermute | solution.py:27
  17.1 1.6 %collective-permute-start.8 = (bf16[16,7296]{1,0:T(8,128)(2,1)S(1)}, bf16[16,7296]{1,0:T(8,128)(2,1)S(1)}, u32[]{:S(2)}, u32[]{:S(2)}) collective-permute-start(bf16[16,7296]{1,0:T(8,128)(2,1)S(1)} %shard_map.66.refs_2_.refs_4_), channel_id=1, source_target_pairs={{0,4},{1,3},{2,6},{3,1},{4,0},{5,7},{6,2},{7,5},{8,12},{9,11},{10,... | collective-permute-start | bytes 700424 | tf_op jit(solution)/shard_map/ppermute | solution.py:27
  18.7 1.5 %collective-permute-start.12 = (bf16[8,7296]{1,0:T(8,128)(2,1)S(1)}, bf16[8,7296]{1,0:T(8,128)(2,1)S(1)}, u32[]{:S(2)}, u32[]{:S(2)}) collective-permute-start(bf16[8,7296]{1,0:T(8,128)(2,1)S(1)} %collective-permute-done.1.refs_3_.refs_0_), channel_id=1, source_target_pairs={{0,2},{1,5},{2,0},{3,7},{4,6},{5,1},{6,4},{7,3},{8,10},{9,13},{10,... | collective-permute-start | bytes 350216 | tf_op jit(solution)/shard_map/ppermute | solution.py:27
  20.7 2.8 %collective-permute-done.12.refs_1_ = bf16[8,7296]{1,0:T(8,128)(2,1)S(1)} collective-permute-done((bf16[8,7296]{1,0:T(8,128)(2,1)S(1)}, bf16[8,7296]{1,0:T(8,128)(2,1)S(1)}, u32[]{:S(2)}, u32[]{:S(2)}) %collective-permute-start.12) | collective-permute-done | bytes 116768 | tf_op jit(solution)/shard_map/ppermute | solution.py:27
  25.0 2.3 %collective-permute-start.17 = (bf16[16,7296]{1,0:T(8,128)(2,1)S(1)}, bf16[16,7296]{1,0:T(8,128)(2,1)S(1)}, u32[]{:S(2)}, u32[]{:S(2)}) collective-permute-start(bf16[16,7296]{1,0:T(8,128)(2,1)S(1)} %shard_map.68.refs_3_.refs_4_), channel_id=1, source_target_pairs={{0,4},{1,3},{2,6},{3,1},{4,0},{5,7},{6,2},{7,5},{8,12},{9,11},{10,... | collective-permute-start | bytes 700424 | tf_op jit(solution)/shard_map/ppermute | solution.py:27
  27.5 4.2 %shard_map.69 = (bf16[7168,256]{1,0:T(8,128)(2,1)S(1)}, bf16[7168,256]{1,0:T(8,128)(2,1)S(1)}, bf16[256,7168]{1,0:T(8,128)(2,1)S(1)}) custom-call(bf16[7168,256]{1,0:T(8,128)(2,1)} %bitcast.6, bf16[7168,256]{1,0:T(8,128)(2,1)} %bitcast.7, bf16[256,7168]{1,0:T(8,128)(2,1)} %bitcast.8, bf16[16,7296]{1,0:T(8,128)(2,1)S(1)} %shard_map.68.refs_3_.refs_4_), custom_call_target="tpu_custom_call" | custom-call | bytes 14400000 | tf_op jit(solution)/shard_map/pallas_call | solution.py:139
  36.9 1.2 %shard_map.73 = (bf16[128,256]{1,0:T(8,128)(2,1)S(1)}, f32[128,128]{1,0:T(8,128)S(1)}) custom-call(s32[1]{0:T(128)} %bitcast.mine_ref, bf16[16,7296]{1,0:T(8,128)(2,1)S(1)} %shard_map.67.refs_2_.refs_0_, bf16[16,7296]{1,0:T(8,128)(2,1)S(1)} %collective-permute-done.14.refs_1_, bf16[16,7296]{1,0:T(8,128)(2,1)S(1)} %collective-permute-done.15.refs_2_, ...), custom_call_target="tpu_custom_call" | custom-call | tf_op jit(solution)/shard_map/pallas_call | solution.py:215
  40.9 2.0 %collective-permute-start.21 = (bf16[16,7168]{1,0:T(8,128)(2,1)S(1)}, bf16[16,7168]{1,0:T(8,128)(2,1)S(1)}, u32[]{:S(2)}, u32[]{:S(2)}) collective-permute-start(bf16[16,7168]{1,0:T(8,128)(2,1)S(1)} %get-tuple-element.54.refs_2_), channel_id=1, source_target_pairs={{0,4},{1,3},{2,6},{3,1},{4,0},{5,7},{6,2},{7,5},{8,12},{9,11},{10,... | collective-permute-start | bytes 688136 | tf_op jit(solution)/shard_map/ppermute | solution.py:27
  43.9 1.3 %collective-permute-start.29 = (bf16[16,7168]{1,0:T(8,128)(2,1)S(1)}, bf16[16,7168]{1,0:T(8,128)(2,1)S(1)}, u32[]{:S(2)}, u32[]{:S(2)}) collective-permute-start(bf16[16,7168]{1,0:T(8,128)(2,1)S(1)} %get-tuple-element.58.refs_2_), channel_id=1, source_target_pairs={{0,4},{1,3},{2,6},{3,1},{4,0},{5,7},{6,2},{7,5},{8,12},{9,11},{10,... | collective-permute-start | bytes 688136 | tf_op jit(solution)/shard_map/ppermute | solution.py:27
  45.2 1.8 %collective-permute-done.21.refs_1_ = bf16[16,7168]{1,0:T(8,128)(2,1)S(1)} collective-permute-done((bf16[16,7168]{1,0:T(8,128)(2,1)S(1)}, bf16[16,7168]{1,0:T(8,128)(2,1)S(1)}, u32[]{:S(2)}, u32[]{:S(2)}) %collective-permute-start.21) | collective-permute-done | bytes 229408 | tf_op jit(solution)/shard_map/ppermute | solution.py:27
  47.0 1.5 %collective-permute-start.27 = (bf16[8,7168]{1,0:T(8,128)(2,1)S(1)}, bf16[8,7168]{1,0:T(8,128)(2,1)S(1)}, u32[]{:S(2)}, u32[]{:S(2)}) collective-permute-start(bf16[8,7168]{1,0:T(8,128)(2,1)S(1)} %get-tuple-element.59.refs_2_), channel_id=1, source_target_pairs={{0,2},{1,5},{2,0},{3,7},{4,6},{5,1},{6,4},{7,3},{8,10},{9,13},{10,... | collective-permute-start | bytes 344072 | tf_op jit(solution)/shard_map/ppermute | solution.py:27
  48.6 2.0 %collective-permute-start.24 = (bf16[16,7168]{1,0:T(8,128)(2,1)S(1)}, bf16[16,7168]{1,0:T(8,128)(2,1)S(1)}, u32[]{:S(2)}, u32[]{:S(2)}) collective-permute-start(bf16[16,7168]{1,0:T(8,128)(2,1)S(1)} %get-tuple-element.61.refs_2_), channel_id=1, source_target_pairs={{0,4},{1,3},{2,6},{3,1},{4,0},{5,7},{6,2},{7,5},{8,12},{9,11},{10,... | collective-permute-start | bytes 688136 | tf_op jit(solution)/shard_map/ppermute | solution.py:27
  51.3 1.9 %collective-permute-done.27.refs_1_ = bf16[8,7168]{1,0:T(8,128)(2,1)S(1)} collective-permute-done((bf16[8,7168]{1,0:T(8,128)(2,1)S(1)}, bf16[8,7168]{1,0:T(8,128)(2,1)S(1)}, u32[]{:S(2)}, u32[]{:S(2)}) %collective-permute-start.27) | collective-permute-done | bytes 114720 | tf_op jit(solution)/shard_map/ppermute | solution.py:27
  54.1 1.9 %collective-permute-start.32 = (bf16[8,7168]{1,0:T(8,128)(2,1)S(1)}, bf16[8,7168]{1,0:T(8,128)(2,1)S(1)}, u32[]{:S(2)}, u32[]{:S(2)}) collective-permute-start(bf16[8,7168]{1,0:T(8,128)(2,1)S(1)} %get-tuple-element.67.refs_3_), channel_id=1, source_target_pairs={{0,2},{1,5},{2,0},{3,7},{4,6},{5,1},{6,4},{7,3},{8,10},{9,13},{10,... | collective-permute-start | bytes 344072 | tf_op jit(solution)/shard_map/ppermute | solution.py:27
  56.0 2.0 %collective-permute-done.28.refs_2_ = bf16[8,7168]{1,0:T(8,128)(2,1)S(1)} collective-permute-done((bf16[8,7168]{1,0:T(8,128)(2,1)S(1)}, bf16[8,7168]{1,0:T(8,128)(2,1)S(1)}, u32[]{:S(2)}, u32[]{:S(2)}) %collective-permute-start.28) | collective-permute-done | bytes 114720 | tf_op jit(solution)/shard_map/ppermute | solution.py:27
  59.4 2.1 %collective-permute-start.33 = (bf16[8,7168]{1,0:T(8,128)(2,1)S(1)}, bf16[8,7168]{1,0:T(8,128)(2,1)S(1)}, u32[]{:S(2)}, u32[]{:S(2)}) collective-permute-start(bf16[8,7168]{1,0:T(8,128)(2,1)S(1)} %shard_map.86.refs_4_), channel_id=1, source_target_pairs={{0,8},{1,9},{2,10},{3,11},{4,12},{5,13},{6,14},{7,15},{8,0},{9,1},... | collective-permute-start | bytes 344072 | tf_op jit(solution)/shard_map/ppermute | solution.py:27
  61.4 1.5 %collective-permute-start.30 = (bf16[8,7168]{1,0:T(8,128)(2,1)S(1)}, bf16[8,7168]{1,0:T(8,128)(2,1)S(1)}, u32[]{:S(2)}, u32[]{:S(2)}) collective-permute-start(bf16[8,7168]{1,0:T(8,128)(2,1)S(1)} %get-tuple-element.69.refs_2_), channel_id=1, source_target_pairs={{0,2},{1,5},{2,0},{3,7},{4,6},{5,1},{6,4},{7,3},{8,10},{9,13},{10,... | collective-permute-start | bytes 344072 | tf_op jit(solution)/shard_map/ppermute | solution.py:27
  62.9 2.2 %collective-permute-done.31.refs_2_ = bf16[8,7168]{1,0:T(8,128)(2,1)S(1)} collective-permute-done((bf16[8,7168]{1,0:T(8,128)(2,1)S(1)}, bf16[8,7168]{1,0:T(8,128)(2,1)S(1)}, u32[]{:S(2)}, u32[]{:S(2)}) %collective-permute-start.31) | collective-permute-done | bytes 114720 | tf_op jit(solution)/shard_map/ppermute | solution.py:27
  (69 shorter events, 17.8 us)
Async XLA Ops:
  1.1 7.5 %collective-permute-start.5 = (bf16[8,7296]{1,0:T(8,128)(2,1)S(1)}, bf16[8,7296]{1,0:T(8,128)(2,1)S(1)}, u32[]{:S(2)}, u32[]{:S(2)}) collective-permute-start(bf16[8,7296]{1,0:T(8,128)(2,1)S(1)} %shard_map.64.refs_0_.refs_2_), channel_id=1, source_target_pairs={{0,8},{1,9},{2,10},{3,11},{4,12},{5,13},{6,14},{7,15},{8,0},{9,1},... | collective-permute-start | bytes 350216 | tf_op jit(solution)/shard_map/ppermute | solution.py:27
  4.2 8.1 %collective-permute-start.1 = (bf16[8,7296]{1,0:T(8,128)(2,1)S(1)}, bf16[8,7296]{1,0:T(8,128)(2,1)S(1)}, u32[]{:S(2)}, u32[]{:S(2)}) collective-permute-start(bf16[8,7296]{1,0:T(8,128)(2,1)S(1)} %shard_map.64.refs_0_.refs_2_), channel_id=1, source_target_pairs={{0,16},{1,17},{2,18},{3,19},{4,20},{5,21},{6,22},{7,23},{8,24},{9,... | collective-permute-start | bytes 350216 | tf_op jit(solution)/shard_map/ppermute | solution.py:27
  6.7 6.0 %collective-permute-start = (bf16[8,7296]{1,0:T(8,128)(2,1)S(1)}, bf16[8,7296]{1,0:T(8,128)(2,1)S(1)}, u32[]{:S(2)}, u32[]{:S(2)}) collective-permute-start(bf16[8,7296]{1,0:T(8,128)(2,1)S(1)} %shard_map.64.refs_0_.refs_2_), channel_id=1, source_target_pairs={{0,2},{1,5},{2,0},{3,7},{4,6},{5,1},{6,4},{7,3},{8,10},{9,13},{10,... | collective-permute-start | bytes 350216 | tf_op jit(solution)/shard_map/ppermute | solution.py:27
  8.6 5.8 %collective-permute-start.6 = (bf16[8,7296]{1,0:T(8,128)(2,1)S(1)}, bf16[8,7296]{1,0:T(8,128)(2,1)S(1)}, u32[]{:S(2)}, u32[]{:S(2)}) collective-permute-start(bf16[8,7296]{1,0:T(8,128)(2,1)S(1)} %collective-permute-done.5.refs_0_), channel_id=1, source_target_pairs={{0,2},{1,5},{2,0},{3,7},{4,6},{5,1},{6,4},{7,3},{8,10},{9,13},{10,... | collective-permute-start | bytes 350216 | tf_op jit(solution)/shard_map/ppermute | solution.py:27
  12.7 11.7 %collective-permute-start.2 = (bf16[16,7296]{1,0:T(8,128)(2,1)S(1)}, bf16[16,7296]{1,0:T(8,128)(2,1)S(1)}, u32[]{:S(2)}, u32[]{:S(2)}) collective-permute-start(bf16[16,7296]{1,0:T(8,128)(2,1)S(1)} %shard_map.65.refs_2_.refs_0_), channel_id=1, source_target_pairs={{0,4},{1,3},{2,6},{3,1},{4,0},{5,7},{6,2},{7,5},{8,12},{9,11},{10,... | collective-permute-start | bytes 700424 | tf_op jit(solution)/shard_map/ppermute | solution.py:27
  17.1 7.6 %collective-permute-start.8 = (bf16[16,7296]{1,0:T(8,128)(2,1)S(1)}, bf16[16,7296]{1,0:T(8,128)(2,1)S(1)}, u32[]{:S(2)}, u32[]{:S(2)}) collective-permute-start(bf16[16,7296]{1,0:T(8,128)(2,1)S(1)} %shard_map.66.refs_2_.refs_4_), channel_id=1, source_target_pairs={{0,4},{1,3},{2,6},{3,1},{4,0},{5,7},{6,2},{7,5},{8,12},{9,11},{10,... | collective-permute-start | bytes 700424 | tf_op jit(solution)/shard_map/ppermute | solution.py:27
  18.7 8.7 %collective-permute-start.3 = (bf16[16,7296]{1,0:T(8,128)(2,1)S(1)}, bf16[16,7296]{1,0:T(8,128)(2,1)S(1)}, u32[]{:S(2)}, u32[]{:S(2)}) collective-permute-start(bf16[16,7296]{1,0:T(8,128)(2,1)S(1)} %shard_map.65.refs_2_.refs_0_), channel_id=1, source_target_pairs={{0,1},{1,0},{2,3},{3,2},{4,5},{5,4},{6,7},{7,6},{8,9},{9,8},{10,11... | collective-permute-start | bytes 700424 | tf_op jit(solution)/shard_map/ppermute | solution.py:27
  18.7 4.8 %collective-permute-start.12 = (bf16[8,7296]{1,0:T(8,128)(2,1)S(1)}, bf16[8,7296]{1,0:T(8,128)(2,1)S(1)}, u32[]{:S(2)}, u32[]{:S(2)}) collective-permute-start(bf16[8,7296]{1,0:T(8,128)(2,1)S(1)} %collective-permute-done.1.refs_3_.refs_0_), channel_id=1, source_target_pairs={{0,2},{1,5},{2,0},{3,7},{4,6},{5,1},{6,4},{7,3},{8,10},{9,13},{10,... | collective-permute-start | bytes 350216 | tf_op jit(solution)/shard_map/ppermute | solution.py:27
  23.5 8.2 %collective-permute-start.9 = (bf16[16,7296]{1,0:T(8,128)(2,1)S(1)}, bf16[16,7296]{1,0:T(8,128)(2,1)S(1)}, u32[]{:S(2)}, u32[]{:S(2)}) collective-permute-start(bf16[16,7296]{1,0:T(8,128)(2,1)S(1)} %shard_map.66.refs_2_.refs_4_), channel_id=1, source_target_pairs={{0,1},{1,0},{2,3},{3,2},{4,5},{5,4},{6,7},{7,6},{8,9},{9,8},{10,11... | collective-permute-start | bytes 700424 | tf_op jit(solution)/shard_map/ppermute | solution.py:27
  24.4 7.4 %collective-permute-start.4 = (bf16[16,7296]{1,0:T(8,128)(2,1)S(1)}, bf16[16,7296]{1,0:T(8,128)(2,1)S(1)}, u32[]{:S(2)}, u32[]{:S(2)}) collective-permute-start(bf16[16,7296]{1,0:T(8,128)(2,1)S(1)} %collective-permute-done.2.refs_1_), channel_id=1, source_target_pairs={{0,1},{1,0},{2,3},{3,2},{4,5},{5,4},{6,7},{7,6},{8,9},{9,8},{10,11... | collective-permute-start | bytes 700424 | tf_op jit(solution)/shard_map/ppermute | solution.py:27
  24.7 7.6 %collective-permute-start.10 = (bf16[16,7296]{1,0:T(8,128)(2,1)S(1)}, bf16[16,7296]{1,0:T(8,128)(2,1)S(1)}, u32[]{:S(2)}, u32[]{:S(2)}) collective-permute-start(bf16[16,7296]{1,0:T(8,128)(2,1)S(1)} %collective-permute-done.8.refs_5_), channel_id=1, source_target_pairs={{0,1},{1,0},{2,3},{3,2},{4,5},{5,4},{6,7},{7,6},{8,9},{9,8},{10,11... | collective-permute-start | bytes 700424 | tf_op jit(solution)/shard_map/ppermute | solution.py:27
  25.0 10.0 %collective-permute-start.17 = (bf16[16,7296]{1,0:T(8,128)(2,1)S(1)}, bf16[16,7296]{1,0:T(8,128)(2,1)S(1)}, u32[]{:S(2)}, u32[]{:S(2)}) collective-permute-start(bf16[16,7296]{1,0:T(8,128)(2,1)S(1)} %shard_map.68.refs_3_.refs_4_), channel_id=1, source_target_pairs={{0,4},{1,3},{2,6},{3,1},{4,0},{5,7},{6,2},{7,5},{8,12},{9,11},{10,... | collective-permute-start | bytes 700424 | tf_op jit(solution)/shard_map/ppermute | solution.py:27
  27.4 7.6 %collective-permute-start.14 = (bf16[16,7296]{1,0:T(8,128)(2,1)S(1)}, bf16[16,7296]{1,0:T(8,128)(2,1)S(1)}, u32[]{:S(2)}, u32[]{:S(2)}) collective-permute-start(bf16[16,7296]{1,0:T(8,128)(2,1)S(1)} %shard_map.67.refs_2_.refs_0_), channel_id=1, source_target_pairs={{0,4},{1,3},{2,6},{3,1},{4,0},{5,7},{6,2},{7,5},{8,12},{9,11},{10,... | collective-permute-start | bytes 700424 | tf_op jit(solution)/shard_map/ppermute | solution.py:27
  40.5 8.1 %collective-permute-start.13 = (bf16[32,7168]{1,0:T(8,128)(2,1)S(1)}, bf16[32,7168]{1,0:T(8,128)(2,1)S(1)}, u32[]{:S(2)}, u32[]{:S(2)}) collective-permute-start(bf16[32,7168]{1,0:T(8,128)(2,1)S(1)} %get-tuple-element.45.refs_10_), channel_id=1, source_target_pairs={{0,1},{1,0},{2,3},{3,2},{4,5},{5,4},{6,7},{7,6},{8,9},{9,8},{10,11... | collective-permute-start | bytes 1376264 | tf_op jit(solution)/shard_map/ppermute | solution.py:27
  40.9 6.1 %collective-permute-start.21 = (bf16[16,7168]{1,0:T(8,128)(2,1)S(1)}, bf16[16,7168]{1,0:T(8,128)(2,1)S(1)}, u32[]{:S(2)}, u32[]{:S(2)}) collective-permute-start(bf16[16,7168]{1,0:T(8,128)(2,1)S(1)} %get-tuple-element.54.refs_2_), channel_id=1, source_target_pairs={{0,4},{1,3},{2,6},{3,1},{4,0},{5,7},{6,2},{7,5},{8,12},{9,11},{10,... | collective-permute-start | bytes 688136 | tf_op jit(solution)/shard_map/ppermute | solution.py:27
  43.0 7.7 %collective-permute-start.25 = (bf16[16,7168]{1,0:T(8,128)(2,1)S(1)}, bf16[16,7168]{1,0:T(8,128)(2,1)S(1)}, u32[]{:S(2)}, u32[]{:S(2)}) collective-permute-start(bf16[16,7168]{1,0:T(8,128)(2,1)S(1)} %get-tuple-element.57.refs_2_), channel_id=1, source_target_pairs={{0,4},{1,3},{2,6},{3,1},{4,0},{5,7},{6,2},{7,5},{8,12},{9,11},{10,... | collective-permute-start | bytes 688136 | tf_op jit(solution)/shard_map/ppermute | solution.py:27
  43.9 10.1 %collective-permute-start.29 = (bf16[16,7168]{1,0:T(8,128)(2,1)S(1)}, bf16[16,7168]{1,0:T(8,128)(2,1)S(1)}, u32[]{:S(2)}, u32[]{:S(2)}) collective-permute-start(bf16[16,7168]{1,0:T(8,128)(2,1)S(1)} %get-tuple-element.58.refs_2_), channel_id=1, source_target_pairs={{0,4},{1,3},{2,6},{3,1},{4,0},{5,7},{6,2},{7,5},{8,12},{9,11},{10,... | collective-permute-start | bytes 688136 | tf_op jit(solution)/shard_map/ppermute | solution.py:27
  47.0 6.2 %collective-permute-start.27 = (bf16[8,7168]{1,0:T(8,128)(2,1)S(1)}, bf16[8,7168]{1,0:T(8,128)(2,1)S(1)}, u32[]{:S(2)}, u32[]{:S(2)}) collective-permute-start(bf16[8,7168]{1,0:T(8,128)(2,1)S(1)} %get-tuple-element.59.refs_2_), channel_id=1, source_target_pairs={{0,2},{1,5},{2,0},{3,7},{4,6},{5,1},{6,4},{7,3},{8,10},{9,13},{10,... | collective-permute-start | bytes 344072 | tf_op jit(solution)/shard_map/ppermute | solution.py:27
  48.6 10.6 %collective-permute-start.24 = (bf16[16,7168]{1,0:T(8,128)(2,1)S(1)}, bf16[16,7168]{1,0:T(8,128)(2,1)S(1)}, u32[]{:S(2)}, u32[]{:S(2)}) collective-permute-start(bf16[16,7168]{1,0:T(8,128)(2,1)S(1)} %get-tuple-element.61.refs_2_), channel_id=1, source_target_pairs={{0,4},{1,3},{2,6},{3,1},{4,0},{5,7},{6,2},{7,5},{8,12},{9,11},{10,... | collective-permute-start | bytes 688136 | tf_op jit(solution)/shard_map/ppermute | solution.py:27
  50.7 5.3 %collective-permute-start.26 = (bf16[8,7168]{1,0:T(8,128)(2,1)S(1)}, bf16[8,7168]{1,0:T(8,128)(2,1)S(1)}, u32[]{:S(2)}, u32[]{:S(2)}) collective-permute-start(bf16[8,7168]{1,0:T(8,128)(2,1)S(1)} %get-tuple-element.64.refs_2_), channel_id=1, source_target_pairs={{0,2},{1,5},{2,0},{3,7},{4,6},{5,1},{6,4},{7,3},{8,10},{9,13},{10,... | collective-permute-start | bytes 344072 | tf_op jit(solution)/shard_map/ppermute | solution.py:27
  53.2 4.9 %collective-permute-start.28 = (bf16[8,7168]{1,0:T(8,128)(2,1)S(1)}, bf16[8,7168]{1,0:T(8,128)(2,1)S(1)}, u32[]{:S(2)}, u32[]{:S(2)}) collective-permute-start(bf16[8,7168]{1,0:T(8,128)(2,1)S(1)} %shard_map.82.refs_2_), channel_id=1, source_target_pairs={{0,8},{1,9},{2,10},{3,11},{4,12},{5,13},{6,14},{7,15},{8,0},{9,1},... | collective-permute-start | bytes 344072 | tf_op jit(solution)/shard_map/ppermute | solution.py:27
  54.1 5.2 %collective-permute-start.32 = (bf16[8,7168]{1,0:T(8,128)(2,1)S(1)}, bf16[8,7168]{1,0:T(8,128)(2,1)S(1)}, u32[]{:S(2)}, u32[]{:S(2)}) collective-permute-start(bf16[8,7168]{1,0:T(8,128)(2,1)S(1)} %get-tuple-element.67.refs_3_), channel_id=1, source_target_pairs={{0,2},{1,5},{2,0},{3,7},{4,6},{5,1},{6,4},{7,3},{8,10},{9,13},{10,... | collective-permute-start | bytes 344072 | tf_op jit(solution)/shard_map/ppermute | solution.py:27
  58.1 7.0 %collective-permute-start.31 = (bf16[8,7168]{1,0:T(8,128)(2,1)S(1)}, bf16[8,7168]{1,0:T(8,128)(2,1)S(1)}, u32[]{:S(2)}, u32[]{:S(2)}) collective-permute-start(bf16[8,7168]{1,0:T(8,128)(2,1)S(1)} %shard_map.84.refs_2_), channel_id=1, source_target_pairs={{0,16},{1,17},{2,18},{3,19},{4,20},{5,21},{6,22},{7,23},{8,24},{9,... | collective-permute-start | bytes 344072 | tf_op jit(solution)/shard_map/ppermute | solution.py:27
  59.4 5.9 %collective-permute-start.33 = (bf16[8,7168]{1,0:T(8,128)(2,1)S(1)}, bf16[8,7168]{1,0:T(8,128)(2,1)S(1)}, u32[]{:S(2)}, u32[]{:S(2)}) collective-permute-start(bf16[8,7168]{1,0:T(8,128)(2,1)S(1)} %shard_map.86.refs_4_), channel_id=1, source_target_pairs={{0,8},{1,9},{2,10},{3,11},{4,12},{5,13},{6,14},{7,15},{8,0},{9,1},... | collective-permute-start | bytes 344072 | tf_op jit(solution)/shard_map/ppermute | solution.py:27
  (10 other events, 33.9 us)

commit v4 on v3

--- a/solution.py
+++ b/solution.py
@@ -95,15 +95,15 @@
     scale_ref[...] = jnp.broadcast_to(scale, scale_ref.shape)
 
 
-def down_kernel(start, hidden_ref, scale_ref, down_ref, kept_ref, sent_ref):
-    half, features = kept_ref.shape
-    hidden = hidden_ref[start : start + 2 * half, :]
-    scale = scale_ref[start : start + 2 * half, :1]
+def down_kernel(hidden_ref, scale_ref, down_ref, *refs):
+    half, features = refs[0].shape
     for lo in range(0, features, TILE):
         tile = slice(lo, lo + TILE)
-        out = jnp.dot(hidden, down_ref[:, tile], preferred_element_type=F32) * scale
-        kept_ref[:, tile] = out[:half]
-        sent_ref[:, tile] = out[half:].astype(BF16)
+        out = jnp.dot(hidden_ref[...], down_ref[:, tile], preferred_element_type=F32) * scale_ref[:, :1]
+        for n in range(2):
+            begin = 2 * n * half
+            refs[2 * n][:, tile] = out[begin : begin + half]
+            refs[2 * n + 1][:, tile] = out[begin + half : begin + 2 * half].astype(BF16)
 
 
 def add_kernel(kept_ref, got_ref, next_ref, sent_ref):
@@ -121,7 +121,7 @@
 
 
 def load(arrays, after):
-    count, parts = len(arrays), 2
+    count, parts = len(arrays), 8
 
     def run(*refs):
         outs, sems = refs[count + len(after) : -1], refs[-1]
@@ -152,10 +152,11 @@
     steps = [("fetch", e) for e in sorted(range(1, experts), key=lambda e: (bin(e).count("1"), -e))]
     steps += [("behind", far[0]), ("stack", 0), ("behind", far[-1])] + [("stack", e) for e in range(1, experts)]
     steps += [("load",)]
-    for e in near[::2]:
-        steps += [("gate", (e, e + 1)), ("down", e + 1), ("down", e)]
-    steps += [("hold", e, near[-2]) for e in far]
-    steps += [("gate", (e, e + 1)) for e in far[::2]] + [("down", e) for e in far[::-1]]
+    steps += [("gate", (e, e + 1)) for e in near[::2]]
+    steps += [("hold", e, (near[-2], near[-1])) for e in far]
+    steps += [("down", (e, e + 1)) for e in near[::2]]
+    steps += [("gate", (e, e + 1)) for e in far[::2]]
+    steps += [("down", (e, e + 1)) for e in far[::2][::-1]]
     back = range(experts)[::-1]
     for slot in range(experts + 3):
         for step, lag in (("add1", 0), ("add2", 2), ("close", 3)):
@@ -190,7 +191,7 @@
     mine = (lax.axis_index("local") // SPLIT).astype(jnp.int32)[None]
     weights = [gate_weight[0], up_weight[0], down_weight[0]]
     height = SPLIT * rows
-    blocks, pairs, fars, nears, downs = {0: payload}, {}, {}, {}, {}
+    blocks, pairs, fars, nears = {0: payload}, {}, {}, {}
     hidden_of, state, home = {}, {}, {e: [] for e in range(experts)}
     last = (payload,)
     for step, *at in plan(experts):
@@ -202,7 +203,7 @@
             last = (*last, blocks[e])
             continue
         if step == "hold":
-            fars[e], _ = lax.optimization_barrier((fars[e], downs[at[1]]))
+            fars[e], _ = lax.optimization_barrier((fars[e], hidden_of[at[1]][0]))
             continue
         if step == "stack":
             (out,) = call(stack_kernel, [shape(2 * rows, full, BF16)], [blocks[e], first(blocks[e])], last)
@@ -220,19 +221,17 @@
                 compiler_params=pltpu.CompilerParams(vmem_limit_bytes=8 * MIB),
                 cost_estimate=cost(0),
             )(mine, *xs, weights[0], weights[1], *last)
-            for n, g in enumerate(e):
-                hidden_of[g] = (n * height, out, scale)
+            hidden_of[e] = (out, scale)
         elif step == "down":
-            begin, hidden, scale = hidden_of[e]
             half = height // 2
-            kept, out = call(
-                functools.partial(down_kernel, begin),
-                [shape(half, features, F32), shape(half, features, BF16)],
-                [hidden, scale, weights[2]],
+            made = call(
+                down_kernel,
+                [shape(half, features, t) for t in (F32, BF16, F32, BF16)],
+                [*hidden_of[e], weights[2]],
                 last,
             )
-            downs[e] = out
-            state[e] = (kept, sibling(out))
+            out = made[-1]
+            state[e[1]], state[e[0]] = (made[2], sibling(out)), (made[0], sibling(made[1]))
         elif step in ("add1", "add2"):
             kept, got = state[e]
             half = kept.shape[0] // 2

time: 67.1 us -> 65.6 us (0.978)
  Pallas kernels: 11.4 us -> 9.8 us
    pallas_call x20 -> x18, Pallas kernels: 3.79 us -> 2.08 us  [call(): pl.pallas_call(run, out_shape=[pltpu.VMEM(o.shape, o.dtype) for o in outs...]
  transfers between devices with their start and end apart: 34 -> 34, of which waited for: 15 -> 17; matrix products, arithmetic and copies ran while one was open for 0% -> 0% of each run, Pallas kernels for 13% -> 10%
where the time goes in v4:
time: 65.6 us; the launch traced here: 65.4 us
  starting transfers between devices  36.1 us (55%)
  waiting for transfers between devices  18.7 us (29%)
  Pallas kernels  9.8 us (15%)
    ppermute x34, starting transfers between devices, swap(): return lambda x: lax.ppermute(x, 'local', pairs)  36.1 us
    ppermute x34, waiting for transfers between devices, swap(): return lambda x: lax.ppermute(x, 'local', pairs)  18.7 us
    pallas_call x1, Pallas kernels, load(): pl.pallas_call(run, out_shape=[pltpu.VMEM(a.shape, a.dtype) for a in arra...  4.32 us
    pallas_call x2, Pallas kernels, body(): pl.pallas_call(functools.partial(gate_kernel, len(xs), experts), out_shap...  2.34 us
    pallas_call x18, Pallas kernels, call(): pl.pallas_call(run, out_shape=[pltpu.VMEM(o.shape, o.dtype) for o in outs...  2.08 us
  transfers between devices with their start and end apart: 34, of which 17 were waited for; matrix products, arithmetic and copies ran while one was open for 0% of the time, Pallas kernels for 10%

profile of v4, /device:TPU:0, one launch (start us, length us, event | category | flops | bytes accessed | tf_op | source)
XLA Modules:
  0.0 65.4 jit_solution(12501718666779775533)
XLA Ops:
  1.1 3.1 %collective-permute-start.5 = (bf16[8,7296]{1,0:T(8,128)(2,1)S(1)}, bf16[8,7296]{1,0:T(8,128)(2,1)S(1)}, u32[]{:S(2)}, u32[]{:S(2)}) collective-permute-start(bf16[8,7296]{1,0:T(8,128)(2,1)S(1)} %shard_map.64.refs_0_.refs_2_), channel_id=1, source_target_pairs={{0,8},{1,9},{2,10},{3,11},{4,12},{5,13},{6,14},{7,15},{8,0},{9,1},... | collective-permute-start | bytes 350216 | tf_op jit(solution)/shard_map/ppermute | solution.py:27
  4.2 2.6 %collective-permute-start.1 = (bf16[8,7296]{1,0:T(8,128)(2,1)S(1)}, bf16[8,7296]{1,0:T(8,128)(2,1)S(1)}, u32[]{:S(2)}, u32[]{:S(2)}) collective-permute-start(bf16[8,7296]{1,0:T(8,128)(2,1)S(1)} %shard_map.64.refs_0_.refs_2_), channel_id=1, source_target_pairs={{0,16},{1,17},{2,18},{3,19},{4,20},{5,21},{6,22},{7,23},{8,24},{9,... | collective-permute-start | bytes 350216 | tf_op jit(solution)/shard_map/ppermute | solution.py:27
  6.7 1.5 %collective-permute-start = (bf16[8,7296]{1,0:T(8,128)(2,1)S(1)}, bf16[8,7296]{1,0:T(8,128)(2,1)S(1)}, u32[]{:S(2)}, u32[]{:S(2)}) collective-permute-start(bf16[8,7296]{1,0:T(8,128)(2,1)S(1)} %shard_map.64.refs_0_.refs_2_), channel_id=1, source_target_pairs={{0,2},{1,5},{2,0},{3,7},{4,6},{5,1},{6,4},{7,3},{8,10},{9,13},{10,... | collective-permute-start | bytes 350216 | tf_op jit(solution)/shard_map/ppermute | solution.py:27
  8.6 1.8 %collective-permute-start.6 = (bf16[8,7296]{1,0:T(8,128)(2,1)S(1)}, bf16[8,7296]{1,0:T(8,128)(2,1)S(1)}, u32[]{:S(2)}, u32[]{:S(2)}) collective-permute-start(bf16[8,7296]{1,0:T(8,128)(2,1)S(1)} %collective-permute-done.5.refs_0_), channel_id=1, source_target_pairs={{0,2},{1,5},{2,0},{3,7},{4,6},{5,1},{6,4},{7,3},{8,10},{9,13},{10,... | collective-permute-start | bytes 350216 | tf_op jit(solution)/shard_map/ppermute | solution.py:27
  10.4 1.9 %collective-permute-done.1.refs_3_.refs_0_ = bf16[8,7296]{1,0:T(8,128)(2,1)S(1)} collective-permute-done((bf16[8,7296]{1,0:T(8,128)(2,1)S(1)}, bf16[8,7296]{1,0:T(8,128)(2,1)S(1)}, u32[]{:S(2)}, u32[]{:S(2)}) %collective-permute-start.1) | collective-permute-done | bytes 116768 | tf_op jit(solution)/shard_map/ppermute | solution.py:27
  12.7 1.6 %collective-permute-start.2 = (bf16[16,7296]{1,0:T(8,128)(2,1)S(1)}, bf16[16,7296]{1,0:T(8,128)(2,1)S(1)}, u32[]{:S(2)}, u32[]{:S(2)}) collective-permute-start(bf16[16,7296]{1,0:T(8,128)(2,1)S(1)} %shard_map.65.refs_2_.refs_0_), channel_id=1, source_target_pairs={{0,4},{1,3},{2,6},{3,1},{4,0},{5,7},{6,2},{7,5},{8,12},{9,11},{10,... | collective-permute-start | bytes 700424 | tf_op jit(solution)/shard_map/ppermute | solution.py:27
  14.3 2.7 %collective-permute-done.7.refs_3_.refs_0_ = bf16[8,7296]{1,0:T(8,128)(2,1)S(1)} collective-permute-done((bf16[8,7296]{1,0:T(8,128)(2,1)S(1)}, bf16[8,7296]{1,0:T(8,128)(2,1)S(1)}, u32[]{:S(2)}, u32[]{:S(2)}) %collective-permute-start.7) | collective-permute-done | bytes 116768 | tf_op jit(solution)/shard_map/ppermute | solution.py:27
  17.1 1.6 %collective-permute-start.8 = (bf16[16,7296]{1,0:T(8,128)(2,1)S(1)}, bf16[16,7296]{1,0:T(8,128)(2,1)S(1)}, u32[]{:S(2)}, u32[]{:S(2)}) collective-permute-start(bf16[16,7296]{1,0:T(8,128)(2,1)S(1)} %shard_map.66.refs_2_.refs_4_), channel_id=1, source_target_pairs={{0,4},{1,3},{2,6},{3,1},{4,0},{5,7},{6,2},{7,5},{8,12},{9,11},{10,... | collective-permute-start | bytes 700424 | tf_op jit(solution)/shard_map/ppermute | solution.py:27
  18.7 1.5 %collective-permute-start.12 = (bf16[8,7296]{1,0:T(8,128)(2,1)S(1)}, bf16[8,7296]{1,0:T(8,128)(2,1)S(1)}, u32[]{:S(2)}, u32[]{:S(2)}) collective-permute-start(bf16[8,7296]{1,0:T(8,128)(2,1)S(1)} %collective-permute-done.1.refs_3_.refs_0_), channel_id=1, source_target_pairs={{0,2},{1,5},{2,0},{3,7},{4,6},{5,1},{6,4},{7,3},{8,10},{9,13},{10,... | collective-permute-start | bytes 350216 | tf_op jit(solution)/shard_map/ppermute | solution.py:27
  20.7 2.8 %collective-permute-done.12.refs_1_ = bf16[8,7296]{1,0:T(8,128)(2,1)S(1)} collective-permute-done((bf16[8,7296]{1,0:T(8,128)(2,1)S(1)}, bf16[8,7296]{1,0:T(8,128)(2,1)S(1)}, u32[]{:S(2)}, u32[]{:S(2)}) %collective-permute-start.12) | collective-permute-done | bytes 116768 | tf_op jit(solution)/shard_map/ppermute | solution.py:27
  25.0 2.3 %collective-permute-start.17 = (bf16[16,7296]{1,0:T(8,128)(2,1)S(1)}, bf16[16,7296]{1,0:T(8,128)(2,1)S(1)}, u32[]{:S(2)}, u32[]{:S(2)}) collective-permute-start(bf16[16,7296]{1,0:T(8,128)(2,1)S(1)} %shard_map.68.refs_3_.refs_4_), channel_id=1, source_target_pairs={{0,4},{1,3},{2,6},{3,1},{4,0},{5,7},{6,2},{7,5},{8,12},{9,11},{10,... | collective-permute-start | bytes 700424 | tf_op jit(solution)/shard_map/ppermute | solution.py:27
  27.5 4.3 %shard_map.69 = (bf16[7168,256]{1,0:T(8,128)(2,1)S(1)}, bf16[7168,256]{1,0:T(8,128)(2,1)S(1)}, bf16[256,7168]{1,0:T(8,128)(2,1)S(1)}) custom-call(bf16[7168,256]{1,0:T(8,128)(2,1)} %bitcast.6, bf16[7168,256]{1,0:T(8,128)(2,1)} %bitcast.7, bf16[256,7168]{1,0:T(8,128)(2,1)} %bitcast.8, bf16[16,7296]{1,0:T(8,128)(2,1)S(1)} %shard_map.68.refs_3_.refs_4_), custom_call_target="tpu_custom_call" | custom-call | bytes 14400000 | tf_op jit(solution)/shard_map/pallas_call | solution.py:139
  39.6 2.1 %collective-permute-start.21 = (bf16[16,7168]{1,0:T(8,128)(2,1)S(1)}, bf16[16,7168]{1,0:T(8,128)(2,1)S(1)}, u32[]{:S(2)}, u32[]{:S(2)}) collective-permute-start(bf16[16,7168]{1,0:T(8,128)(2,1)S(1)} %get-tuple-element.53.refs_2_), channel_id=1, source_target_pairs={{0,4},{1,3},{2,6},{3,1},{4,0},{5,7},{6,2},{7,5},{8,12},{9,11},{10,... | collective-permute-start | bytes 688136 | tf_op jit(solution)/shard_map/ppermute | solution.py:27
  42.4 1.6 %collective-permute-start.29 = (bf16[16,7168]{1,0:T(8,128)(2,1)S(1)}, bf16[16,7168]{1,0:T(8,128)(2,1)S(1)}, u32[]{:S(2)}, u32[]{:S(2)}) collective-permute-start(bf16[16,7168]{1,0:T(8,128)(2,1)S(1)} %get-tuple-element.58.refs_2_), channel_id=1, source_target_pairs={{0,4},{1,3},{2,6},{3,1},{4,0},{5,7},{6,2},{7,5},{8,12},{9,11},{10,... | collective-permute-start | bytes 688136 | tf_op jit(solution)/shard_map/ppermute | solution.py:27
  44.0 1.7 %collective-permute-done.21.refs_1_ = bf16[16,7168]{1,0:T(8,128)(2,1)S(1)} collective-permute-done((bf16[16,7168]{1,0:T(8,128)(2,1)S(1)}, bf16[16,7168]{1,0:T(8,128)(2,1)S(1)}, u32[]{:S(2)}, u32[]{:S(2)}) %collective-permute-start.21) | collective-permute-done | bytes 229408 | tf_op jit(solution)/shard_map/ppermute | solution.py:27
  45.7 1.6 %collective-permute-start.27 = (bf16[8,7168]{1,0:T(8,128)(2,1)S(1)}, bf16[8,7168]{1,0:T(8,128)(2,1)S(1)}, u32[]{:S(2)}, u32[]{:S(2)}) collective-permute-start(bf16[8,7168]{1,0:T(8,128)(2,1)S(1)} %get-tuple-element.59.refs_2_), channel_id=1, source_target_pairs={{0,2},{1,5},{2,0},{3,7},{4,6},{5,1},{6,4},{7,3},{8,10},{9,13},{10,... | collective-permute-start | bytes 344072 | tf_op jit(solution)/shard_map/ppermute | solution.py:27
  47.4 2.1 %collective-permute-start.24 = (bf16[16,7168]{1,0:T(8,128)(2,1)S(1)}, bf16[16,7168]{1,0:T(8,128)(2,1)S(1)}, u32[]{:S(2)}, u32[]{:S(2)}) collective-permute-start(bf16[16,7168]{1,0:T(8,128)(2,1)S(1)} %get-tuple-element.61.refs_2_), channel_id=1, source_target_pairs={{0,4},{1,3},{2,6},{3,1},{4,0},{5,7},{6,2},{7,5},{8,12},{9,11},{10,... | collective-permute-start | bytes 688136 | tf_op jit(solution)/shard_map/ppermute | solution.py:27
  50.1 1.8 %collective-permute-done.27.refs_1_ = bf16[8,7168]{1,0:T(8,128)(2,1)S(1)} collective-permute-done((bf16[8,7168]{1,0:T(8,128)(2,1)S(1)}, bf16[8,7168]{1,0:T(8,128)(2,1)S(1)}, u32[]{:S(2)}, u32[]{:S(2)}) %collective-permute-start.27) | collective-permute-done | bytes 114720 | tf_op jit(solution)/shard_map/ppermute | solution.py:27
  52.7 1.9 %collective-permute-start.32 = (bf16[8,7168]{1,0:T(8,128)(2,1)S(1)}, bf16[8,7168]{1,0:T(8,128)(2,1)S(1)}, u32[]{:S(2)}, u32[]{:S(2)}) collective-permute-start(bf16[8,7168]{1,0:T(8,128)(2,1)S(1)} %get-tuple-element.67.refs_3_), channel_id=1, source_target_pairs={{0,2},{1,5},{2,0},{3,7},{4,6},{5,1},{6,4},{7,3},{8,10},{9,13},{10,... | collective-permute-start | bytes 344072 | tf_op jit(solution)/shard_map/ppermute | solution.py:27
  54.7 2.0 %collective-permute-done.28.refs_2_ = bf16[8,7168]{1,0:T(8,128)(2,1)S(1)} collective-permute-done((bf16[8,7168]{1,0:T(8,128)(2,1)S(1)}, bf16[8,7168]{1,0:T(8,128)(2,1)S(1)}, u32[]{:S(2)}, u32[]{:S(2)}) %collective-permute-start.28) | collective-permute-done | bytes 114720 | tf_op jit(solution)/shard_map/ppermute | solution.py:27
  56.8 1.2 %collective-permute-start.31 = (bf16[8,7168]{1,0:T(8,128)(2,1)S(1)}, bf16[8,7168]{1,0:T(8,128)(2,1)S(1)}, u32[]{:S(2)}, u32[]{:S(2)}) collective-permute-start(bf16[8,7168]{1,0:T(8,128)(2,1)S(1)} %shard_map.82.refs_2_), channel_id=1, source_target_pairs={{0,16},{1,17},{2,18},{3,19},{4,20},{5,21},{6,22},{7,23},{8,24},{9,... | collective-permute-start | bytes 344072 | tf_op jit(solution)/shard_map/ppermute | solution.py:27
  58.0 1.6 %collective-permute-start.30 = (bf16[8,7168]{1,0:T(8,128)(2,1)S(1)}, bf16[8,7168]{1,0:T(8,128)(2,1)S(1)}, u32[]{:S(2)}, u32[]{:S(2)}) collective-permute-start(bf16[8,7168]{1,0:T(8,128)(2,1)S(1)} %get-tuple-element.69.refs_2_), channel_id=1, source_target_pairs={{0,2},{1,5},{2,0},{3,7},{4,6},{5,1},{6,4},{7,3},{8,10},{9,13},{10,... | collective-permute-start | bytes 344072 | tf_op jit(solution)/shard_map/ppermute | solution.py:27
  59.6 2.1 %collective-permute-start.33 = (bf16[8,7168]{1,0:T(8,128)(2,1)S(1)}, bf16[8,7168]{1,0:T(8,128)(2,1)S(1)}, u32[]{:S(2)}, u32[]{:S(2)}) collective-permute-start(bf16[8,7168]{1,0:T(8,128)(2,1)S(1)} %shard_map.84.refs_4_), channel_id=1, source_target_pairs={{0,8},{1,9},{2,10},{3,11},{4,12},{5,13},{6,14},{7,15},{8,0},{9,1},... | collective-permute-start | bytes 344072 | tf_op jit(solution)/shard_map/ppermute | solution.py:27
  61.7 1.2 %collective-permute-done.30.refs_1_ = bf16[8,7168]{1,0:T(8,128)(2,1)S(1)} collective-permute-done((bf16[8,7168]{1,0:T(8,128)(2,1)S(1)}, bf16[8,7168]{1,0:T(8,128)(2,1)S(1)}, u32[]{:S(2)}, u32[]{:S(2)}) %collective-permute-start.30) | collective-permute-done | bytes 114720 | tf_op jit(solution)/shard_map/ppermute | solution.py:27
  (67 shorter events, 16.8 us)
Async XLA Ops:
  1.1 7.5 %collective-permute-start.5 = (bf16[8,7296]{1,0:T(8,128)(2,1)S(1)}, bf16[8,7296]{1,0:T(8,128)(2,1)S(1)}, u32[]{:S(2)}, u32[]{:S(2)}) collective-permute-start(bf16[8,7296]{1,0:T(8,128)(2,1)S(1)} %shard_map.64.refs_0_.refs_2_), channel_id=1, source_target_pairs={{0,8},{1,9},{2,10},{3,11},{4,12},{5,13},{6,14},{7,15},{8,0},{9,1},... | collective-permute-start | bytes 350216 | tf_op jit(solution)/shard_map/ppermute | solution.py:27
  4.2 8.1 %collective-permute-start.1 = (bf16[8,7296]{1,0:T(8,128)(2,1)S(1)}, bf16[8,7296]{1,0:T(8,128)(2,1)S(1)}, u32[]{:S(2)}, u32[]{:S(2)}) collective-permute-start(bf16[8,7296]{1,0:T(8,128)(2,1)S(1)} %shard_map.64.refs_0_.refs_2_), channel_id=1, source_target_pairs={{0,16},{1,17},{2,18},{3,19},{4,20},{5,21},{6,22},{7,23},{8,24},{9,... | collective-permute-start | bytes 350216 | tf_op jit(solution)/shard_map/ppermute | solution.py:27
  6.7 6.0 %collective-permute-start = (bf16[8,7296]{1,0:T(8,128)(2,1)S(1)}, bf16[8,7296]{1,0:T(8,128)(2,1)S(1)}, u32[]{:S(2)}, u32[]{:S(2)}) collective-permute-start(bf16[8,7296]{1,0:T(8,128)(2,1)S(1)} %shard_map.64.refs_0_.refs_2_), channel_id=1, source_target_pairs={{0,2},{1,5},{2,0},{3,7},{4,6},{5,1},{6,4},{7,3},{8,10},{9,13},{10,... | collective-permute-start | bytes 350216 | tf_op jit(solution)/shard_map/ppermute | solution.py:27
  8.6 5.8 %collective-permute-start.6 = (bf16[8,7296]{1,0:T(8,128)(2,1)S(1)}, bf16[8,7296]{1,0:T(8,128)(2,1)S(1)}, u32[]{:S(2)}, u32[]{:S(2)}) collective-permute-start(bf16[8,7296]{1,0:T(8,128)(2,1)S(1)} %collective-permute-done.5.refs_0_), channel_id=1, source_target_pairs={{0,2},{1,5},{2,0},{3,7},{4,6},{5,1},{6,4},{7,3},{8,10},{9,13},{10,... | collective-permute-start | bytes 350216 | tf_op jit(solution)/shard_map/ppermute | solution.py:27
  12.7 11.7 %collective-permute-start.2 = (bf16[16,7296]{1,0:T(8,128)(2,1)S(1)}, bf16[16,7296]{1,0:T(8,128)(2,1)S(1)}, u32[]{:S(2)}, u32[]{:S(2)}) collective-permute-start(bf16[16,7296]{1,0:T(8,128)(2,1)S(1)} %shard_map.65.refs_2_.refs_0_), channel_id=1, source_target_pairs={{0,4},{1,3},{2,6},{3,1},{4,0},{5,7},{6,2},{7,5},{8,12},{9,11},{10,... | collective-permute-start | bytes 700424 | tf_op jit(solution)/shard_map/ppermute | solution.py:27
  17.1 7.6 %collective-permute-start.8 = (bf16[16,7296]{1,0:T(8,128)(2,1)S(1)}, bf16[16,7296]{1,0:T(8,128)(2,1)S(1)}, u32[]{:S(2)}, u32[]{:S(2)}) collective-permute-start(bf16[16,7296]{1,0:T(8,128)(2,1)S(1)} %shard_map.66.refs_2_.refs_4_), channel_id=1, source_target_pairs={{0,4},{1,3},{2,6},{3,1},{4,0},{5,7},{6,2},{7,5},{8,12},{9,11},{10,... | collective-permute-start | bytes 700424 | tf_op jit(solution)/shard_map/ppermute | solution.py:27
  18.7 8.7 %collective-permute-start.3 = (bf16[16,7296]{1,0:T(8,128)(2,1)S(1)}, bf16[16,7296]{1,0:T(8,128)(2,1)S(1)}, u32[]{:S(2)}, u32[]{:S(2)}) collective-permute-start(bf16[16,7296]{1,0:T(8,128)(2,1)S(1)} %shard_map.65.refs_2_.refs_0_), channel_id=1, source_target_pairs={{0,1},{1,0},{2,3},{3,2},{4,5},{5,4},{6,7},{7,6},{8,9},{9,8},{10,11... | collective-permute-start | bytes 700424 | tf_op jit(solution)/shard_map/ppermute | solution.py:27
  23.5 8.3 %collective-permute-start.9 = (bf16[16,7296]{1,0:T(8,128)(2,1)S(1)}, bf16[16,7296]{1,0:T(8,128)(2,1)S(1)}, u32[]{:S(2)}, u32[]{:S(2)}) collective-permute-start(bf16[16,7296]{1,0:T(8,128)(2,1)S(1)} %shard_map.66.refs_2_.refs_4_), channel_id=1, source_target_pairs={{0,1},{1,0},{2,3},{3,2},{4,5},{5,4},{6,7},{7,6},{8,9},{9,8},{10,11... | collective-permute-start | bytes 700424 | tf_op jit(solution)/shard_map/ppermute | solution.py:27
  24.4 7.5 %collective-permute-start.4 = (bf16[16,7296]{1,0:T(8,128)(2,1)S(1)}, bf16[16,7296]{1,0:T(8,128)(2,1)S(1)}, u32[]{:S(2)}, u32[]{:S(2)}) collective-permute-start(bf16[16,7296]{1,0:T(8,128)(2,1)S(1)} %collective-permute-done.2.refs_1_), channel_id=1, source_target_pairs={{0,1},{1,0},{2,3},{3,2},{4,5},{5,4},{6,7},{7,6},{8,9},{9,8},{10,11... | collective-permute-start | bytes 700424 | tf_op jit(solution)/shard_map/ppermute | solution.py:27
  24.7 7.7 %collective-permute-start.10 = (bf16[16,7296]{1,0:T(8,128)(2,1)S(1)}, bf16[16,7296]{1,0:T(8,128)(2,1)S(1)}, u32[]{:S(2)}, u32[]{:S(2)}) collective-permute-start(bf16[16,7296]{1,0:T(8,128)(2,1)S(1)} %collective-permute-done.8.refs_5_), channel_id=1, source_target_pairs={{0,1},{1,0},{2,3},{3,2},{4,5},{5,4},{6,7},{7,6},{8,9},{9,8},{10,11... | collective-permute-start | bytes 700424 | tf_op jit(solution)/shard_map/ppermute | solution.py:27
  25.0 8.5 %collective-permute-start.17 = (bf16[16,7296]{1,0:T(8,128)(2,1)S(1)}, bf16[16,7296]{1,0:T(8,128)(2,1)S(1)}, u32[]{:S(2)}, u32[]{:S(2)}) collective-permute-start(bf16[16,7296]{1,0:T(8,128)(2,1)S(1)} %shard_map.68.refs_3_.refs_4_), channel_id=1, source_target_pairs={{0,4},{1,3},{2,6},{3,1},{4,0},{5,7},{6,2},{7,5},{8,12},{9,11},{10,... | collective-permute-start | bytes 700424 | tf_op jit(solution)/shard_map/ppermute | solution.py:27
  27.4 6.5 %collective-permute-start.14 = (bf16[16,7296]{1,0:T(8,128)(2,1)S(1)}, bf16[16,7296]{1,0:T(8,128)(2,1)S(1)}, u32[]{:S(2)}, u32[]{:S(2)}) collective-permute-start(bf16[16,7296]{1,0:T(8,128)(2,1)S(1)} %shard_map.67.refs_2_.refs_0_), channel_id=1, source_target_pairs={{0,4},{1,3},{2,6},{3,1},{4,0},{5,7},{6,2},{7,5},{8,12},{9,11},{10,... | collective-permute-start | bytes 700424 | tf_op jit(solution)/shard_map/ppermute | solution.py:27
  38.4 8.9 %collective-permute-start.13 = (bf16[32,7168]{1,0:T(8,128)(2,1)S(1)}, bf16[32,7168]{1,0:T(8,128)(2,1)S(1)}, u32[]{:S(2)}, u32[]{:S(2)}) collective-permute-start(bf16[32,7168]{1,0:T(8,128)(2,1)S(1)} %get-tuple-element.44), channel_id=1, source_target_pairs={{0,1},{1,0},{2,3},{3,2},{4,5},{5,4},{6,7},{7,6},{8,9},{9,8},{10,11... | collective-permute-start | bytes 1376264 | tf_op jit(solution)/shard_map/ppermute | solution.py:27
  39.6 6.1 %collective-permute-start.21 = (bf16[16,7168]{1,0:T(8,128)(2,1)S(1)}, bf16[16,7168]{1,0:T(8,128)(2,1)S(1)}, u32[]{:S(2)}, u32[]{:S(2)}) collective-permute-start(bf16[16,7168]{1,0:T(8,128)(2,1)S(1)} %get-tuple-element.53.refs_2_), channel_id=1, source_target_pairs={{0,4},{1,3},{2,6},{3,1},{4,0},{5,7},{6,2},{7,5},{8,12},{9,11},{10,... | collective-permute-start | bytes 688136 | tf_op jit(solution)/shard_map/ppermute | solution.py:27
  41.8 7.7 %collective-permute-start.25 = (bf16[16,7168]{1,0:T(8,128)(2,1)S(1)}, bf16[16,7168]{1,0:T(8,128)(2,1)S(1)}, u32[]{:S(2)}, u32[]{:S(2)}) collective-permute-start(bf16[16,7168]{1,0:T(8,128)(2,1)S(1)} %get-tuple-element.57.refs_2_), channel_id=1, source_target_pairs={{0,4},{1,3},{2,6},{3,1},{4,0},{5,7},{6,2},{7,5},{8,12},{9,11},{10,... | collective-permute-start | bytes 688136 | tf_op jit(solution)/shard_map/ppermute | solution.py:27
  42.4 10.2 %collective-permute-start.29 = (bf16[16,7168]{1,0:T(8,128)(2,1)S(1)}, bf16[16,7168]{1,0:T(8,128)(2,1)S(1)}, u32[]{:S(2)}, u32[]{:S(2)}) collective-permute-start(bf16[16,7168]{1,0:T(8,128)(2,1)S(1)} %get-tuple-element.58.refs_2_), channel_id=1, source_target_pairs={{0,4},{1,3},{2,6},{3,1},{4,0},{5,7},{6,2},{7,5},{8,12},{9,11},{10,... | collective-permute-start | bytes 688136 | tf_op jit(solution)/shard_map/ppermute | solution.py:27
  45.7 6.1 %collective-permute-start.27 = (bf16[8,7168]{1,0:T(8,128)(2,1)S(1)}, bf16[8,7168]{1,0:T(8,128)(2,1)S(1)}, u32[]{:S(2)}, u32[]{:S(2)}) collective-permute-start(bf16[8,7168]{1,0:T(8,128)(2,1)S(1)} %get-tuple-element.59.refs_2_), channel_id=1, source_target_pairs={{0,2},{1,5},{2,0},{3,7},{4,6},{5,1},{6,4},{7,3},{8,10},{9,13},{10,... | collective-permute-start | bytes 344072 | tf_op jit(solution)/shard_map/ppermute | solution.py:27
  47.4 10.6 %collective-permute-start.24 = (bf16[16,7168]{1,0:T(8,128)(2,1)S(1)}, bf16[16,7168]{1,0:T(8,128)(2,1)S(1)}, u32[]{:S(2)}, u32[]{:S(2)}) collective-permute-start(bf16[16,7168]{1,0:T(8,128)(2,1)S(1)} %get-tuple-element.61.refs_2_), channel_id=1, source_target_pairs={{0,4},{1,3},{2,6},{3,1},{4,0},{5,7},{6,2},{7,5},{8,12},{9,11},{10,... | collective-permute-start | bytes 688136 | tf_op jit(solution)/shard_map/ppermute | solution.py:27
  49.5 5.2 %collective-permute-start.26 = (bf16[8,7168]{1,0:T(8,128)(2,1)S(1)}, bf16[8,7168]{1,0:T(8,128)(2,1)S(1)}, u32[]{:S(2)}, u32[]{:S(2)}) collective-permute-start(bf16[8,7168]{1,0:T(8,128)(2,1)S(1)} %get-tuple-element.64.refs_2_), channel_id=1, source_target_pairs={{0,2},{1,5},{2,0},{3,7},{4,6},{5,1},{6,4},{7,3},{8,10},{9,13},{10,... | collective-permute-start | bytes 344072 | tf_op jit(solution)/shard_map/ppermute | solution.py:27
  51.9 4.9 %collective-permute-start.28 = (bf16[8,7168]{1,0:T(8,128)(2,1)S(1)}, bf16[8,7168]{1,0:T(8,128)(2,1)S(1)}, u32[]{:S(2)}, u32[]{:S(2)}) collective-permute-start(bf16[8,7168]{1,0:T(8,128)(2,1)S(1)} %shard_map.80.refs_2_), channel_id=1, source_target_pairs={{0,8},{1,9},{2,10},{3,11},{4,12},{5,13},{6,14},{7,15},{8,0},{9,1},... | collective-permute-start | bytes 344072 | tf_op jit(solution)/shard_map/ppermute | solution.py:27
  52.7 6.9 %collective-permute-start.32 = (bf16[8,7168]{1,0:T(8,128)(2,1)S(1)}, bf16[8,7168]{1,0:T(8,128)(2,1)S(1)}, u32[]{:S(2)}, u32[]{:S(2)}) collective-permute-start(bf16[8,7168]{1,0:T(8,128)(2,1)S(1)} %get-tuple-element.67.refs_3_), channel_id=1, source_target_pairs={{0,2},{1,5},{2,0},{3,7},{4,6},{5,1},{6,4},{7,3},{8,10},{9,13},{10,... | collective-permute-start | bytes 344072 | tf_op jit(solution)/shard_map/ppermute | solution.py:27
  56.8 6.9 %collective-permute-start.31 = (bf16[8,7168]{1,0:T(8,128)(2,1)S(1)}, bf16[8,7168]{1,0:T(8,128)(2,1)S(1)}, u32[]{:S(2)}, u32[]{:S(2)}) collective-permute-start(bf16[8,7168]{1,0:T(8,128)(2,1)S(1)} %shard_map.82.refs_2_), channel_id=1, source_target_pairs={{0,16},{1,17},{2,18},{3,19},{4,20},{5,21},{6,22},{7,23},{8,24},{9,... | collective-permute-start | bytes 344072 | tf_op jit(solution)/shard_map/ppermute | solution.py:27
  58.0 4.9 %collective-permute-start.30 = (bf16[8,7168]{1,0:T(8,128)(2,1)S(1)}, bf16[8,7168]{1,0:T(8,128)(2,1)S(1)}, u32[]{:S(2)}, u32[]{:S(2)}) collective-permute-start(bf16[8,7168]{1,0:T(8,128)(2,1)S(1)} %get-tuple-element.69.refs_2_), channel_id=1, source_target_pairs={{0,2},{1,5},{2,0},{3,7},{4,6},{5,1},{6,4},{7,3},{8,10},{9,13},{10,... | collective-permute-start | bytes 344072 | tf_op jit(solution)/shard_map/ppermute | solution.py:27
  59.6 5.1 %collective-permute-start.33 = (bf16[8,7168]{1,0:T(8,128)(2,1)S(1)}, bf16[8,7168]{1,0:T(8,128)(2,1)S(1)}, u32[]{:S(2)}, u32[]{:S(2)}) collective-permute-start(bf16[8,7168]{1,0:T(8,128)(2,1)S(1)} %shard_map.84.refs_4_), channel_id=1, source_target_pairs={{0,8},{1,9},{2,10},{3,11},{4,12},{5,13},{6,14},{7,15},{8,0},{9,1},... | collective-permute-start | bytes 344072 | tf_op jit(solution)/shard_map/ppermute | solution.py:27
  (10 other events, 34.1 us)

commit v5 on v4

--- a/solution.py
+++ b/solution.py
@@ -150,16 +150,19 @@
 def plan(experts):
     near, far = range(experts // 2), range(experts // 2, experts)
     steps = [("fetch", e) for e in sorted(range(1, experts), key=lambda e: (bin(e).count("1"), -e))]
-    steps += [("behind", far[0]), ("stack", 0), ("behind", far[-1])] + [("stack", e) for e in range(1, experts)]
+    steps += [("behind", far[0])] + [("stack", e) for e in near]
+    steps += [("behind", far[-1]), ("after", 0)] + [("stack", e) for e in far[:-1]]
+    steps += [("behind", 1), ("stack", far[-1])]
     steps += [("load",)]
     steps += [("gate", (e, e + 1)) for e in near[::2]]
-    steps += [("hold", e, (near[-2], near[-1])) for e in far]
+    steps += [("hold", far[-1], (near[-2], near[-1]))]
     steps += [("down", (e, e + 1)) for e in near[::2]]
     steps += [("gate", (e, e + 1)) for e in far[::2]]
     steps += [("down", (e, e + 1)) for e in far[::2][::-1]]
     back = range(experts)[::-1]
-    for slot in range(experts + 3):
-        for step, lag in (("add1", 0), ("add2", 2), ("close", 3)):
+    steps += [("add1", e) for e in back]
+    for slot in range(experts + 1):
+        for step, lag in (("add2", 0), ("close", 1)):
             if 0 <= slot - lag < experts:
                 steps.append((step, back[slot - lag]))
     return steps
@@ -192,7 +195,7 @@
     weights = [gate_weight[0], up_weight[0], down_weight[0]]
     height = SPLIT * rows
     blocks, pairs, fars, nears = {0: payload}, {}, {}, {}
-    hidden_of, state, home = {}, {}, {e: [] for e in range(experts)}
+    hidden_of, state, home = {}, {}, []
     last = (payload,)
     for step, *at in plan(experts):
         e = at[0] if at else None
@@ -201,6 +204,9 @@
             continue
         if step == "behind":
             last = (*last, blocks[e])
+            continue
+        if step == "after":
+            last = (*last, fars[e])
             continue
         if step == "hold":
             fars[e], _ = lax.optimization_barrier((fars[e], hidden_of[at[1]][0]))
@@ -219,7 +225,7 @@
                 in_specs=[pl.BlockSpec(memory_space=pltpu.SMEM)] + [VMEM] * (len(xs) + 2) + [ANY] * len(last),
                 out_specs=[VMEM, VMEM],
                 compiler_params=pltpu.CompilerParams(vmem_limit_bytes=8 * MIB),
-                cost_estimate=cost(0),
+                cost_estimate=cost(2),
             )(mine, *xs, weights[0], weights[1], *last)
             hidden_of[e] = (out, scale)
         elif step == "down":
@@ -240,10 +246,10 @@
             )
             state[e] = (kept, (second if step == "add1" else first)(out))
         else:
-            (out,) = call(close_kernel, [shape(rows, features, BF16)], [*state[e], *home[e]], last)
+            (out,) = call(close_kernel, [shape(rows, features, BF16)], [*state[e], *(home if e == 0 else [])], last)
             if not e:
                 return out
-            home[e & (e - 1)].append(outer[e](out))
+            home.append(swap(members, lambda d: e * SPLIT)(out))
         last = (out,)
 
 

time: 65.6 us -> 63.2 us (0.963)
  waiting for transfers between devices: 18.7 us -> 17.1 us
  starting transfers between devices: 36.1 us -> 35.3 us
    ppermute x34, waiting for transfers between devices: 18.7 us -> 17.1 us  [swap(): return lambda x: lax.ppermute(x, 'local', pairs)]
    ppermute x34, starting transfers between devices: 36.1 us -> 35.3 us  [swap(): return lambda x: lax.ppermute(x, 'local', pairs)]
  transfers between devices with their start and end apart: 34 -> 34, of which waited for: 17 -> 15; matrix products, arithmetic and copies ran while one was open for 0% -> 0% of each run, Pallas kernels for 10% -> 11%
where the time goes in v5:
time: 63.2 us; the launch traced here: 63.1 us
  starting transfers between devices  35.3 us (56%)
  waiting for transfers between devices  17.1 us (27%)
  Pallas kernels  9.82 us (16%)
  local copies, waits for them, and re-layouts  0.65 us (1%)
    ppermute x34, starting transfers between devices, swap(): return lambda x: lax.ppermute(x, 'local', pairs)  35.3 us
    ppermute x34, waiting for transfers between devices, swap(): return lambda x: lax.ppermute(x, 'local', pairs)  17.1 us
    pallas_call x1, Pallas kernels, load(): pl.pallas_call(run, out_shape=[pltpu.VMEM(a.shape, a.dtype) for a in arra...  4.32 us
    pallas_call x2, Pallas kernels, body(): pl.pallas_call(functools.partial(gate_kernel, len(xs), experts), out_shap...  2.35 us
    pallas_call x18, Pallas kernels, call(): pl.pallas_call(run, out_shape=[pltpu.VMEM(o.shape, o.dtype) for o in outs...  2.09 us
  transfers between devices with their start and end apart: 34, of which 15 were waited for; matrix products, arithmetic and copies ran while one was open for 0% of the time, Pallas kernels for 11%

profile of v5, /device:TPU:0, one launch (start us, length us, event | category | flops | bytes accessed | tf_op | source)
XLA Modules:
  0.0 63.1 jit_solution(6507059242980390703)
XLA Ops:
  1.1 3.1 %collective-permute-start.5 = (bf16[8,7296]{1,0:T(8,128)(2,1)S(1)}, bf16[8,7296]{1,0:T(8,128)(2,1)S(1)}, u32[]{:S(2)}, u32[]{:S(2)}) collective-permute-start(bf16[8,7296]{1,0:T(8,128)(2,1)S(1)} %shard_map.64.refs_0_.refs_2_), channel_id=1, source_target_pairs={{0,8},{1,9},{2,10},{3,11},{4,12},{5,13},{6,14},{7,15},{8,0},{9,1},... | collective-permute-start | bytes 350216 | tf_op jit(solution)/shard_map/ppermute | solution.py:27
  4.2 2.6 %collective-permute-start.1 = (bf16[8,7296]{1,0:T(8,128)(2,1)S(1)}, bf16[8,7296]{1,0:T(8,128)(2,1)S(1)}, u32[]{:S(2)}, u32[]{:S(2)}) collective-permute-start(bf16[8,7296]{1,0:T(8,128)(2,1)S(1)} %shard_map.64.refs_0_.refs_2_), channel_id=1, source_target_pairs={{0,16},{1,17},{2,18},{3,19},{4,20},{5,21},{6,22},{7,23},{8,24},{9,... | collective-permute-start | bytes 350216 | tf_op jit(solution)/shard_map/ppermute | solution.py:27
  6.7 1.5 %collective-permute-start = (bf16[8,7296]{1,0:T(8,128)(2,1)S(1)}, bf16[8,7296]{1,0:T(8,128)(2,1)S(1)}, u32[]{:S(2)}, u32[]{:S(2)}) collective-permute-start(bf16[8,7296]{1,0:T(8,128)(2,1)S(1)} %shard_map.64.refs_0_.refs_2_), channel_id=1, source_target_pairs={{0,2},{1,5},{2,0},{3,7},{4,6},{5,1},{6,4},{7,3},{8,10},{9,13},{10,... | collective-permute-start | bytes 350216 | tf_op jit(solution)/shard_map/ppermute | solution.py:27
  8.6 1.8 %collective-permute-start.6 = (bf16[8,7296]{1,0:T(8,128)(2,1)S(1)}, bf16[8,7296]{1,0:T(8,128)(2,1)S(1)}, u32[]{:S(2)}, u32[]{:S(2)}) collective-permute-start(bf16[8,7296]{1,0:T(8,128)(2,1)S(1)} %collective-permute-done.5.refs_0_.refs_3_), channel_id=1, source_target_pairs={{0,2},{1,5},{2,0},{3,7},{4,6},{5,1},{6,4},{7,3},{8,10},{9,13},{10,... | collective-permute-start | bytes 350216 | tf_op jit(solution)/shard_map/ppermute | solution.py:27
  10.4 1.9 %collective-permute-done.1.refs_3_.refs_0_ = bf16[8,7296]{1,0:T(8,128)(2,1)S(1)} collective-permute-done((bf16[8,7296]{1,0:T(8,128)(2,1)S(1)}, bf16[8,7296]{1,0:T(8,128)(2,1)S(1)}, u32[]{:S(2)}, u32[]{:S(2)}) %collective-permute-start.1) | collective-permute-done | bytes 116768 | tf_op jit(solution)/shard_map/ppermute | solution.py:27
  12.3 1.6 %collective-permute-start.2 = (bf16[16,7296]{1,0:T(8,128)(2,1)S(1)}, bf16[16,7296]{1,0:T(8,128)(2,1)S(1)}, u32[]{:S(2)}, u32[]{:S(2)}) collective-permute-start(bf16[16,7296]{1,0:T(8,128)(2,1)S(1)} %shard_map.65.refs_2_.refs_0_), channel_id=1, source_target_pairs={{0,4},{1,3},{2,6},{3,1},{4,0},{5,7},{6,2},{7,5},{8,12},{9,11},{10,... | collective-permute-start | bytes 700424 | tf_op jit(solution)/shard_map/ppermute | solution.py:27
  14.4 2.0 %collective-permute-start.7 = (bf16[16,7296]{1,0:T(8,128)(2,1)S(1)}, bf16[16,7296]{1,0:T(8,128)(2,1)S(1)}, u32[]{:S(2)}, u32[]{:S(2)}) collective-permute-start(bf16[16,7296]{1,0:T(8,128)(2,1)S(1)} %shard_map.66.refs_2_.refs_4_), channel_id=1, source_target_pairs={{0,4},{1,3},{2,6},{3,1},{4,0},{5,7},{6,2},{7,5},{8,12},{9,11},{10,... | collective-permute-start | bytes 700424 | tf_op jit(solution)/shard_map/ppermute | solution.py:27
  16.4 1.5 %collective-permute-start.12 = (bf16[8,7296]{1,0:T(8,128)(2,1)S(1)}, bf16[8,7296]{1,0:T(8,128)(2,1)S(1)}, u32[]{:S(2)}, u32[]{:S(2)}) collective-permute-start(bf16[8,7296]{1,0:T(8,128)(2,1)S(1)} %collective-permute-done.1.refs_3_.refs_0_), channel_id=1, source_target_pairs={{0,2},{1,5},{2,0},{3,7},{4,6},{5,1},{6,4},{7,3},{8,10},{9,13},{10,... | collective-permute-start | bytes 350216 | tf_op jit(solution)/shard_map/ppermute | solution.py:27
  18.7 1.5 %collective-permute-start.11 = (bf16[8,7296]{1,0:T(8,128)(2,1)S(1)}, bf16[8,7296]{1,0:T(8,128)(2,1)S(1)}, u32[]{:S(2)}, u32[]{:S(2)}) collective-permute-start(bf16[8,7296]{1,0:T(8,128)(2,1)S(1)} %collective-permute-done.10.refs_3_.refs_0_), channel_id=1, source_target_pairs={{0,2},{1,5},{2,0},{3,7},{4,6},{5,1},{6,4},{7,3},{8,10},{9,13},{10,... | collective-permute-start | bytes 350216 | tf_op jit(solution)/shard_map/ppermute | solution.py:27
  25.1 4.3 %shard_map.69 = (bf16[7168,256]{1,0:T(8,128)(2,1)S(1)}, bf16[7168,256]{1,0:T(8,128)(2,1)S(1)}, bf16[256,7168]{1,0:T(8,128)(2,1)S(1)}) custom-call(bf16[7168,256]{1,0:T(8,128)(2,1)} %bitcast.6, bf16[7168,256]{1,0:T(8,128)(2,1)} %bitcast.7, bf16[256,7168]{1,0:T(8,128)(2,1)} %bitcast.8, bf16[16,7296]{1,0:T(8,128)(2,1)S(1)} %shard_map.68.refs_3_.refs_4_), custom_call_target="tpu_custom_call" | custom-call | bytes 14400000 | tf_op jit(solution)/shard_map/pallas_call | solution.py:139
  30.3 1.2 %shard_map.70 = (bf16[128,256]{1,0:T(8,128)(2,1)S(1)}, f32[128,128]{1,0:T(8,128)S(1)}) custom-call(s32[1]{0:T(128)} %bitcast.mine_ref, bf16[16,7296]{1,0:T(8,128)(2,1)S(1)} %shard_map.65.refs_2_.refs_0_, bf16[16,7296]{1,0:T(8,128)(2,1)S(1)} %collective-permute-done.2.refs_4_.refs_1_, bf16[16,7296]{1,0:T(8,128)(2,1)S(1)} %collective-permute-done.3.refs_2_, ...), custom_call_target="tpu_custom_call" | custom-call | bytes 7200000 | tf_op jit(solution)/shard_map/pallas_call | solution.py:222
  33.1 1.2 %shard_map.72 = (bf16[128,256]{1,0:T(8,128)(2,1)S(1)}, f32[128,128]{1,0:T(8,128)S(1)}) custom-call(s32[1]{0:T(128)} %bitcast.mine_ref, bf16[16,7296]{1,0:T(8,128)(2,1)S(1)} %shard_map.67.refs_2_.refs_0_, bf16[16,7296]{1,0:T(8,128)(2,1)S(1)} %collective-permute-done.15.refs_1_, bf16[16,7296]{1,0:T(8,128)(2,1)S(1)} %collective-permute-done.16.refs_2_, ...), custom_call_target="tpu_custom_call" | custom-call | bytes 7200000 | tf_op jit(solution)/shard_map/pallas_call | solution.py:222
  36.9 1.5 %collective-permute-start.25 = (bf16[16,7168]{1,0:T(8,128)(2,1)S(1)}, bf16[16,7168]{1,0:T(8,128)(2,1)S(1)}, u32[]{:S(2)}, u32[]{:S(2)}) collective-permute-start(bf16[16,7168]{1,0:T(8,128)(2,1)S(1)} %get-tuple-element.53.refs_2_), channel_id=1, source_target_pairs={{0,4},{1,3},{2,6},{3,1},{4,0},{5,7},{6,2},{7,5},{8,12},{9,11},{10,... | collective-permute-start | bytes 688136 | tf_op jit(solution)/shard_map/ppermute | solution.py:27
  39.2 1.5 %collective-permute-start.27 = (bf16[16,7168]{1,0:T(8,128)(2,1)S(1)}, bf16[16,7168]{1,0:T(8,128)(2,1)S(1)}, u32[]{:S(2)}, u32[]{:S(2)}) collective-permute-start(bf16[16,7168]{1,0:T(8,128)(2,1)S(1)} %get-tuple-element.55.refs_2_), channel_id=1, source_target_pairs={{0,4},{1,3},{2,6},{3,1},{4,0},{5,7},{6,2},{7,5},{8,12},{9,11},{10,... | collective-permute-start | bytes 688136 | tf_op jit(solution)/shard_map/ppermute | solution.py:27
  40.8 2.2 %collective-permute-done.25.refs_1_ = bf16[16,7168]{1,0:T(8,128)(2,1)S(1)} collective-permute-done((bf16[16,7168]{1,0:T(8,128)(2,1)S(1)}, bf16[16,7168]{1,0:T(8,128)(2,1)S(1)}, u32[]{:S(2)}, u32[]{:S(2)}) %collective-permute-start.25) | collective-permute-done | bytes 229408 | tf_op jit(solution)/shard_map/ppermute | solution.py:27
  43.0 1.4 %collective-permute-start.28 = (bf16[8,7168]{1,0:T(8,128)(2,1)S(1)}, bf16[8,7168]{1,0:T(8,128)(2,1)S(1)}, u32[]{:S(2)}, u32[]{:S(2)}) collective-permute-start(bf16[8,7168]{1,0:T(8,128)(2,1)S(1)} %get-tuple-element.60.refs_2_), channel_id=1, source_target_pairs={{0,2},{1,5},{2,0},{3,7},{4,6},{5,1},{6,4},{7,3},{8,10},{9,13},{10,... | collective-permute-start | bytes 344072 | tf_op jit(solution)/shard_map/ppermute | solution.py:27
  45.8 1.2 %collective-permute-start.26 = (bf16[8,7168]{1,0:T(8,128)(2,1)S(1)}, bf16[8,7168]{1,0:T(8,128)(2,1)S(1)}, u32[]{:S(2)}, u32[]{:S(2)}) collective-permute-start(bf16[8,7168]{1,0:T(8,128)(2,1)S(1)} %get-tuple-element.62.refs_2_), channel_id=1, source_target_pairs={{0,2},{1,5},{2,0},{3,7},{4,6},{5,1},{6,4},{7,3},{8,10},{9,13},{10,... | collective-permute-start | bytes 344072 | tf_op jit(solution)/shard_map/ppermute | solution.py:27
  47.1 2.1 %collective-permute-done.28.refs_1_ = bf16[8,7168]{1,0:T(8,128)(2,1)S(1)} collective-permute-done((bf16[8,7168]{1,0:T(8,128)(2,1)S(1)}, bf16[8,7168]{1,0:T(8,128)(2,1)S(1)}, u32[]{:S(2)}, u32[]{:S(2)}) %collective-permute-start.28) | collective-permute-done | bytes 114720 | tf_op jit(solution)/shard_map/ppermute | solution.py:27
  50.4 1.4 %collective-permute-start.32 = (bf16[8,7168]{1,0:T(8,128)(2,1)S(1)}, bf16[8,7168]{1,0:T(8,128)(2,1)S(1)}, u32[]{:S(2)}, u32[]{:S(2)}) collective-permute-start(bf16[8,7168]{1,0:T(8,128)(2,1)S(1)} %get-tuple-element.65.refs_2_), channel_id=1, source_target_pairs={{0,2},{1,5},{2,0},{3,7},{4,6},{5,1},{6,4},{7,3},{8,10},{9,13},{10,... | collective-permute-start | bytes 344072 | tf_op jit(solution)/shard_map/ppermute | solution.py:27
  51.8 3.5 %collective-permute-start.30 = (bf16[8,7168]{1,0:T(8,128)(2,1)S(1)}, bf16[8,7168]{1,0:T(8,128)(2,1)S(1)}, u32[]{:S(2)}, u32[]{:S(2)}) collective-permute-start(bf16[8,7168]{1,0:T(8,128)(2,1)S(1)} %shard_map.80.refs_2_), channel_id=1, source_target_pairs={{0,24},{1,25},{2,26},{3,27},{4,28},{5,29},{6,30},{7,31},{8,16},{9,... | collective-permute-start | bytes 344072 | tf_op jit(solution)/shard_map/ppermute | solution.py:27
  56.1 1.4 %collective-permute-start.33 = (bf16[8,7168]{1,0:T(8,128)(2,1)S(1)}, bf16[8,7168]{1,0:T(8,128)(2,1)S(1)}, u32[]{:S(2)}, u32[]{:S(2)}) collective-permute-start(bf16[8,7168]{1,0:T(8,128)(2,1)S(1)} %shard_map.84.refs_5_), channel_id=1, source_target_pairs={{0,8},{1,9},{2,10},{3,11},{4,12},{5,13},{6,14},{7,15},{8,0},{9,1},... | collective-permute-start | bytes 344072 | tf_op jit(solution)/shard_map/ppermute | solution.py:27
  57.5 1.4 %collective-permute-done.30.refs_2_ = bf16[8,7168]{1,0:T(8,128)(2,1)S(1)} collective-permute-done((bf16[8,7168]{1,0:T(8,128)(2,1)S(1)}, bf16[8,7168]{1,0:T(8,128)(2,1)S(1)}, u32[]{:S(2)}, u32[]{:S(2)}) %collective-permute-start.30) | collective-permute-done | bytes 114720 | tf_op jit(solution)/shard_map/ppermute | solution.py:27
  58.9 1.4 %collective-permute-done.29.refs_1_ = bf16[8,7168]{1,0:T(8,128)(2,1)S(1)} collective-permute-done((bf16[8,7168]{1,0:T(8,128)(2,1)S(1)}, bf16[8,7168]{1,0:T(8,128)(2,1)S(1)}, u32[]{:S(2)}, u32[]{:S(2)}) %collective-permute-start.29) | collective-permute-done | bytes 114720 | tf_op jit(solution)/shard_map/ppermute | solution.py:27
  60.3 1.9 %collective-permute-done.31.refs_3_ = bf16[8,7168]{1,0:T(8,128)(2,1)S(1)} collective-permute-done((bf16[8,7168]{1,0:T(8,128)(2,1)S(1)}, bf16[8,7168]{1,0:T(8,128)(2,1)S(1)}, u32[]{:S(2)}, u32[]{:S(2)}) %collective-permute-start.31) | collective-permute-done | bytes 114720 | tf_op jit(solution)/shard_map/ppermute | solution.py:27
  (67 shorter events, 17.8 us)
Async XLA Ops:
  1.1 7.5 %collective-permute-start.5 = (bf16[8,7296]{1,0:T(8,128)(2,1)S(1)}, bf16[8,7296]{1,0:T(8,128)(2,1)S(1)}, u32[]{:S(2)}, u32[]{:S(2)}) collective-permute-start(bf16[8,7296]{1,0:T(8,128)(2,1)S(1)} %shard_map.64.refs_0_.refs_2_), channel_id=1, source_target_pairs={{0,8},{1,9},{2,10},{3,11},{4,12},{5,13},{6,14},{7,15},{8,0},{9,1},... | collective-permute-start | bytes 350216 | tf_op jit(solution)/shard_map/ppermute | solution.py:27
  4.2 8.1 %collective-permute-start.1 = (bf16[8,7296]{1,0:T(8,128)(2,1)S(1)}, bf16[8,7296]{1,0:T(8,128)(2,1)S(1)}, u32[]{:S(2)}, u32[]{:S(2)}) collective-permute-start(bf16[8,7296]{1,0:T(8,128)(2,1)S(1)} %shard_map.64.refs_0_.refs_2_), channel_id=1, source_target_pairs={{0,16},{1,17},{2,18},{3,19},{4,20},{5,21},{6,22},{7,23},{8,24},{9,... | collective-permute-start | bytes 350216 | tf_op jit(solution)/shard_map/ppermute | solution.py:27
  6.7 5.5 %collective-permute-start = (bf16[8,7296]{1,0:T(8,128)(2,1)S(1)}, bf16[8,7296]{1,0:T(8,128)(2,1)S(1)}, u32[]{:S(2)}, u32[]{:S(2)}) collective-permute-start(bf16[8,7296]{1,0:T(8,128)(2,1)S(1)} %shard_map.64.refs_0_.refs_2_), channel_id=1, source_target_pairs={{0,2},{1,5},{2,0},{3,7},{4,6},{5,1},{6,4},{7,3},{8,10},{9,13},{10,... | collective-permute-start | bytes 350216 | tf_op jit(solution)/shard_map/ppermute | solution.py:27
  8.6 5.8 %collective-permute-start.6 = (bf16[8,7296]{1,0:T(8,128)(2,1)S(1)}, bf16[8,7296]{1,0:T(8,128)(2,1)S(1)}, u32[]{:S(2)}, u32[]{:S(2)}) collective-permute-start(bf16[8,7296]{1,0:T(8,128)(2,1)S(1)} %collective-permute-done.5.refs_0_.refs_3_), channel_id=1, source_target_pairs={{0,2},{1,5},{2,0},{3,7},{4,6},{5,1},{6,4},{7,3},{8,10},{9,13},{10,... | collective-permute-start | bytes 350216 | tf_op jit(solution)/shard_map/ppermute | solution.py:27
  12.3 9.8 %collective-permute-start.2 = (bf16[16,7296]{1,0:T(8,128)(2,1)S(1)}, bf16[16,7296]{1,0:T(8,128)(2,1)S(1)}, u32[]{:S(2)}, u32[]{:S(2)}) collective-permute-start(bf16[16,7296]{1,0:T(8,128)(2,1)S(1)} %shard_map.65.refs_2_.refs_0_), channel_id=1, source_target_pairs={{0,4},{1,3},{2,6},{3,1},{4,0},{5,7},{6,2},{7,5},{8,12},{9,11},{10,... | collective-permute-start | bytes 700424 | tf_op jit(solution)/shard_map/ppermute | solution.py:27
  14.4 9.2 %collective-permute-start.7 = (bf16[16,7296]{1,0:T(8,128)(2,1)S(1)}, bf16[16,7296]{1,0:T(8,128)(2,1)S(1)}, u32[]{:S(2)}, u32[]{:S(2)}) collective-permute-start(bf16[16,7296]{1,0:T(8,128)(2,1)S(1)} %shard_map.66.refs_2_.refs_4_), channel_id=1, source_target_pairs={{0,4},{1,3},{2,6},{3,1},{4,0},{5,7},{6,2},{7,5},{8,12},{9,11},{10,... | collective-permute-start | bytes 700424 | tf_op jit(solution)/shard_map/ppermute | solution.py:27
  16.4 7.7 %collective-permute-start.3 = (bf16[16,7296]{1,0:T(8,128)(2,1)S(1)}, bf16[16,7296]{1,0:T(8,128)(2,1)S(1)}, u32[]{:S(2)}, u32[]{:S(2)}) collective-permute-start(bf16[16,7296]{1,0:T(8,128)(2,1)S(1)} %shard_map.65.refs_2_.refs_0_), channel_id=1, source_target_pairs={{0,1},{1,0},{2,3},{3,2},{4,5},{5,4},{6,7},{7,6},{8,9},{9,8},{10,11... | collective-permute-start | bytes 700424 | tf_op jit(solution)/shard_map/ppermute | solution.py:27
  21.2 8.2 %collective-permute-start.8 = (bf16[16,7296]{1,0:T(8,128)(2,1)S(1)}, bf16[16,7296]{1,0:T(8,128)(2,1)S(1)}, u32[]{:S(2)}, u32[]{:S(2)}) collective-permute-start(bf16[16,7296]{1,0:T(8,128)(2,1)S(1)} %shard_map.66.refs_2_.refs_4_), channel_id=1, source_target_pairs={{0,1},{1,0},{2,3},{3,2},{4,5},{5,4},{6,7},{7,6},{8,9},{9,8},{10,11... | collective-permute-start | bytes 700424 | tf_op jit(solution)/shard_map/ppermute | solution.py:27
  22.2 7.6 %collective-permute-start.15 = (bf16[16,7296]{1,0:T(8,128)(2,1)S(1)}, bf16[16,7296]{1,0:T(8,128)(2,1)S(1)}, u32[]{:S(2)}, u32[]{:S(2)}) collective-permute-start(bf16[16,7296]{1,0:T(8,128)(2,1)S(1)} %shard_map.67.refs_2_.refs_0_), channel_id=1, source_target_pairs={{0,4},{1,3},{2,6},{3,1},{4,0},{5,7},{6,2},{7,5},{8,12},{9,11},{10,... | collective-permute-start | bytes 700424 | tf_op jit(solution)/shard_map/ppermute | solution.py:27
  23.5 6.5 %collective-permute-start.4 = (bf16[16,7296]{1,0:T(8,128)(2,1)S(1)}, bf16[16,7296]{1,0:T(8,128)(2,1)S(1)}, u32[]{:S(2)}, u32[]{:S(2)}) collective-permute-start(bf16[16,7296]{1,0:T(8,128)(2,1)S(1)} %collective-permute-done.2.refs_4_.refs_1_), channel_id=1, source_target_pairs={{0,1},{1,0},{2,3},{3,2},{4,5},{5,4},{6,7},{7,6},{8,9},{9,8},{10,11... | collective-permute-start | bytes 700424 | tf_op jit(solution)/shard_map/ppermute | solution.py:27
  23.6 6.8 %collective-permute-start.9 = (bf16[16,7296]{1,0:T(8,128)(2,1)S(1)}, bf16[16,7296]{1,0:T(8,128)(2,1)S(1)}, u32[]{:S(2)}, u32[]{:S(2)}) collective-permute-start(bf16[16,7296]{1,0:T(8,128)(2,1)S(1)} %collective-permute-done.7.refs_5_), channel_id=1, source_target_pairs={{0,1},{1,0},{2,3},{3,2},{4,5},{5,4},{6,7},{7,6},{8,9},{9,8},{10,11... | collective-permute-start | bytes 700424 | tf_op jit(solution)/shard_map/ppermute | solution.py:27
  24.1 7.4 %collective-permute-start.18 = (bf16[16,7296]{1,0:T(8,128)(2,1)S(1)}, bf16[16,7296]{1,0:T(8,128)(2,1)S(1)}, u32[]{:S(2)}, u32[]{:S(2)}) collective-permute-start(bf16[16,7296]{1,0:T(8,128)(2,1)S(1)} %shard_map.68.refs_3_.refs_4_), channel_id=1, source_target_pairs={{0,4},{1,3},{2,6},{3,1},{4,0},{5,7},{6,2},{7,5},{8,12},{9,11},{10,... | collective-permute-start | bytes 700424 | tf_op jit(solution)/shard_map/ppermute | solution.py:27
  35.7 5.0 %collective-permute-start.13 = (bf16[32,7168]{1,0:T(8,128)(2,1)S(1)}, bf16[32,7168]{1,0:T(8,128)(2,1)S(1)}, u32[]{:S(2)}, u32[]{:S(2)}) collective-permute-start(bf16[32,7168]{1,0:T(8,128)(2,1)S(1)} %get-tuple-element.43), channel_id=1, source_target_pairs={{0,1},{1,0},{2,3},{3,2},{4,5},{5,4},{6,7},{7,6},{8,9},{9,8},{10,11... | collective-permute-start | bytes 1376264 | tf_op jit(solution)/shard_map/ppermute | solution.py:27
  36.9 6.1 %collective-permute-start.25 = (bf16[16,7168]{1,0:T(8,128)(2,1)S(1)}, bf16[16,7168]{1,0:T(8,128)(2,1)S(1)}, u32[]{:S(2)}, u32[]{:S(2)}) collective-permute-start(bf16[16,7168]{1,0:T(8,128)(2,1)S(1)} %get-tuple-element.53.refs_2_), channel_id=1, source_target_pairs={{0,4},{1,3},{2,6},{3,1},{4,0},{5,7},{6,2},{7,5},{8,12},{9,11},{10,... | collective-permute-start | bytes 688136 | tf_op jit(solution)/shard_map/ppermute | solution.py:27
  38.5 7.3 %collective-permute-start.24 = (bf16[16,7168]{1,0:T(8,128)(2,1)S(1)}, bf16[16,7168]{1,0:T(8,128)(2,1)S(1)}, u32[]{:S(2)}, u32[]{:S(2)}) collective-permute-start(bf16[16,7168]{1,0:T(8,128)(2,1)S(1)} %get-tuple-element.54.refs_2_), channel_id=1, source_target_pairs={{0,4},{1,3},{2,6},{3,1},{4,0},{5,7},{6,2},{7,5},{8,12},{9,11},{10,... | collective-permute-start | bytes 688136 | tf_op jit(solution)/shard_map/ppermute | solution.py:27
  39.2 11.1 %collective-permute-start.27 = (bf16[16,7168]{1,0:T(8,128)(2,1)S(1)}, bf16[16,7168]{1,0:T(8,128)(2,1)S(1)}, u32[]{:S(2)}, u32[]{:S(2)}) collective-permute-start(bf16[16,7168]{1,0:T(8,128)(2,1)S(1)} %get-tuple-element.55.refs_2_), channel_id=1, source_target_pairs={{0,4},{1,3},{2,6},{3,1},{4,0},{5,7},{6,2},{7,5},{8,12},{9,11},{10,... | collective-permute-start | bytes 688136 | tf_op jit(solution)/shard_map/ppermute | solution.py:27
  43.0 6.1 %collective-permute-start.28 = (bf16[8,7168]{1,0:T(8,128)(2,1)S(1)}, bf16[8,7168]{1,0:T(8,128)(2,1)S(1)}, u32[]{:S(2)}, u32[]{:S(2)}) collective-permute-start(bf16[8,7168]{1,0:T(8,128)(2,1)S(1)} %get-tuple-element.60.refs_2_), channel_id=1, source_target_pairs={{0,2},{1,5},{2,0},{3,7},{4,6},{5,1},{6,4},{7,3},{8,10},{9,13},{10,... | collective-permute-start | bytes 344072 | tf_op jit(solution)/shard_map/ppermute | solution.py:27
  44.4 11.0 %collective-permute-start.23 = (bf16[16,7168]{1,0:T(8,128)(2,1)S(1)}, bf16[16,7168]{1,0:T(8,128)(2,1)S(1)}, u32[]{:S(2)}, u32[]{:S(2)}) collective-permute-start(bf16[16,7168]{1,0:T(8,128)(2,1)S(1)} %get-tuple-element.57.refs_2_), channel_id=1, source_target_pairs={{0,4},{1,3},{2,6},{3,1},{4,0},{5,7},{6,2},{7,5},{8,12},{9,11},{10,... | collective-permute-start | bytes 688136 | tf_op jit(solution)/shard_map/ppermute | solution.py:27
  45.8 9.4 %collective-permute-start.26 = (bf16[8,7168]{1,0:T(8,128)(2,1)S(1)}, bf16[8,7168]{1,0:T(8,128)(2,1)S(1)}, u32[]{:S(2)}, u32[]{:S(2)}) collective-permute-start(bf16[8,7168]{1,0:T(8,128)(2,1)S(1)} %get-tuple-element.62.refs_2_), channel_id=1, source_target_pairs={{0,2},{1,5},{2,0},{3,7},{4,6},{5,1},{6,4},{7,3},{8,10},{9,13},{10,... | collective-permute-start | bytes 344072 | tf_op jit(solution)/shard_map/ppermute | solution.py:27
  50.4 5.7 %collective-permute-start.32 = (bf16[8,7168]{1,0:T(8,128)(2,1)S(1)}, bf16[8,7168]{1,0:T(8,128)(2,1)S(1)}, u32[]{:S(2)}, u32[]{:S(2)}) collective-permute-start(bf16[8,7168]{1,0:T(8,128)(2,1)S(1)} %get-tuple-element.65.refs_2_), channel_id=1, source_target_pairs={{0,2},{1,5},{2,0},{3,7},{4,6},{5,1},{6,4},{7,3},{8,10},{9,13},{10,... | collective-permute-start | bytes 344072 | tf_op jit(solution)/shard_map/ppermute | solution.py:27
  51.8 7.1 %collective-permute-start.30 = (bf16[8,7168]{1,0:T(8,128)(2,1)S(1)}, bf16[8,7168]{1,0:T(8,128)(2,1)S(1)}, u32[]{:S(2)}, u32[]{:S(2)}) collective-permute-start(bf16[8,7168]{1,0:T(8,128)(2,1)S(1)} %shard_map.80.refs_2_), channel_id=1, source_target_pairs={{0,24},{1,25},{2,26},{3,27},{4,28},{5,29},{6,30},{7,31},{8,16},{9,... | collective-permute-start | bytes 344072 | tf_op jit(solution)/shard_map/ppermute | solution.py:27
  55.3 6.9 %collective-permute-start.31 = (bf16[8,7168]{1,0:T(8,128)(2,1)S(1)}, bf16[8,7168]{1,0:T(8,128)(2,1)S(1)}, u32[]{:S(2)}, u32[]{:S(2)}) collective-permute-start(bf16[8,7168]{1,0:T(8,128)(2,1)S(1)} %shard_map.82.refs_2_), channel_id=1, source_target_pairs={{0,16},{1,17},{2,18},{3,19},{4,20},{5,21},{6,22},{7,23},{8,24},{9,... | collective-permute-start | bytes 344072 | tf_op jit(solution)/shard_map/ppermute | solution.py:27
  55.4 4.9 %collective-permute-start.29 = (bf16[8,7168]{1,0:T(8,128)(2,1)S(1)}, bf16[8,7168]{1,0:T(8,128)(2,1)S(1)}, u32[]{:S(2)}, u32[]{:S(2)}) collective-permute-start(bf16[8,7168]{1,0:T(8,128)(2,1)S(1)} %get-tuple-element.67.refs_2_), channel_id=1, source_target_pairs={{0,2},{1,5},{2,0},{3,7},{4,6},{5,1},{6,4},{7,3},{8,10},{9,13},{10,... | collective-permute-start | bytes 344072 | tf_op jit(solution)/shard_map/ppermute | solution.py:27
  56.1 6.3 %collective-permute-start.33 = (bf16[8,7168]{1,0:T(8,128)(2,1)S(1)}, bf16[8,7168]{1,0:T(8,128)(2,1)S(1)}, u32[]{:S(2)}, u32[]{:S(2)}) collective-permute-start(bf16[8,7168]{1,0:T(8,128)(2,1)S(1)} %shard_map.84.refs_5_), channel_id=1, source_target_pairs={{0,8},{1,9},{2,10},{3,11},{4,12},{5,13},{6,14},{7,15},{8,0},{9,1},... | collective-permute-start | bytes 344072 | tf_op jit(solution)/shard_map/ppermute | solution.py:27
  (10 other events, 32.8 us)

commit v6 on v5

--- a/solution.py
+++ b/solution.py
@@ -56,9 +56,8 @@
     ]
     for copy in copies:
         copy.start()
-    for copy in copies:
+    for copy in copies[:2]:
         copy.wait()
-    out_ref[:, :features] = tokens_ref[...]
     width = out_ref.shape[1] - features
     column = lax.broadcasted_iota(jnp.int32, (rows, width), 1)
     square = (rows, rows)
@@ -73,6 +72,8 @@
     low = coef - high - middle
     terms = jnp.where(column < experts, high, jnp.where(column < 2 * experts, middle, low))
     out_ref[:, features:] = jnp.where(column < 3 * experts, terms, 0.0).astype(BF16)
+    copies[2].wait()
+    out_ref[:, :features] = tokens_ref[...]
 
 
 def stack_kernel(*refs):

time: 63.2 us -> 63.1 us (level)
  no operation moved by 1% of the time
where the time goes in v6:
time: 63.1 us; the launch traced here: 63 us
  starting transfers between devices  35.4 us (56%)
  waiting for transfers between devices  17 us (27%)
  Pallas kernels  9.72 us (15%)
  local copies, waits for them, and re-layouts  0.65 us (1%)
    ppermute x34, starting transfers between devices, swap(): return lambda x: lax.ppermute(x, 'local', pairs)  35.4 us
    ppermute x34, waiting for transfers between devices, swap(): return lambda x: lax.ppermute(x, 'local', pairs)  17 us
    pallas_call x1, Pallas kernels, load(): pl.pallas_call(run, out_shape=[pltpu.VMEM(a.shape, a.dtype) for a in arra...  4.32 us
    pallas_call x2, Pallas kernels, body(): pl.pallas_call(functools.partial(gate_kernel, len(xs), experts), out_shap...  2.35 us
    pallas_call x18, Pallas kernels, call(): pl.pallas_call(run, out_shape=[pltpu.VMEM(o.shape, o.dtype) for o in outs...  2.09 us
  transfers between devices with their start and end apart: 34, of which 15 were waited for; matrix products, arithmetic and copies ran while one was open for 0% of the time, Pallas kernels for 11%

profile of v6, /device:TPU:0, one launch (start us, length us, event | category | flops | bytes accessed | tf_op | source)
XLA Modules:
  0.0 63.0 jit_solution(16688200083744402573)
XLA Ops:
  1.0 3.1 %collective-permute-start.5 = (bf16[8,7296]{1,0:T(8,128)(2,1)S(1)}, bf16[8,7296]{1,0:T(8,128)(2,1)S(1)}, u32[]{:S(2)}, u32[]{:S(2)}) collective-permute-start(bf16[8,7296]{1,0:T(8,128)(2,1)S(1)} %shard_map.64.refs_0_.refs_2_), channel_id=1, source_target_pairs={{0,8},{1,9},{2,10},{3,11},{4,12},{5,13},{6,14},{7,15},{8,0},{9,1},... | collective-permute-start | bytes 350216 | tf_op jit(solution)/shard_map/ppermute | solution.py:27
  4.1 2.6 %collective-permute-start.1 = (bf16[8,7296]{1,0:T(8,128)(2,1)S(1)}, bf16[8,7296]{1,0:T(8,128)(2,1)S(1)}, u32[]{:S(2)}, u32[]{:S(2)}) collective-permute-start(bf16[8,7296]{1,0:T(8,128)(2,1)S(1)} %shard_map.64.refs_0_.refs_2_), channel_id=1, source_target_pairs={{0,16},{1,17},{2,18},{3,19},{4,20},{5,21},{6,22},{7,23},{8,24},{9,... | collective-permute-start | bytes 350216 | tf_op jit(solution)/shard_map/ppermute | solution.py:27
  6.7 1.5 %collective-permute-start = (bf16[8,7296]{1,0:T(8,128)(2,1)S(1)}, bf16[8,7296]{1,0:T(8,128)(2,1)S(1)}, u32[]{:S(2)}, u32[]{:S(2)}) collective-permute-start(bf16[8,7296]{1,0:T(8,128)(2,1)S(1)} %shard_map.64.refs_0_.refs_2_), channel_id=1, source_target_pairs={{0,2},{1,5},{2,0},{3,7},{4,6},{5,1},{6,4},{7,3},{8,10},{9,13},{10,... | collective-permute-start | bytes 350216 | tf_op jit(solution)/shard_map/ppermute | solution.py:27
  8.5 1.8 %collective-permute-start.6 = (bf16[8,7296]{1,0:T(8,128)(2,1)S(1)}, bf16[8,7296]{1,0:T(8,128)(2,1)S(1)}, u32[]{:S(2)}, u32[]{:S(2)}) collective-permute-start(bf16[8,7296]{1,0:T(8,128)(2,1)S(1)} %collective-permute-done.5.refs_0_.refs_3_), channel_id=1, source_target_pairs={{0,2},{1,5},{2,0},{3,7},{4,6},{5,1},{6,4},{7,3},{8,10},{9,13},{10,... | collective-permute-start | bytes 350216 | tf_op jit(solution)/shard_map/ppermute | solution.py:27
  10.3 1.9 %collective-permute-done.1.refs_3_.refs_0_ = bf16[8,7296]{1,0:T(8,128)(2,1)S(1)} collective-permute-done((bf16[8,7296]{1,0:T(8,128)(2,1)S(1)}, bf16[8,7296]{1,0:T(8,128)(2,1)S(1)}, u32[]{:S(2)}, u32[]{:S(2)}) %collective-permute-start.1) | collective-permute-done | bytes 116768 | tf_op jit(solution)/shard_map/ppermute | solution.py:27
  12.2 1.6 %collective-permute-start.2 = (bf16[16,7296]{1,0:T(8,128)(2,1)S(1)}, bf16[16,7296]{1,0:T(8,128)(2,1)S(1)}, u32[]{:S(2)}, u32[]{:S(2)}) collective-permute-start(bf16[16,7296]{1,0:T(8,128)(2,1)S(1)} %shard_map.65.refs_2_.refs_0_), channel_id=1, source_target_pairs={{0,4},{1,3},{2,6},{3,1},{4,0},{5,7},{6,2},{7,5},{8,12},{9,11},{10,... | collective-permute-start | bytes 700424 | tf_op jit(solution)/shard_map/ppermute | solution.py:27
  14.3 2.0 %collective-permute-start.7 = (bf16[16,7296]{1,0:T(8,128)(2,1)S(1)}, bf16[16,7296]{1,0:T(8,128)(2,1)S(1)}, u32[]{:S(2)}, u32[]{:S(2)}) collective-permute-start(bf16[16,7296]{1,0:T(8,128)(2,1)S(1)} %shard_map.66.refs_2_.refs_4_), channel_id=1, source_target_pairs={{0,4},{1,3},{2,6},{3,1},{4,0},{5,7},{6,2},{7,5},{8,12},{9,11},{10,... | collective-permute-start | bytes 700424 | tf_op jit(solution)/shard_map/ppermute | solution.py:27
  16.3 1.5 %collective-permute-start.12 = (bf16[8,7296]{1,0:T(8,128)(2,1)S(1)}, bf16[8,7296]{1,0:T(8,128)(2,1)S(1)}, u32[]{:S(2)}, u32[]{:S(2)}) collective-permute-start(bf16[8,7296]{1,0:T(8,128)(2,1)S(1)} %collective-permute-done.1.refs_3_.refs_0_), channel_id=1, source_target_pairs={{0,2},{1,5},{2,0},{3,7},{4,6},{5,1},{6,4},{7,3},{8,10},{9,13},{10,... | collective-permute-start | bytes 350216 | tf_op jit(solution)/shard_map/ppermute | solution.py:27
  18.6 1.5 %collective-permute-start.11 = (bf16[8,7296]{1,0:T(8,128)(2,1)S(1)}, bf16[8,7296]{1,0:T(8,128)(2,1)S(1)}, u32[]{:S(2)}, u32[]{:S(2)}) collective-permute-start(bf16[8,7296]{1,0:T(8,128)(2,1)S(1)} %collective-permute-done.10.refs_3_.refs_0_), channel_id=1, source_target_pairs={{0,2},{1,5},{2,0},{3,7},{4,6},{5,1},{6,4},{7,3},{8,10},{9,13},{10,... | collective-permute-start | bytes 350216 | tf_op jit(solution)/shard_map/ppermute | solution.py:27
  25.0 4.3 %shard_map.69 = (bf16[7168,256]{1,0:T(8,128)(2,1)S(1)}, bf16[7168,256]{1,0:T(8,128)(2,1)S(1)}, bf16[256,7168]{1,0:T(8,128)(2,1)S(1)}) custom-call(bf16[7168,256]{1,0:T(8,128)(2,1)} %bitcast.6, bf16[7168,256]{1,0:T(8,128)(2,1)} %bitcast.7, bf16[256,7168]{1,0:T(8,128)(2,1)} %bitcast.8, bf16[16,7296]{1,0:T(8,128)(2,1)S(1)} %shard_map.68.refs_3_.refs_4_), custom_call_target="tpu_custom_call" | custom-call | bytes 14400000 | tf_op jit(solution)/shard_map/pallas_call | solution.py:140
  30.2 1.2 %shard_map.70 = (bf16[128,256]{1,0:T(8,128)(2,1)S(1)}, f32[128,128]{1,0:T(8,128)S(1)}) custom-call(s32[1]{0:T(128)} %bitcast.mine_ref, bf16[16,7296]{1,0:T(8,128)(2,1)S(1)} %shard_map.65.refs_2_.refs_0_, bf16[16,7296]{1,0:T(8,128)(2,1)S(1)} %collective-permute-done.2.refs_4_.refs_1_, bf16[16,7296]{1,0:T(8,128)(2,1)S(1)} %collective-permute-done.3.refs_2_, ...), custom_call_target="tpu_custom_call" | custom-call | bytes 7200000 | tf_op jit(solution)/shard_map/pallas_call | solution.py:223
  33.0 1.2 %shard_map.72 = (bf16[128,256]{1,0:T(8,128)(2,1)S(1)}, f32[128,128]{1,0:T(8,128)S(1)}) custom-call(s32[1]{0:T(128)} %bitcast.mine_ref, bf16[16,7296]{1,0:T(8,128)(2,1)S(1)} %shard_map.67.refs_2_.refs_0_, bf16[16,7296]{1,0:T(8,128)(2,1)S(1)} %collective-permute-done.15.refs_1_, bf16[16,7296]{1,0:T(8,128)(2,1)S(1)} %collective-permute-done.16.refs_2_, ...), custom_call_target="tpu_custom_call" | custom-call | bytes 7200000 | tf_op jit(solution)/shard_map/pallas_call | solution.py:223
  36.8 1.5 %collective-permute-start.25 = (bf16[16,7168]{1,0:T(8,128)(2,1)S(1)}, bf16[16,7168]{1,0:T(8,128)(2,1)S(1)}, u32[]{:S(2)}, u32[]{:S(2)}) collective-permute-start(bf16[16,7168]{1,0:T(8,128)(2,1)S(1)} %get-tuple-element.53.refs_2_), channel_id=1, source_target_pairs={{0,4},{1,3},{2,6},{3,1},{4,0},{5,7},{6,2},{7,5},{8,12},{9,11},{10,... | collective-permute-start | bytes 688136 | tf_op jit(solution)/shard_map/ppermute | solution.py:27
  39.1 1.5 %collective-permute-start.27 = (bf16[16,7168]{1,0:T(8,128)(2,1)S(1)}, bf16[16,7168]{1,0:T(8,128)(2,1)S(1)}, u32[]{:S(2)}, u32[]{:S(2)}) collective-permute-start(bf16[16,7168]{1,0:T(8,128)(2,1)S(1)} %get-tuple-element.55.refs_2_), channel_id=1, source_target_pairs={{0,4},{1,3},{2,6},{3,1},{4,0},{5,7},{6,2},{7,5},{8,12},{9,11},{10,... | collective-permute-start | bytes 688136 | tf_op jit(solution)/shard_map/ppermute | solution.py:27
  40.7 2.2 %collective-permute-done.25.refs_1_ = bf16[16,7168]{1,0:T(8,128)(2,1)S(1)} collective-permute-done((bf16[16,7168]{1,0:T(8,128)(2,1)S(1)}, bf16[16,7168]{1,0:T(8,128)(2,1)S(1)}, u32[]{:S(2)}, u32[]{:S(2)}) %collective-permute-start.25) | collective-permute-done | bytes 229408 | tf_op jit(solution)/shard_map/ppermute | solution.py:27
  42.9 1.4 %collective-permute-start.28 = (bf16[8,7168]{1,0:T(8,128)(2,1)S(1)}, bf16[8,7168]{1,0:T(8,128)(2,1)S(1)}, u32[]{:S(2)}, u32[]{:S(2)}) collective-permute-start(bf16[8,7168]{1,0:T(8,128)(2,1)S(1)} %get-tuple-element.60.refs_2_), channel_id=1, source_target_pairs={{0,2},{1,5},{2,0},{3,7},{4,6},{5,1},{6,4},{7,3},{8,10},{9,13},{10,... | collective-permute-start | bytes 344072 | tf_op jit(solution)/shard_map/ppermute | solution.py:27
  45.7 1.2 %collective-permute-start.26 = (bf16[8,7168]{1,0:T(8,128)(2,1)S(1)}, bf16[8,7168]{1,0:T(8,128)(2,1)S(1)}, u32[]{:S(2)}, u32[]{:S(2)}) collective-permute-start(bf16[8,7168]{1,0:T(8,128)(2,1)S(1)} %get-tuple-element.62.refs_2_), channel_id=1, source_target_pairs={{0,2},{1,5},{2,0},{3,7},{4,6},{5,1},{6,4},{7,3},{8,10},{9,13},{10,... | collective-permute-start | bytes 344072 | tf_op jit(solution)/shard_map/ppermute | solution.py:27
  47.0 2.1 %collective-permute-done.28.refs_1_ = bf16[8,7168]{1,0:T(8,128)(2,1)S(1)} collective-permute-done((bf16[8,7168]{1,0:T(8,128)(2,1)S(1)}, bf16[8,7168]{1,0:T(8,128)(2,1)S(1)}, u32[]{:S(2)}, u32[]{:S(2)}) %collective-permute-start.28) | collective-permute-done | bytes 114720 | tf_op jit(solution)/shard_map/ppermute | solution.py:27
  50.3 1.4 %collective-permute-start.32 = (bf16[8,7168]{1,0:T(8,128)(2,1)S(1)}, bf16[8,7168]{1,0:T(8,128)(2,1)S(1)}, u32[]{:S(2)}, u32[]{:S(2)}) collective-permute-start(bf16[8,7168]{1,0:T(8,128)(2,1)S(1)} %get-tuple-element.65.refs_2_), channel_id=1, source_target_pairs={{0,2},{1,5},{2,0},{3,7},{4,6},{5,1},{6,4},{7,3},{8,10},{9,13},{10,... | collective-permute-start | bytes 344072 | tf_op jit(solution)/shard_map/ppermute | solution.py:27
  51.7 3.5 %collective-permute-start.30 = (bf16[8,7168]{1,0:T(8,128)(2,1)S(1)}, bf16[8,7168]{1,0:T(8,128)(2,1)S(1)}, u32[]{:S(2)}, u32[]{:S(2)}) collective-permute-start(bf16[8,7168]{1,0:T(8,128)(2,1)S(1)} %shard_map.80.refs_2_), channel_id=1, source_target_pairs={{0,24},{1,25},{2,26},{3,27},{4,28},{5,29},{6,30},{7,31},{8,16},{9,... | collective-permute-start | bytes 344072 | tf_op jit(solution)/shard_map/ppermute | solution.py:27
  56.0 1.4 %collective-permute-start.33 = (bf16[8,7168]{1,0:T(8,128)(2,1)S(1)}, bf16[8,7168]{1,0:T(8,128)(2,1)S(1)}, u32[]{:S(2)}, u32[]{:S(2)}) collective-permute-start(bf16[8,7168]{1,0:T(8,128)(2,1)S(1)} %shard_map.84.refs_5_), channel_id=1, source_target_pairs={{0,8},{1,9},{2,10},{3,11},{4,12},{5,13},{6,14},{7,15},{8,0},{9,1},... | collective-permute-start | bytes 344072 | tf_op jit(solution)/shard_map/ppermute | solution.py:27
  57.4 1.4 %collective-permute-done.30.refs_2_ = bf16[8,7168]{1,0:T(8,128)(2,1)S(1)} collective-permute-done((bf16[8,7168]{1,0:T(8,128)(2,1)S(1)}, bf16[8,7168]{1,0:T(8,128)(2,1)S(1)}, u32[]{:S(2)}, u32[]{:S(2)}) %collective-permute-start.30) | collective-permute-done | bytes 114720 | tf_op jit(solution)/shard_map/ppermute | solution.py:27
  58.8 1.4 %collective-permute-done.29.refs_1_ = bf16[8,7168]{1,0:T(8,128)(2,1)S(1)} collective-permute-done((bf16[8,7168]{1,0:T(8,128)(2,1)S(1)}, bf16[8,7168]{1,0:T(8,128)(2,1)S(1)}, u32[]{:S(2)}, u32[]{:S(2)}) %collective-permute-start.29) | collective-permute-done | bytes 114720 | tf_op jit(solution)/shard_map/ppermute | solution.py:27
  60.2 1.9 %collective-permute-done.31.refs_3_ = bf16[8,7168]{1,0:T(8,128)(2,1)S(1)} collective-permute-done((bf16[8,7168]{1,0:T(8,128)(2,1)S(1)}, bf16[8,7168]{1,0:T(8,128)(2,1)S(1)}, u32[]{:S(2)}, u32[]{:S(2)}) %collective-permute-start.31) | collective-permute-done | bytes 114720 | tf_op jit(solution)/shard_map/ppermute | solution.py:27
  (67 shorter events, 17.7 us)
Async XLA Ops:
  1.0 7.5 %collective-permute-start.5 = (bf16[8,7296]{1,0:T(8,128)(2,1)S(1)}, bf16[8,7296]{1,0:T(8,128)(2,1)S(1)}, u32[]{:S(2)}, u32[]{:S(2)}) collective-permute-start(bf16[8,7296]{1,0:T(8,128)(2,1)S(1)} %shard_map.64.refs_0_.refs_2_), channel_id=1, source_target_pairs={{0,8},{1,9},{2,10},{3,11},{4,12},{5,13},{6,14},{7,15},{8,0},{9,1},... | collective-permute-start | bytes 350216 | tf_op jit(solution)/shard_map/ppermute | solution.py:27
  4.1 8.1 %collective-permute-start.1 = (bf16[8,7296]{1,0:T(8,128)(2,1)S(1)}, bf16[8,7296]{1,0:T(8,128)(2,1)S(1)}, u32[]{:S(2)}, u32[]{:S(2)}) collective-permute-start(bf16[8,7296]{1,0:T(8,128)(2,1)S(1)} %shard_map.64.refs_0_.refs_2_), channel_id=1, source_target_pairs={{0,16},{1,17},{2,18},{3,19},{4,20},{5,21},{6,22},{7,23},{8,24},{9,... | collective-permute-start | bytes 350216 | tf_op jit(solution)/shard_map/ppermute | solution.py:27
  6.7 5.5 %collective-permute-start = (bf16[8,7296]{1,0:T(8,128)(2,1)S(1)}, bf16[8,7296]{1,0:T(8,128)(2,1)S(1)}, u32[]{:S(2)}, u32[]{:S(2)}) collective-permute-start(bf16[8,7296]{1,0:T(8,128)(2,1)S(1)} %shard_map.64.refs_0_.refs_2_), channel_id=1, source_target_pairs={{0,2},{1,5},{2,0},{3,7},{4,6},{5,1},{6,4},{7,3},{8,10},{9,13},{10,... | collective-permute-start | bytes 350216 | tf_op jit(solution)/shard_map/ppermute | solution.py:27
  8.5 5.8 %collective-permute-start.6 = (bf16[8,7296]{1,0:T(8,128)(2,1)S(1)}, bf16[8,7296]{1,0:T(8,128)(2,1)S(1)}, u32[]{:S(2)}, u32[]{:S(2)}) collective-permute-start(bf16[8,7296]{1,0:T(8,128)(2,1)S(1)} %collective-permute-done.5.refs_0_.refs_3_), channel_id=1, source_target_pairs={{0,2},{1,5},{2,0},{3,7},{4,6},{5,1},{6,4},{7,3},{8,10},{9,13},{10,... | collective-permute-start | bytes 350216 | tf_op jit(solution)/shard_map/ppermute | solution.py:27
  12.2 9.8 %collective-permute-start.2 = (bf16[16,7296]{1,0:T(8,128)(2,1)S(1)}, bf16[16,7296]{1,0:T(8,128)(2,1)S(1)}, u32[]{:S(2)}, u32[]{:S(2)}) collective-permute-start(bf16[16,7296]{1,0:T(8,128)(2,1)S(1)} %shard_map.65.refs_2_.refs_0_), channel_id=1, source_target_pairs={{0,4},{1,3},{2,6},{3,1},{4,0},{5,7},{6,2},{7,5},{8,12},{9,11},{10,... | collective-permute-start | bytes 700424 | tf_op jit(solution)/shard_map/ppermute | solution.py:27
  14.3 9.2 %collective-permute-start.7 = (bf16[16,7296]{1,0:T(8,128)(2,1)S(1)}, bf16[16,7296]{1,0:T(8,128)(2,1)S(1)}, u32[]{:S(2)}, u32[]{:S(2)}) collective-permute-start(bf16[16,7296]{1,0:T(8,128)(2,1)S(1)} %shard_map.66.refs_2_.refs_4_), channel_id=1, source_target_pairs={{0,4},{1,3},{2,6},{3,1},{4,0},{5,7},{6,2},{7,5},{8,12},{9,11},{10,... | collective-permute-start | bytes 700424 | tf_op jit(solution)/shard_map/ppermute | solution.py:27
  16.3 7.7 %collective-permute-start.3 = (bf16[16,7296]{1,0:T(8,128)(2,1)S(1)}, bf16[16,7296]{1,0:T(8,128)(2,1)S(1)}, u32[]{:S(2)}, u32[]{:S(2)}) collective-permute-start(bf16[16,7296]{1,0:T(8,128)(2,1)S(1)} %shard_map.65.refs_2_.refs_0_), channel_id=1, source_target_pairs={{0,1},{1,0},{2,3},{3,2},{4,5},{5,4},{6,7},{7,6},{8,9},{9,8},{10,11... | collective-permute-start | bytes 700424 | tf_op jit(solution)/shard_map/ppermute | solution.py:27
  21.1 8.2 %collective-permute-start.8 = (bf16[16,7296]{1,0:T(8,128)(2,1)S(1)}, bf16[16,7296]{1,0:T(8,128)(2,1)S(1)}, u32[]{:S(2)}, u32[]{:S(2)}) collective-permute-start(bf16[16,7296]{1,0:T(8,128)(2,1)S(1)} %shard_map.66.refs_2_.refs_4_), channel_id=1, source_target_pairs={{0,1},{1,0},{2,3},{3,2},{4,5},{5,4},{6,7},{7,6},{8,9},{9,8},{10,11... | collective-permute-start | bytes 700424 | tf_op jit(solution)/shard_map/ppermute | solution.py:27
  22.1 7.6 %collective-permute-start.15 = (bf16[16,7296]{1,0:T(8,128)(2,1)S(1)}, bf16[16,7296]{1,0:T(8,128)(2,1)S(1)}, u32[]{:S(2)}, u32[]{:S(2)}) collective-permute-start(bf16[16,7296]{1,0:T(8,128)(2,1)S(1)} %shard_map.67.refs_2_.refs_0_), channel_id=1, source_target_pairs={{0,4},{1,3},{2,6},{3,1},{4,0},{5,7},{6,2},{7,5},{8,12},{9,11},{10,... | collective-permute-start | bytes 700424 | tf_op jit(solution)/shard_map/ppermute | solution.py:27
  23.4 6.5 %collective-permute-start.4 = (bf16[16,7296]{1,0:T(8,128)(2,1)S(1)}, bf16[16,7296]{1,0:T(8,128)(2,1)S(1)}, u32[]{:S(2)}, u32[]{:S(2)}) collective-permute-start(bf16[16,7296]{1,0:T(8,128)(2,1)S(1)} %collective-permute-done.2.refs_4_.refs_1_), channel_id=1, source_target_pairs={{0,1},{1,0},{2,3},{3,2},{4,5},{5,4},{6,7},{7,6},{8,9},{9,8},{10,11... | collective-permute-start | bytes 700424 | tf_op jit(solution)/shard_map/ppermute | solution.py:27
  23.5 6.8 %collective-permute-start.9 = (bf16[16,7296]{1,0:T(8,128)(2,1)S(1)}, bf16[16,7296]{1,0:T(8,128)(2,1)S(1)}, u32[]{:S(2)}, u32[]{:S(2)}) collective-permute-start(bf16[16,7296]{1,0:T(8,128)(2,1)S(1)} %collective-permute-done.7.refs_5_), channel_id=1, source_target_pairs={{0,1},{1,0},{2,3},{3,2},{4,5},{5,4},{6,7},{7,6},{8,9},{9,8},{10,11... | collective-permute-start | bytes 700424 | tf_op jit(solution)/shard_map/ppermute | solution.py:27
  24.0 7.4 %collective-permute-start.18 = (bf16[16,7296]{1,0:T(8,128)(2,1)S(1)}, bf16[16,7296]{1,0:T(8,128)(2,1)S(1)}, u32[]{:S(2)}, u32[]{:S(2)}) collective-permute-start(bf16[16,7296]{1,0:T(8,128)(2,1)S(1)} %shard_map.68.refs_3_.refs_4_), channel_id=1, source_target_pairs={{0,4},{1,3},{2,6},{3,1},{4,0},{5,7},{6,2},{7,5},{8,12},{9,11},{10,... | collective-permute-start | bytes 700424 | tf_op jit(solution)/shard_map/ppermute | solution.py:27
  35.6 5.0 %collective-permute-start.13 = (bf16[32,7168]{1,0:T(8,128)(2,1)S(1)}, bf16[32,7168]{1,0:T(8,128)(2,1)S(1)}, u32[]{:S(2)}, u32[]{:S(2)}) collective-permute-start(bf16[32,7168]{1,0:T(8,128)(2,1)S(1)} %get-tuple-element.43), channel_id=1, source_target_pairs={{0,1},{1,0},{2,3},{3,2},{4,5},{5,4},{6,7},{7,6},{8,9},{9,8},{10,11... | collective-permute-start | bytes 1376264 | tf_op jit(solution)/shard_map/ppermute | solution.py:27
  36.8 6.1 %collective-permute-start.25 = (bf16[16,7168]{1,0:T(8,128)(2,1)S(1)}, bf16[16,7168]{1,0:T(8,128)(2,1)S(1)}, u32[]{:S(2)}, u32[]{:S(2)}) collective-permute-start(bf16[16,7168]{1,0:T(8,128)(2,1)S(1)} %get-tuple-element.53.refs_2_), channel_id=1, source_target_pairs={{0,4},{1,3},{2,6},{3,1},{4,0},{5,7},{6,2},{7,5},{8,12},{9,11},{10,... | collective-permute-start | bytes 688136 | tf_op jit(solution)/shard_map/ppermute | solution.py:27
  38.4 7.3 %collective-permute-start.24 = (bf16[16,7168]{1,0:T(8,128)(2,1)S(1)}, bf16[16,7168]{1,0:T(8,128)(2,1)S(1)}, u32[]{:S(2)}, u32[]{:S(2)}) collective-permute-start(bf16[16,7168]{1,0:T(8,128)(2,1)S(1)} %get-tuple-element.54.refs_2_), channel_id=1, source_target_pairs={{0,4},{1,3},{2,6},{3,1},{4,0},{5,7},{6,2},{7,5},{8,12},{9,11},{10,... | collective-permute-start | bytes 688136 | tf_op jit(solution)/shard_map/ppermute | solution.py:27
  39.1 11.1 %collective-permute-start.27 = (bf16[16,7168]{1,0:T(8,128)(2,1)S(1)}, bf16[16,7168]{1,0:T(8,128)(2,1)S(1)}, u32[]{:S(2)}, u32[]{:S(2)}) collective-permute-start(bf16[16,7168]{1,0:T(8,128)(2,1)S(1)} %get-tuple-element.55.refs_2_), channel_id=1, source_target_pairs={{0,4},{1,3},{2,6},{3,1},{4,0},{5,7},{6,2},{7,5},{8,12},{9,11},{10,... | collective-permute-start | bytes 688136 | tf_op jit(solution)/shard_map/ppermute | solution.py:27
  42.9 6.1 %collective-permute-start.28 = (bf16[8,7168]{1,0:T(8,128)(2,1)S(1)}, bf16[8,7168]{1,0:T(8,128)(2,1)S(1)}, u32[]{:S(2)}, u32[]{:S(2)}) collective-permute-start(bf16[8,7168]{1,0:T(8,128)(2,1)S(1)} %get-tuple-element.60.refs_2_), channel_id=1, source_target_pairs={{0,2},{1,5},{2,0},{3,7},{4,6},{5,1},{6,4},{7,3},{8,10},{9,13},{10,... | collective-permute-start | bytes 344072 | tf_op jit(solution)/shard_map/ppermute | solution.py:27
  44.3 11.0 %collective-permute-start.23 = (bf16[16,7168]{1,0:T(8,128)(2,1)S(1)}, bf16[16,7168]{1,0:T(8,128)(2,1)S(1)}, u32[]{:S(2)}, u32[]{:S(2)}) collective-permute-start(bf16[16,7168]{1,0:T(8,128)(2,1)S(1)} %get-tuple-element.57.refs_2_), channel_id=1, source_target_pairs={{0,4},{1,3},{2,6},{3,1},{4,0},{5,7},{6,2},{7,5},{8,12},{9,11},{10,... | collective-permute-start | bytes 688136 | tf_op jit(solution)/shard_map/ppermute | solution.py:27
  45.7 9.5 %collective-permute-start.26 = (bf16[8,7168]{1,0:T(8,128)(2,1)S(1)}, bf16[8,7168]{1,0:T(8,128)(2,1)S(1)}, u32[]{:S(2)}, u32[]{:S(2)}) collective-permute-start(bf16[8,7168]{1,0:T(8,128)(2,1)S(1)} %get-tuple-element.62.refs_2_), channel_id=1, source_target_pairs={{0,2},{1,5},{2,0},{3,7},{4,6},{5,1},{6,4},{7,3},{8,10},{9,13},{10,... | collective-permute-start | bytes 344072 | tf_op jit(solution)/shard_map/ppermute | solution.py:27
  50.3 5.7 %collective-permute-start.32 = (bf16[8,7168]{1,0:T(8,128)(2,1)S(1)}, bf16[8,7168]{1,0:T(8,128)(2,1)S(1)}, u32[]{:S(2)}, u32[]{:S(2)}) collective-permute-start(bf16[8,7168]{1,0:T(8,128)(2,1)S(1)} %get-tuple-element.65.refs_2_), channel_id=1, source_target_pairs={{0,2},{1,5},{2,0},{3,7},{4,6},{5,1},{6,4},{7,3},{8,10},{9,13},{10,... | collective-permute-start | bytes 344072 | tf_op jit(solution)/shard_map/ppermute | solution.py:27
  51.7 7.1 %collective-permute-start.30 = (bf16[8,7168]{1,0:T(8,128)(2,1)S(1)}, bf16[8,7168]{1,0:T(8,128)(2,1)S(1)}, u32[]{:S(2)}, u32[]{:S(2)}) collective-permute-start(bf16[8,7168]{1,0:T(8,128)(2,1)S(1)} %shard_map.80.refs_2_), channel_id=1, source_target_pairs={{0,24},{1,25},{2,26},{3,27},{4,28},{5,29},{6,30},{7,31},{8,16},{9,... | collective-permute-start | bytes 344072 | tf_op jit(solution)/shard_map/ppermute | solution.py:27
  55.2 6.9 %collective-permute-start.31 = (bf16[8,7168]{1,0:T(8,128)(2,1)S(1)}, bf16[8,7168]{1,0:T(8,128)(2,1)S(1)}, u32[]{:S(2)}, u32[]{:S(2)}) collective-permute-start(bf16[8,7168]{1,0:T(8,128)(2,1)S(1)} %shard_map.82.refs_2_), channel_id=1, source_target_pairs={{0,16},{1,17},{2,18},{3,19},{4,20},{5,21},{6,22},{7,23},{8,24},{9,... | collective-permute-start | bytes 344072 | tf_op jit(solution)/shard_map/ppermute | solution.py:27
  55.4 4.9 %collective-permute-start.29 = (bf16[8,7168]{1,0:T(8,128)(2,1)S(1)}, bf16[8,7168]{1,0:T(8,128)(2,1)S(1)}, u32[]{:S(2)}, u32[]{:S(2)}) collective-permute-start(bf16[8,7168]{1,0:T(8,128)(2,1)S(1)} %get-tuple-element.67.refs_2_), channel_id=1, source_target_pairs={{0,2},{1,5},{2,0},{3,7},{4,6},{5,1},{6,4},{7,3},{8,10},{9,13},{10,... | collective-permute-start | bytes 344072 | tf_op jit(solution)/shard_map/ppermute | solution.py:27
  56.0 6.3 %collective-permute-start.33 = (bf16[8,7168]{1,0:T(8,128)(2,1)S(1)}, bf16[8,7168]{1,0:T(8,128)(2,1)S(1)}, u32[]{:S(2)}, u32[]{:S(2)}) collective-permute-start(bf16[8,7168]{1,0:T(8,128)(2,1)S(1)} %shard_map.84.refs_5_), channel_id=1, source_target_pairs={{0,8},{1,9},{2,10},{3,11},{4,12},{5,13},{6,14},{7,15},{8,0},{9,1},... | collective-permute-start | bytes 344072 | tf_op jit(solution)/shard_map/ppermute | solution.py:27
  (10 other events, 32.8 us)
